TPU v7x, 512 devices: a whole 4x8x8 slice. The times are simulated.
512 devices in a mesh: gx: 32 (over y, x), gy: 16 (over z, core).
Axes of the slice: x: 4, y: 8, z: 8, core: 2. Of those that a mesh axis runs over, the one named last changes fastest.
Arguments:
- diag_block: float32 [4, 4, 6, 64, 4096], P(None, None, None, 'gx', 'gy'), may hold values from -1.1 to 4.1
- block_inverse: float32 [4, 4, 6, 64, 4096], P(None, None, None, 'gx', 'gy'), may hold values from -0.4 to 1.4
- viscosity: float32 [6, 64, 4096], P(None, 'gx', 'gy'), may hold values from 0.4 to 1
- coupling: float32 [6, 4, 4], replicated, may hold values from -0.7 to 0.7
- active_layers: int32 [64, 4096], P('gx', 'gy'), may hold values from 3 to 6
- grounded: int32 [64, 4096], P('gx', 'gy'), may hold values 0 or 1
- weight_pattern: int32 [64, 4096], P('gx', 'gy'), may hold values from 0 to 3
- beta_step: float32 [64, 4096], P('gx', 'gy'), may hold values from -6 to 6
- base_vel: float32 [2, 64, 4096], P(None, 'gx', 'gy'), may hold values from -18 to 18
Outputs:
- hessian_vec: float32 [64, 4096], P('gx', 'gy')
- adjoint: float32 [4, 6, 64, 4096], P(None, None, 'gx', 'gy')
All inputs are finite; a program needn't handle non-finite values. No bound on the sum of `grounded` on one device may be relied on, other than what follows from the above.
Results may differ from a plain program's by a relative error of at most 0.0001.
Values sent between devices are 32-bit elements; how exact they have to be, the bound alone decides.
No kernel may reach another device: no remote copies, remote signals or barrier semaphores. Data moves between devices by JAX's collectives and lax.ppermute only.
A program may use at most 192 MiB of HBM per device.

v0:
```python
import jax
import jax.numpy as jnp
from jax import lax
from jax.sharding import PartitionSpec as P

SWEEPS = 2


DIRECTIONS = ((0, 1), (0, -1), (1, 1), (1, -1), (2, 1), (2, -1))
OPPOSITE = (1, 0, 3, 2, 5, 4)
PRIOR_WEIGHT = 0.05
EPSILON = 1e-06


def padded(block, sides, width):
    for axis, dim in sides:
        count = lax.axis_size(axis)
        forward = [(i, i + 1) for i in range(count - 1)]
        backward = [(target, source) for source, target in forward]
        low = lax.ppermute(
            lax.slice_in_dim(block, block.shape[dim] - width, None, axis=dim), axis, forward
        )
        high = lax.ppermute(lax.slice_in_dim(block, 0, width, axis=dim), axis, backward)
        block = jnp.concatenate([low, block, high], axis=dim)
    return block


def shifted(values, dim_at, offset):
    length = values.shape[dim_at]
    widths = [(0, 0)] * values.ndim
    if offset > 0:
        kept_part = lax.slice_in_dim(values, offset, length, axis=dim_at)
        widths[dim_at] = (0, offset)
    else:
        kept_part = lax.slice_in_dim(values, 0, length + offset, axis=dim_at)
        widths[dim_at] = (-offset, 0)
    return jnp.pad(kept_part, widths)


def block_apply(blocks, values):
    return jnp.sum(blocks * values[None], axis=1)


def small_apply(matrix, values):
    return jnp.sum(matrix.reshape(matrix.shape + (1,) * (values.ndim - 1)) * values[None], axis=1)


def operate(values, diagonal, viscous, active, couplings, axis_set):
    carried = viscous[None] * values
    summed = jnp.zeros_like(values)
    for direction in range(6):
        dim_at = axis_set[DIRECTIONS[direction][0]]
        summed = summed + small_apply(
            couplings[direction], shifted(carried, dim_at, DIRECTIONS[direction][1])
        )
    return (
        active[None] * block_apply(diagonal, active[None] * values)
        + (1.0 - active[None]) * values
        - viscous[None] * summed
    )


def precondition(values, inverse, active):
    return active[None] * block_apply(inverse, values) + (1.0 - active[None]) * values


def local_solve(residual, diagonal, inverse, viscous, active, couplings, axis_set):
    initial = precondition(residual, inverse, active)
    return initial + precondition(
        residual - operate(initial, diagonal, viscous, active, couplings, axis_set), inverse, active
    )


def clear_corners(values):
    plane = values.shape[-2:]
    row_at = lax.broadcasted_iota(jnp.int32, plane, 0)
    col_at = lax.broadcasted_iota(jnp.int32, plane, 1)
    corner = ((row_at == 0) | (row_at == plane[0] - 1)) & ((col_at == 0) | (col_at == plane[1] - 1))
    return jnp.where(corner, 0.0, values)


def per_device(
    diag_block,
    block_inverse,
    viscosity,
    coupling,
    active_layers,
    grounded,
    weight_pattern,
    beta_step,
    base_vel,
):
    layers, rows_dev, cols_dev = viscosity.shape
    cell_shape = viscosity.shape
    layer_at = lax.broadcasted_iota(jnp.int32, cell_shape, 0)
    active = (layer_at < active_layers[None]).astype(jnp.float32)
    viscous = viscosity * active
    pattern_f = weight_pattern.astype(jnp.float32)
    stacked = jnp.concatenate(
        [
            diag_block.reshape((16,) + cell_shape),
            block_inverse.reshape((16,) + cell_shape),
            viscous[None],
            active[None],
            jnp.broadcast_to(beta_step[None, None], (1,) + cell_shape),
            jnp.broadcast_to(pattern_f[None, None], (1,) + cell_shape),
        ],
        axis=0,
    )
    wide_tables = padded(stacked, (("gx", 2), ("gy", 3)), 2)
    widened = clear_corners(wide_tables[..., 1:-1, 1:-1])
    ext_shape = (layers, rows_dev + 2, cols_dev + 2)
    diag_ext = widened[:16].reshape((4, 4) + ext_shape)
    inverse_ext = widened[16:32].reshape((4, 4) + ext_shape)
    viscous_ext = widened[32]
    active_ext = widened[33]
    beta_ext = widened[34, 0]
    wide_x = rows_dev + 4
    wide_y = cols_dev + 4
    gx_at = lax.axis_index("gx")
    gy_at = lax.axis_index("gy")
    blocks_x = lax.axis_size("gx")
    blocks_y = lax.axis_size("gy")
    west_on = (gx_at > 0).astype(jnp.float32)
    east_on = (gx_at < blocks_x - 1).astype(jnp.float32)
    south_on = (gy_at > 0).astype(jnp.float32)
    north_on = (gy_at < blocks_y - 1).astype(jnp.float32)
    col_at = lax.broadcasted_iota(jnp.int32, (rows_dev, cols_dev), 0)
    row_at = lax.broadcasted_iota(jnp.int32, (rows_dev, cols_dev), 1)
    shared = west_on * (col_at == 0).astype(jnp.float32) + east_on * (
        col_at == rows_dev - 1
    ).astype(jnp.float32)
    shared = (
        shared
        + south_on * (row_at == 0).astype(jnp.float32)
        + north_on * (row_at == cols_dev - 1).astype(jnp.float32)
    )
    own_weight = jnp.where(shared > 0, (1.0 + pattern_f) / 5.0, 1.0)
    near_weight = (1.0 - own_weight) / jnp.maximum(shared, 1.0)
    global_x = gx_at * rows_dev - 2 + lax.broadcasted_iota(jnp.int32, (wide_x, wide_y), 0)
    global_y = gy_at * cols_dev - 2 + lax.broadcasted_iota(jnp.int32, (wide_x, wide_y), 1)
    spans_x = {-1: (0, 4), 0: (0, wide_x), 1: (wide_x - 4, wide_x)}
    spans_y = {-1: (0, 4), 0: (0, wide_y), 1: (wide_y - 4, wide_y)}
    block_list = []
    counted = jnp.zeros((wide_x, wide_y), jnp.float32)
    for step_x in (-1, 0, 1):
        for step_y in (-1, 0, 1):
            index_x = gx_at + step_x
            index_y = gy_at + step_y
            inside_x = (global_x >= index_x * rows_dev) & (global_x < index_x * rows_dev + rows_dev)
            inside_y = (global_y >= index_y * cols_dev) & (global_y < index_y * cols_dev + cols_dev)
            edge_x = (global_x == index_x * rows_dev - 1) | (
                global_x == index_x * rows_dev + rows_dev
            )
            edge_y = (global_y == index_y * cols_dev - 1) | (
                global_y == index_y * cols_dev + cols_dev
            )
            region = inside_x & inside_y | edge_x & inside_y | inside_x & edge_y
            exists = (
                (index_x >= 0) & (index_x < blocks_x) & (index_y >= 0) & (index_y < blocks_y)
            ).astype(jnp.float32)
            keep = region.astype(jnp.float32) * exists
            counted = counted + keep
            block_list.append(
                (spans_x[step_x], spans_y[step_y], keep, (inside_x & inside_y).astype(jnp.float32))
            )

    def schwarz(residual, diagonal_ext, inverse_blocks, couplings):
        residual_ext = clear_corners(padded(residual, (("gx", 2), ("gy", 3)), 1))
        solved = local_solve(
            residual_ext,
            diagonal_ext,
            inverse_blocks,
            viscous_ext,
            active_ext,
            couplings,
            (1, 2, 3),
        )
        own_part = solved[:, :, 1:-1, 1:-1]
        pack_x = (
            jnp.zeros_like(own_part)
            .at[:, :, 0, :]
            .set(solved[:, :, 0, 1:-1])
            .at[:, :, -1, :]
            .set(solved[:, :, -1, 1:-1])
        )
        pack_y = (
            jnp.zeros_like(own_part)
            .at[:, :, :, 0]
            .set(solved[:, :, 1:-1, 0])
            .at[:, :, :, -1]
            .set(solved[:, :, 1:-1, -1])
        )
        arrived = padded(jnp.concatenate([pack_x, pack_y], axis=0), (("gx", 2), ("gy", 3)), 1)
        from_west = arrived[:4, :, 0, 1:-1]
        from_east = arrived[:4, :, -1, 1:-1]
        from_south = arrived[4:, :, 1:-1, 0]
        from_north = arrived[4:, :, 1:-1, -1]
        nearby = jnp.pad(from_west[:, :, None, :], ((0, 0), (0, 0), (0, rows_dev - 1), (0, 0)))
        nearby = nearby + jnp.pad(
            from_east[:, :, None, :], ((0, 0), (0, 0), (rows_dev - 1, 0), (0, 0))
        )
        nearby = nearby + jnp.pad(
            from_south[:, :, :, None], ((0, 0), (0, 0), (0, 0), (0, cols_dev - 1))
        )
        nearby = nearby + jnp.pad(
            from_north[:, :, :, None], ((0, 0), (0, 0), (0, 0), (cols_dev - 1, 0))
        )
        return own_weight * own_part + near_weight * nearby

    def apply_global(update, diagonal_ext, couplings):
        update_ext = padded(update, (("gx", 2), ("gy", 3)), 1)
        return operate(update_ext, diagonal_ext, viscous_ext, active_ext, couplings, (1, 2, 3))[
            :, :, 1:-1, 1:-1
        ]

    def solve(rhs, diagonal_ext, inverse_blocks, couplings):
        solution = jnp.zeros_like(rhs)
        residual = rhs
        for sweep_at in range(SWEEPS):
            update = schwarz(residual, diagonal_ext, inverse_blocks, couplings)
            image = apply_global(update, diagonal_ext, couplings)
            along, squared = lax.psum(
                (jnp.sum(residual * image), jnp.sum(image * image)), ("gx", "gy")
            )
            omega = along / (squared + EPSILON)
            solution = solution + omega * update
            residual = residual - omega * image
        return solution

    coupling_t = jnp.stack([coupling[OPPOSITE[direction]].T for direction in range(6)])
    grounded_f = grounded.astype(jnp.float32)
    basal = -(grounded_f * beta_step)[None] * base_vel
    rhs_forward = jnp.zeros((4,) + cell_shape, jnp.float32).at[0:2, 0].set(basal)
    increment = solve(rhs_forward, diag_ext, inverse_ext, coupling)
    counts = active_layers.astype(jnp.float32)
    average = jnp.sum(active[None] * increment[0:2], axis=1) / counts[None]
    rhs_adjoint = (
        jnp.zeros((4,) + cell_shape, jnp.float32)
        .at[0:2]
        .set(-active[None] * (average / counts[None])[:, None])
    )
    adjoint = solve(
        rhs_adjoint, jnp.swapaxes(diag_ext, 0, 1), jnp.swapaxes(inverse_ext, 0, 1), coupling_t
    )
    prior = 4.0 * beta_step - (
        beta_ext[2:, 1:-1] + beta_ext[:-2, 1:-1] + beta_ext[1:-1, 2:] + beta_ext[1:-1, :-2]
    )
    data_term = grounded_f * (base_vel[0] * adjoint[0, 0] + base_vel[1] * adjoint[1, 0])
    hessian_vec = data_term + PRIOR_WEIGHT * prior
    return (hessian_vec, adjoint)


def solution(mesh):
    placed = (
        P(None, None, None, "gx", "gy"),
        P(None, None, None, "gx", "gy"),
        P(None, "gx", "gy"),
        P(),
        P("gx", "gy"),
        P("gx", "gy"),
        P("gx", "gy"),
        P("gx", "gy"),
        P(None, "gx", "gy"),
    )
    return jax.shard_map(
        per_device,
        mesh=mesh,
        in_specs=placed,
        out_specs=(P("gx", "gy"), P(None, None, "gx", "gy")),
        check_vma=False,
    )
```

profile of v0, /device:TPU:1, one launch (start us, length us, event | category | flops | bytes accessed | tf_op | source)
XLA Modules:
  0.0 711.5 jit_solution(16721909297147945914)
XLA Ops:
  6.6 5.4 collective-permute-start
  14.7 4.0 collective-permute-start.4
  22.0 9.3 %collective-permute-start.7 = (f32[4,6,4,1]{3,2,1,0:T(4,128)S(1)}, f32[4,6,4,1]{3,2,1,0:T(4,128)S(1)}, u32[]{:S(2)}, u32[]{:S(2)}) collective-permute-start(f32[4,6,4,1]{3,2,1,0:T(4,128)S(1)} %get-tuple-element.362), channel_id=1, source_target_pairs={{1,0},{2,1},{3,2},{4,3},{5,4},{6,5},{7,6},{8,7},{9,8},{10,9},{11,1... | collective-permute-start | bytes 1160 | tf_op jit(solution)/shard_map/ppermute | solution.py:23
  43.8 4.4 fusion
  55.4 4.0 collective-permute-start.8
  63.5 4.0 collective-permute-start.10
  70.7 4.6 collective-permute-start.12
  78.3 5.6 collective-permute-start.14
  88.3 115.1 %all-reduce.73 = (f32[]{:T(128)}, f32[]{:T(128)}) all-reduce(f32[]{:T(128)} %get-tuple-element.225, f32[]{:T(128)} %get-tuple-element.224), channel_id=1, replica_groups=mesh['gx'=32,'gy'=16] {'gx','gy'}, use_global_device_ids=true, to_apply=%region_17.18 | all-reduce | flops 2 | bytes 16 | tf_op jit(solution)/shard_map/psum | solution.py:223
  206.1 4.3 collective-permute-start.16
  211.5 3.4 collective-permute-start.19
  214.9 4.0 collective-permute-start.18
  227.2 4.6 collective-permute-start.20
  235.1 5.1 collective-permute-start.22
  243.4 4.6 collective-permute-start.24
  251.0 5.2 collective-permute-start.26
  260.8 110.5 %all-reduce.72 = (f32[]{:T(128)}, f32[]{:T(128)}) all-reduce(f32[]{:T(128)} %get-tuple-element.223, f32[]{:T(128)} %get-tuple-element.222), channel_id=1, replica_groups=mesh['gx'=32,'gy'=16] {'gx','gy'}, use_global_device_ids=true, to_apply=%region_37.38 | all-reduce | flops 2 | bytes 16 | tf_op jit(solution)/shard_map/psum | solution.py:223
  374.0 4.3 collective-permute-start.28
  382.9 4.0 collective-permute-start.30
  395.2 4.6 collective-permute-start.32
  403.2 5.1 collective-permute-start.34
  411.4 4.6 collective-permute-start.36
  419.0 5.2 collective-permute-start.38
  429.7 110.3 %all-reduce.71 = (f32[]{:T(128)}, f32[]{:T(128)}) all-reduce(f32[]{:T(128)} %get-tuple-element.221, f32[]{:T(128)} %get-tuple-element.220), channel_id=1, replica_groups=mesh['gx'=32,'gy'=16] {'gx','gy'}, use_global_device_ids=true, to_apply=%region_58.59 | all-reduce | flops 2 | bytes 16 | tf_op jit(solution)/shard_map/psum | solution.py:223
  543.5 4.3 collective-permute-start.40
  548.9 3.4 collective-permute-start.43
  552.3 4.2 collective-permute-start.42
  564.9 4.6 collective-permute-start.44
  572.9 5.1 collective-permute-start.46
  581.1 4.6 collective-permute-start.48
  588.7 5.2 collective-permute-start.50
  598.7 110.3 %all-reduce.70 = (f32[]{:T(128)}, f32[]{:T(128)}) all-reduce(f32[]{:T(128)} %get-tuple-element.219, f32[]{:T(128)} %get-tuple-element.218), channel_id=1, replica_groups=mesh['gx'=32,'gy'=16] {'gx','gy'}, use_global_device_ids=true, to_apply=%region_78.79 | all-reduce | flops 2 | bytes 16 | tf_op jit(solution)/shard_map/psum | solution.py:223
  (455 shorter events, 124.8 us)
Async XLA Ops:
  5.3 27.9 %collective-permute-start.1 = (f32[36,6,2,256]{3,2,1,0:T(2,128)S(1)}, f32[36,6,2,256]{3,2,1,0:T(2,128)}, u32[]{:S(2)}, u32[]{:S(2)}) collective-permute-start(f32[36,6,2,256]{3,2,1,0:T(2,128)S(1)} %constant_dynamic-update-slice_fusion), channel_id=1, source_target_pairs={{16,0},{32,16},{48,32},{64,48},{80,64},{96,80},{112,96},{128,112},... | collective-permute-start | bytes 1327112 | tf_op jit(solution)/shard_map/ppermute | solution.py:23
  6.6 26.6 %collective-permute-start = (f32[36,6,2,256]{3,2,1,0:T(2,128)S(1)}, f32[36,6,2,256]{3,2,1,0:T(2,128)}, u32[]{:S(2)}, u32[]{:S(2)}) collective-permute-start(f32[36,6,2,256]{3,2,1,0:T(2,128)S(1)} %constant_dynamic-update-slice_fusion), channel_id=1, source_target_pairs={{0,16},{16,32},{32,48},{48,64},{64,80},{80,96},{96,112},{112,128},... | collective-permute-start | bytes 1327112 | tf_op jit(solution)/shard_map/ppermute | solution.py:20
  13.4 8.3 %collective-permute-start.5 = (f32[4,6,1,256]{3,2,1,0:T(1,128)S(1)}, f32[4,6,1,256]{3,2,1,0:T(1,128)S(1)}, u32[]{:S(2)}, u32[]{:S(2)}) collective-permute-start(f32[4,6,1,256]{3,2,1,0:T(1,128)S(1)} %get-tuple-element.378), channel_id=1, source_target_pairs={{16,0},{32,16},{48,32},{64,48},{80,64},{96,80},{112,96},{128,112},... | collective-permute-start | bytes 73736 | tf_op jit(solution)/shard_map/ppermute | solution.py:23
  14.7 7.1 collective-permute-start.4
  22.0 19.7 %collective-permute-start.7 = (f32[4,6,4,1]{3,2,1,0:T(4,128)S(1)}, f32[4,6,4,1]{3,2,1,0:T(4,128)S(1)}, u32[]{:S(2)}, u32[]{:S(2)}) collective-permute-start(f32[4,6,4,1]{3,2,1,0:T(4,128)S(1)} %get-tuple-element.362), channel_id=1, source_target_pairs={{1,0},{2,1},{3,2},{4,3},{5,4},{6,5},{7,6},{8,7},{9,8},{10,9},{11,1... | collective-permute-start | bytes 1160 | tf_op jit(solution)/shard_map/ppermute | solution.py:23
  31.3 10.4 %collective-permute-start.6 = (f32[4,6,4,1]{3,2,1,0:T(4,128)S(1)}, f32[4,6,4,1]{3,2,1,0:T(4,128)S(1)}, u32[]{:S(2)}, u32[]{:S(2)}) collective-permute-start(f32[4,6,4,1]{3,2,1,0:T(4,128)S(1)} %get-tuple-element.361), channel_id=1, source_target_pairs={{0,1},{1,2},{2,3},{3,4},{4,5},{5,6},{6,7},{7,8},{8,9},{9,10},{10,1... | collective-permute-start | bytes 1160 | tf_op jit(solution)/shard_map/ppermute | solution.py:20
  35.7 7.1 collective-permute-start.3
  61.2 6.7 collective-permute-start.11
  69.4 5.9 collective-permute-start.13
  76.4 7.8 %collective-permute-start.15 = (f32[4,6,4,1]{3,2,1,0:T(4,128)S(1)}, f32[4,6,4,1]{3,2,1,0:T(4,128)S(1)}, u32[]{:S(2)}, u32[]{:S(2)}) collective-permute-start(f32[4,6,4,1]{3,2,1,0:T(4,128)S(1)} %get-tuple-element.358), channel_id=1, source_target_pairs={{1,0},{2,1},{3,2},{4,3},{5,4},{6,5},{7,6},{8,7},{9,8},{10,9},{11,1... | collective-permute-start | bytes 1160 | tf_op jit(solution)/shard_map/ppermute | solution.py:23
  78.3 6.3 collective-permute-start.14
  211.5 7.4 %collective-permute-start.19 = (f32[4,6,4,1]{3,2,1,0:T(4,128)S(1)}, f32[4,6,4,1]{3,2,1,0:T(4,128)S(1)}, u32[]{:S(2)}, u32[]{:S(2)}) collective-permute-start(f32[4,6,4,1]{3,2,1,0:T(4,128)S(1)} %get-tuple-element.356), channel_id=1, source_target_pairs={{1,0},{2,1},{3,2},{4,3},{5,4},{6,5},{7,6},{8,7},{9,8},{10,9},{11,1... | collective-permute-start | bytes 1160 | tf_op jit(solution)/shard_map/ppermute | solution.py:23
  225.9 5.9 collective-permute-start.21
  233.2 7.4 %collective-permute-start.23 = (f32[8,6,4,1]{3,2,1,0:T(4,128)S(1)}, f32[8,6,4,1]{3,2,1,0:T(4,128)S(1)}, u32[]{:S(2)}, u32[]{:S(2)}) collective-permute-start(f32[8,6,4,1]{3,2,1,0:T(4,128)S(1)} %get-tuple-element.272), channel_id=1, source_target_pairs={{1,0},{2,1},{3,2},{4,3},{5,4},{6,5},{7,6},{8,7},{9,8},{10,9},{11,1... | collective-permute-start | bytes 2312 | tf_op jit(solution)/shard_map/ppermute | solution.py:23
  235.1 6.7 collective-permute-start.22
  242.1 5.9 collective-permute-start.25
  249.1 7.1 collective-permute-start.27
  251.0 6.3 collective-permute-start.26
  372.7 6.2 collective-permute-start.29
  379.4 7.7 %collective-permute-start.31 = (f32[4,6,4,1]{3,2,1,0:T(4,128)S(1)}, f32[4,6,4,1]{3,2,1,0:T(4,128)S(1)}, u32[]{:S(2)}, u32[]{:S(2)}) collective-permute-start(f32[4,6,4,1]{3,2,1,0:T(4,128)S(1)} %get-tuple-element.350), channel_id=1, source_target_pairs={{1,0},{2,1},{3,2},{4,3},{5,4},{6,5},{7,6},{8,7},{9,8},{10,9},{11,1... | collective-permute-start | bytes 1160 | tf_op jit(solution)/shard_map/ppermute | solution.py:23
  393.9 5.9 collective-permute-start.33
  401.2 7.4 %collective-permute-start.35 = (f32[8,6,4,1]{3,2,1,0:T(4,128)S(1)}, f32[8,6,4,1]{3,2,1,0:T(4,128)S(1)}, u32[]{:S(2)}, u32[]{:S(2)}) collective-permute-start(f32[8,6,4,1]{3,2,1,0:T(4,128)S(1)} %get-tuple-element.270), channel_id=1, source_target_pairs={{1,0},{2,1},{3,2},{4,3},{5,4},{6,5},{7,6},{8,7},{9,8},{10,9},{11,1... | collective-permute-start | bytes 2312 | tf_op jit(solution)/shard_map/ppermute | solution.py:23
  403.2 6.7 collective-permute-start.34
  410.1 5.9 collective-permute-start.37
  417.1 7.1 collective-permute-start.39
  419.0 6.3 collective-permute-start.38
  548.9 7.7 %collective-permute-start.43 = (f32[4,6,4,1]{3,2,1,0:T(4,128)S(1)}, f32[4,6,4,1]{3,2,1,0:T(4,128)S(1)}, u32[]{:S(2)}, u32[]{:S(2)}) collective-permute-start(f32[4,6,4,1]{3,2,1,0:T(4,128)S(1)} %get-tuple-element.344), channel_id=1, source_target_pairs={{1,0},{2,1},{3,2},{4,3},{5,4},{6,5},{7,6},{8,7},{9,8},{10,9},{11,1... | collective-permute-start | bytes 1160 | tf_op jit(solution)/shard_map/ppermute | solution.py:23
  570.9 7.4 %collective-permute-start.47 = (f32[8,6,4,1]{3,2,1,0:T(4,128)S(1)}, f32[8,6,4,1]{3,2,1,0:T(4,128)S(1)}, u32[]{:S(2)}, u32[]{:S(2)}) collective-permute-start(f32[8,6,4,1]{3,2,1,0:T(4,128)S(1)} %get-tuple-element.268), channel_id=1, source_target_pairs={{1,0},{2,1},{3,2},{4,3},{5,4},{6,5},{7,6},{8,7},{9,8},{10,9},{11,1... | collective-permute-start | bytes 2312 | tf_op jit(solution)/shard_map/ppermute | solution.py:23
  572.9 6.7 collective-permute-start.46
  579.8 5.9 collective-permute-start.49
  586.8 7.1 collective-permute-start.51
  588.7 6.3 collective-permute-start.50
  (63 other events, 903.2 us)
where the time goes:
time: 723 us; the launch traced here: 711 us
  blocking collectives  446 us (62%)
  starting transfers between devices  171 us (24%)
  other arithmetic  39.5 us (5%)
  waiting for transfers between devices  23.9 us (3%)
  local copies, waits for them, and re-layouts  22.4 us (3%)
  between operations  8.86 us (1%)
    psum x4, blocking collectives, solve(): lax.psum((jnp.sum(residual * image), jnp.sum(image * image)), ('gx', 'gy'))  446 us
    ppermute x26, starting transfers between devices, padded(): lax.ppermute(lax.slice_in_dim(block, block.shape[dim] - width, None, axis...  116 us
    ppermute x26, starting transfers between devices, padded(): lax.ppermute(lax.slice_in_dim(block, 0, width, axis=dim), axis, backward)  54.6 us
    ppermute x26, waiting for transfers between devices, padded(): lax.ppermute(lax.slice_in_dim(block, block.shape[dim] - width, None, axis...  22.6 us
  transfers between devices with their start and end apart: 52, of which 26 were waited for; matrix products, arithmetic and copies ran while one was open for 1% of the time, Pallas kernels for 0%

commit v1 on v0

v1 whole, which is shorter than its diff:
```python
import functools

import jax
import jax.numpy as jnp
from jax import lax
from jax.experimental import pallas as pl
from jax.experimental.pallas import tpu as pltpu
from jax.sharding import PartitionSpec as P

PRIOR_WEIGHT = 0.05
EPSILON = 1e-06
OPPOSITE = (1, 0, 3, 2, 5, 4)
F32 = jnp.float32
LAYERS = 6
ROWS = 2
COLS = 256
WIDE = 384
HALO = 8
INV_AT, VIS_AT, SMALL_AT, DIAG1_AT, GROUPS = 16, 48, 50, 52, 68
SENT = 52
COUNT_ROW, PATTERN_ROW, RHS_ROW, BETA_ROW = 0, 1, 2, 4
HALO_TILES = 9


def iota(shape, dim):
    return lax.broadcasted_iota(jnp.int32, shape, dim)


def edge_lanes(shape):
    lane = iota(shape, 1)
    return (lane < HALO) | (lane >= 128 - HALO)


def prep_kernel(diag, inv, visc, count, grounded, pattern, beta, vel, own, to_west, to_east, north, south):
    layer = iota((LAYERS, COLS), 0)
    actives = [layer < count[r : r + 1, :] for r in range(ROWS)]
    lane = iota((8, 128), 1)
    north[...] = jnp.zeros(north.shape, F32)
    south[...] = jnp.zeros(south.shape, F32)

    def put(group, values, tile, slot, west=None, east=None):
        own[group, 0:LAYERS, :] = values
        own[group, LAYERS:8, :] = jnp.zeros((8 - LAYERS, COLS), F32)
        whole = own[group]
        if west is not None:
            to_west[west] = whole
        if east is not None:
            to_east[east] = whole
        shift = slot * 16 + HALO
        north[tile] += pltpu.roll(jnp.where(lane >= 128 - HALO, whole[:, 128:], 0.0), shift, 1)
        south[tile] += pltpu.roll(jnp.where(lane < HALO, whole[:, :128], 0.0), shift, 1)

    for half in range(2):

        def body(k, carry):
            cp = half * 8 + k
            eye = jnp.where(cp % 5 == 0, 1.0, 0.0).astype(F32)
            for r in range(ROWS):
                at = INV_AT + cp * 2 + r
                put(at, jnp.where(actives[r], inv[cp, :, r, :], eye), r * 2 + half, k, at, at - 16)
                values = jnp.where(actives[r], diag[cp, :, r, :], eye)
                if r == 0:
                    put(cp, values, 4 + half, k, cp, None)
                else:
                    put(DIAG1_AT + cp, values, 6 + half, k, None, DIAG1_AT - 16 + cp)
            return carry

        lax.fori_loop(0, 8, body, 0)
    for r in range(ROWS):
        at = VIS_AT + r
        put(at, jnp.where(actives[r], visc[:, r, :], 0.0), 8, r, at, at - 16)
        at = SMALL_AT + r
        row = slice(r, r + 1)
        force = -(grounded[row, :].astype(F32) * beta[row, :])
        own[at] = jnp.zeros((8, COLS), F32)
        own[at, COUNT_ROW : COUNT_ROW + 1, :] = count[row, :].astype(F32)
        own[at, PATTERN_ROW : PATTERN_ROW + 1, :] = pattern[row, :].astype(F32)
        own[at, RHS_ROW : RHS_ROW + 1, :] = force * vel[0, row, :]
        own[at, RHS_ROW + 1 : RHS_ROW + 2, :] = force * vel[1, row, :]
        own[at, BETA_ROW : BETA_ROW + 1, :] = beta[row, :]
        put(at, own[at, 0:LAYERS, :], 8, 2 + r, at, at - 16)


def unpack(tile, slot):
    rolled = pltpu.roll(tile, 128 - HALO - 16 * slot, 1)
    return jnp.where(edge_lanes((8, 128)), rolled, 0.0)


def block_times(table, base, values, transposed):
    out = []
    for c in range(4):
        total = None
        for k in range(4):
            entry = table[base + (k * 4 + c if transposed else c * 4 + k)] * values[k]
            total = entry if total is None else total + entry
        out.append(total)
    return out


def coupled(coupling, direction, values, transposed, sums):
    for c in range(4):
        for k in range(4):
            if transposed:
                factor = coupling[OPPOSITE[direction] * 16 + k * 4 + c]
            else:
                factor = coupling[direction * 16 + c * 4 + k]
            entry = factor * values[k]
            sums[c] = entry if sums[c] is None else sums[c] + entry
    return sums


def stencil(field, base, coupling, transposed, kappa):
    here = [field[base + c] for c in range(4)]
    sums = [None] * 4
    sums = coupled(coupling, 0, [pltpu.roll(h, 7, 0) for h in here], transposed, sums)
    sums = coupled(coupling, 1, [pltpu.roll(h, 1, 0) for h in here], transposed, sums)

    def weighted(direction, tiles):
        if kappa is None:
            return tiles
        weight = kappa(direction)
        return [weight * t for t in tiles]

    sums = coupled(coupling, 2, weighted(0, [field[base + 4 + c] for c in range(4)]), transposed, sums)
    sums = coupled(coupling, 3, weighted(1, [field[base - 4 + c] for c in range(4)]), transposed, sums)
    sums = coupled(
        coupling, 4, weighted(2, [pltpu.roll(h, WIDE - 1, 1) for h in here]), transposed, sums
    )
    sums = coupled(coupling, 5, weighted(3, [pltpu.roll(h, 1, 1) for h in here]), transposed, sums)
    return sums


def sweep(vectors, res, first, carried, update, image, inv, diag, vis, kappa, coupling, transposed):
    def initial(i, carry):
        row = i % 6
        values = [res[i * 4 + c] for c in range(4)]
        nu = vis[row]
        for c, y in enumerate(block_times(inv, row * 16, values, transposed)):
            first[i * 4 + c] = y
            carried[i * 4 + c] = nu * y
        return carry

    lax.fori_loop(0, vectors * 6, initial, 0)

    def correct(i, carry):
        v, row = i // 4, i % 4 + 1
        base = (v * 6 + row) * 4
        nu = vis[row]
        sums = stencil(
            carried, base, coupling, transposed, lambda d: kappa[(row - 1) * 4 + d]
        )
        y0 = [first[base + c] for c in range(4)]
        own = block_times(diag, (row - 1) * 16, y0, transposed)
        rest = [res[base + c] - own[c] + nu * sums[c] for c in range(4)]
        for c, y in enumerate(block_times(inv, row * 16, rest, transposed)):
            update[base + c] = y0[c] + y
        return carry

    lax.fori_loop(0, vectors * 4, correct, 0)

    def carry_on(i, carry):
        v, row = i // 4, i % 4 + 1
        base = (v * 6 + row) * 4
        nu = vis[row]
        for c in range(4):
            carried[base + c] = nu * update[base + c]
        return carry

    lax.fori_loop(0, vectors * 4, carry_on, 0)

    def apply(i, carry):
        v, row = i // 2, i % 2 + 2
        base = (v * 6 + row) * 4
        sums = stencil(carried, base, coupling, transposed, None)
        own = block_times(diag, (row - 1) * 16, [update[base + c] for c in range(4)], transposed)
        nu = vis[row]
        for c in range(4):
            image[i * 4 + c] = own[c] - nu * sums[c]
        return carry

    lax.fori_loop(0, vectors * 2, apply, 0)


def send_rows(message, vector, tiles):
    packed = jnp.zeros((8, 128), F32)
    keep = edge_lanes((8, 128))
    for t in range(8):
        tile = tiles[t]
        message[vector * 17 + 2 * t] = tile[:, 0:128]
        message[vector * 17 + 2 * t + 1] = tile[:, 128:256]
        packed += pltpu.roll(jnp.where(keep, tile[:, 256:], 0.0), 16 * t + HALO, 1)
    message[vector * 17 + 16] = packed


def receive_rows(res, vector, own, west, east):
    for source, row_at in ((west, 0), (east, 4)):
        packed = source[vector * 17 + 16]
        for t in range(8):
            at = (vector * 6 + row_at) * 4 + t
            res[at, :, 0:128] = source[vector * 17 + 2 * t]
            res[at, :, 128:256] = source[vector * 17 + 2 * t + 1]
            res[at, :, 256:] = unpack(packed, t)
    for t in range(8):
        res[(vector * 6 + 2) * 4 + t] = own[vector * 8 + t]


def layer_sums(update, vector, active_of, put):
    for c in range(2):
        for r in range(ROWS):
            tile = update[(vector * 6 + 2 + r) * 4 + c] * active_of(r)
            put(c * 2 + r, jnp.sum(tile, axis=0, keepdims=True))


def setup_kernel(
    coupling, own, west, east, halo_own, halo_west, halo_east,
    inv, diag, vis, kappa, spread, residual, image, sums, prior,
    small, res, first, carried, update,
):
    gx, gy = lax.axis_index("gx"), lax.axis_index("gy")
    nx, ny = lax.axis_size("gx"), lax.axis_size("gy")
    sources = ((west, halo_west, 0, 16), (own, halo_own, 2, 0), (east, halo_east, 4, 0))

    def place(target, at, source, group, halos, tile, slot):
        target[at, :, 0:COLS] = source[group]
        target[at, :, COLS:] = unpack(halos[tile], slot)

    for half in range(2):

        def body(k, carry):
            cp = half * 8 + k
            for source, halos, row, drop in sources:
                for r in range(ROWS):
                    group = INV_AT + cp * 2 + r - drop
                    place(inv, (row + r) * 16 + cp, source, group, halos, r * 2 + half, k)
            place(diag, cp, west, DIAG1_AT - 16 + cp, halo_west, 6 + half, k)
            place(diag, 16 + cp, own, cp, halo_own, 4 + half, k)
            place(diag, 32 + cp, own, DIAG1_AT + cp, halo_own, 6 + half, k)
            place(diag, 48 + cp, east, cp, halo_east, 4 + half, k)
            return carry

        lax.fori_loop(0, 8, body, 0)
    for source, halos, row, drop in sources:
        for r in range(ROWS):
            place(vis, row + r, source, VIS_AT + r - drop, halos, 8, r)
            place(small, row + r, source, SMALL_AT + r - drop, halos, 8, 2 + r)

    lane = iota((1, WIDE), 1)
    column = jnp.where(lane < COLS, lane, jnp.where(lane < COLS + 64, lane - COLS, lane - 128))
    block_y = gy + jnp.where(lane < COLS, 0, jnp.where(lane < COLS + 64, 1, -1))
    south_on = jnp.where((column == 0) & (block_y > 0), 1.0, 0.0)
    north_on = jnp.where((column == COLS - 1) & (block_y < ny - 1), 1.0, 0.0)
    south_in = jnp.where(column == 0, 0.0, 1.0)
    north_in = jnp.where(column == COLS - 1, 0.0, 1.0)
    layer = iota((8, WIDE), 0)
    for row in range(6):
        tile = small[row]
        counts = tile[COUNT_ROW : COUNT_ROW + 1]
        whole = jnp.maximum(counts, 1.0)
        active = jnp.where(layer.astype(F32) < counts, 1.0, 0.0)
        spread[row] = -active / (whole * whole)
        for c in range(2):
            rhs = tile[RHS_ROW + c : RHS_ROW + c + 1]
            res[row * 4 + c] = jnp.where(layer == 0, rhs, 0.0)
        for c in range(2, 4):
            res[row * 4 + c] = jnp.zeros((8, WIDE), F32)
        if row == 0 or row == 5:
            continue
        block_x = gx + (row // 2 - 1)
        level = (1.0 + tile[PATTERN_ROW : PATTERN_ROW + 1]) / 5.0
        first_row = row % 2 == 0
        side = jnp.where(block_x > 0, 1.0, 0.0) if first_row else jnp.where(block_x < nx - 1, 1.0, 0.0)
        shared = south_on + north_on + side
        own_weight = jnp.where(shared > 0, level, 1.0)
        near = (1.0 - own_weight) / jnp.maximum(shared, 1.0)
        rim = near * (south_on + north_on)
        away = own_weight
        toward = own_weight + near * side
        east_part = away + rim if first_row else toward
        west_part = toward if first_row else away + rim
        north_part = own_weight + near * (north_on + side * north_in)
        south_part = own_weight + near * (south_on + side * south_in)
        for d, part in enumerate((east_part, west_part, north_part, south_part)):
            kappa[(row - 1) * 4 + d] = jnp.broadcast_to(part, (8, WIDE))

    prior[...] = jnp.zeros(prior.shape, F32)
    for r in range(ROWS):
        betas = [small[2 + r + k] for k in (-1, 0, 1)]
        around = (
            betas[0] + betas[2] + pltpu.roll(betas[1], 1, 1) + pltpu.roll(betas[1], WIDE - 1, 1)
        )
        line = 4.0 * betas[1] - around
        prior[r : r + 1, :] = line[BETA_ROW : BETA_ROW + 1, :COLS]

    sweep(1, res, first, carried, update, image, inv, diag, vis, kappa, coupling, False)
    for t in range(8):
        residual[t] = res[8 + t] - image[t]
    sums[...] = jnp.zeros(sums.shape, F32)

    def put(at, line):
        sums[at : at + 1, :] = line

    def active_of(r):
        return jnp.where(spread[2 + r] < 0.0, 1.0, 0.0)

    layer_sums(update, 0, active_of, put)


def first_kernel(*refs):
    outs = refs[7:16]
    message = refs[16]
    setup_kernel(*refs[:7], *outs, *refs[17:])
    residual = outs[5]
    send_rows(message, 0, [residual[t] for t in range(8)])


def dots_of(residual, image, last, pairs, vectors, lane):
    total = jnp.zeros((8, 128), F32)
    at = 0

    def dot(x, i, y, j):
        part = jnp.zeros((8, 128), F32)
        for t in range(8):
            product = x[i * 8 + t, :, 0:COLS] * y[j * 8 + t, :, 0:COLS]
            part += product[:, 0:128] + product[:, 128:256]
        return part

    for x, y in ((image, image), (residual, image), (residual, last), (image, last), (last, last)):
        for i, j in pairs:
            part = dot(x, i, y, j)
            if i != j and x is not y:
                part += dot(x, j, y, i)
            elif i != j:
                part += part
            line = jnp.sum(part, axis=0, keepdims=True)
            total += jnp.where(lane == at, jnp.sum(line, axis=1, keepdims=True), 0.0)
            at += 1
    return total


def second_kernel(
    coupling, inv, diag, vis, kappa, spread, residual, image, sums, west, east,
    uv, dots,
    res, first, carried, update, last,
):
    receive_rows(res, 0, residual, west, east)
    sweep(1, res, first, carried, update, last, inv, diag, vis, kappa, coupling, False)
    uv[0:4, :] = sums[0:4, :]

    def put(at, line):
        uv[4 + at : 5 + at, :] = line

    def active_of(r):
        return jnp.where(spread[2 + r] < 0.0, 1.0, 0.0)

    layer_sums(update, 0, active_of, put)
    dots[...] = dots_of(residual, image, last, ((0, 0),), 1, iota((8, 128), 1))


def third_kernel(
    coupling, inv, diag, vis, kappa, spread, uv, west, east,
    residual, image, start, message,
    res, first, carried, update,
):
    for v in range(2):
        for row in range(6):
            source = (west, uv, east)[row // 2]
            for c in range(2):
                at = v * 4 + c * 2 + row % 2
                res[(v * 6 + row) * 4 + c] = spread[row] * source[at : at + 1, :]
            for c in range(2, 4):
                res[(v * 6 + row) * 4 + c] = jnp.zeros((8, WIDE), F32)
    sweep(2, res, first, carried, update, image, inv, diag, vis, kappa, coupling, True)
    for v in range(2):
        for t in range(8):
            at = (v * 6 + 2) * 4 + t
            residual[v * 8 + t] = res[at] - image[v * 8 + t]
            start[v * 8 + t] = update[at, :, 0:COLS]
        send_rows(message, v, [residual[v * 8 + t] for t in range(8)])


def fourth_kernel(
    coupling, inv, diag, vis, kappa, residual, image, west, east, dots,
    end, spread_dots,
    res, first, carried, update, last,
):
    for v in range(2):
        receive_rows(res, v, residual, west, east)
    sweep(2, res, first, carried, update, last, inv, diag, vis, kappa, coupling, True)
    for v in range(2):
        for t in range(8):
            end[v * 8 + t] = update[(v * 6 + 2) * 4 + t, :, 0:COLS]
    lane = iota((8, 128), 1)
    pairs = ((0, 0), (0, 1), (1, 1))
    adjoint_dots = dots_of(residual, image, last, pairs, 2, lane - 5)
    line = (dots[...] + adjoint_dots)[0:1]
    spread_dots[...] = jnp.broadcast_to(line, spread_dots.shape)


def steps(image2, residual_image, residual_last, image_last, last2):
    one = (residual_image + image2) / (image2 + EPSILON)
    off = 1.0 - one
    along = off * residual_image + one * residual_last + off * off * image2 + off * one * image_last
    squared = off * off * image2 + 2.0 * off * one * image_last + one * one * last2
    two = along / (squared + EPSILON)
    return one + two * off, one * two


def final_kernel(dots, start, end, prior, grounded, vel, hessian, adjoint):
    line = jnp.sum(dots[...], axis=0, keepdims=True)
    lane = iota((1, 128), 1)

    def get(k):
        return jnp.sum(jnp.where(lane == k, line, 0.0), axis=1, keepdims=True)

    a, b = steps(*[get(k) for k in range(5)])
    kinds = []
    for k in range(5):
        at = 5 + 3 * k
        kinds.append(a * a * get(at) + a * b * get(at + 1) + b * b * get(at + 2))
    p, q = steps(*kinds)
    weights = (p * a, p * b, q * a, q * b)
    lines = []
    for r in range(ROWS):
        for c in range(4):
            t = r * 4 + c
            total = (
                weights[0] * start[t]
                + weights[1] * start[8 + t]
                + weights[2] * end[t]
                + weights[3] * end[8 + t]
            )
            adjoint[c, :, r, :] = total[0:LAYERS]
            lines.append(total[0:1])
    for r in range(ROWS):
        row = slice(r, r + 1)
        data = grounded[row, :].astype(F32) * (
            vel[0, row, :] * lines[r * 4] + vel[1, row, :] * lines[r * 4 + 1]
        )
        hessian[row, :] = data + PRIOR_WEIGHT * prior[row, :]


VMEM = pl.BlockSpec(memory_space=pltpu.VMEM)
SMEM = pl.BlockSpec(memory_space=pltpu.SMEM)


def call(kernel, name, operands, outs, scratch=(), smem=True):
    return pl.pallas_call(
        kernel,
        out_shape=[jax.ShapeDtypeStruct(shape, F32) for shape in outs],
        in_specs=[SMEM if i == 0 and smem else VMEM for i in range(len(operands))],
        out_specs=[VMEM] * len(outs),
        scratch_shapes=[pltpu.VMEM(shape, F32) for shape in scratch],
        compiler_params=pltpu.CompilerParams(vmem_limit_bytes=40 * 1024 * 1024),
        name=name,
    )(*operands)


def shift_pairs(axis, step):
    count = lax.axis_size(axis)
    return [(i, i + step) for i in range(count) if 0 <= i + step < count]


def from_low(values, axis):
    return lax.ppermute(values, axis, shift_pairs(axis, 1))


def from_high(values, axis):
    return lax.ppermute(values, axis, shift_pairs(axis, -1))


def total_over(lines, axis, fan_out):
    swapped = lax.all_to_all(lines, axis, 0, 0, tiled=True)
    if fan_out is None:
        return swapped
    return jnp.broadcast_to(jnp.sum(swapped, axis=0, keepdims=True), (fan_out, 128))


def per_device(
    diag_block,
    block_inverse,
    viscosity,
    coupling,
    active_layers,
    grounded,
    weight_pattern,
    beta_step,
    base_vel,
):
    table = (16,) + viscosity.shape
    factors = coupling.reshape(96)
    own, to_west, to_east, to_north, to_south = call(
        prep_kernel,
        "prepare",
        [
            diag_block.reshape(table),
            block_inverse.reshape(table),
            viscosity,
            active_layers,
            grounded,
            weight_pattern,
            beta_step,
            base_vel,
        ],
        [
            (GROUPS, 8, COLS),
            (SENT, 8, COLS),
            (SENT, 8, COLS),
            (HALO_TILES, 8, 128),
            (HALO_TILES, 8, 128),
        ],
        smem=False,
    )
    halo_own = from_low(to_north, "gy") + from_high(to_south, "gy")
    west, east = from_low(to_east, "gx"), from_high(to_west, "gx")
    halo_west, halo_east = from_low(halo_own, "gx"), from_high(halo_own, "gx")

    def field(count):
        return (count, 8, WIDE)

    def work(vectors):
        return [field(24 * vectors)] * 4

    inv, diag, vis, kappa, spread, residual, image, sums, prior, message = call(
        first_kernel,
        "forward_first",
        [factors, own, west, east, halo_own, halo_west, halo_east],
        [
            field(96),
            field(64),
            field(6),
            field(16),
            field(6),
            field(8),
            field(8),
            (8, WIDE),
            (8, COLS),
            (17, 8, 128),
        ],
        [field(6)] + work(1),
    )
    west, east = from_low(message, "gx"), from_high(message, "gx")
    uv, dots = call(
        second_kernel,
        "forward_second",
        [factors, inv, diag, vis, kappa, spread, residual, image, sums, west, east],
        [(8, WIDE), (8, 128)],
        work(1) + [field(8)],
    )
    west, east = from_low(uv, "gx"), from_high(uv, "gx")
    residual, image, start, message = call(
        third_kernel,
        "adjoint_first",
        [factors, inv, diag, vis, kappa, spread, uv, west, east],
        [field(16), field(16), (16, 8, COLS), (34, 8, 128)],
        work(2),
    )
    west, east = from_low(message, "gx"), from_high(message, "gx")
    n_gx, n_gy = lax.axis_size("gx"), lax.axis_size("gy")
    end, lines = call(
        fourth_kernel,
        "adjoint_second",
        [factors, inv, diag, vis, kappa, residual, image, west, east, dots],
        [(16, 8, COLS), (n_gx, 128)],
        work(2) + [field(16)],
    )
    lines = total_over(lines, "gx", n_gy)
    lines = total_over(lines, "gy", None)
    hessian_vec, adjoint = call(
        final_kernel,
        "combine",
        [lines, start, end, prior, grounded, base_vel],
        [beta_step.shape, (4,) + viscosity.shape],
        smem=False,
    )
    return hessian_vec, adjoint


def solution(mesh):
    placed = (
        P(None, None, None, "gx", "gy"),
        P(None, None, None, "gx", "gy"),
        P(None, "gx", "gy"),
        P(),
        P("gx", "gy"),
        P("gx", "gy"),
        P("gx", "gy"),
        P("gx", "gy"),
        P(None, "gx", "gy"),
    )
    return jax.shard_map(
        per_device,
        mesh=mesh,
        in_specs=placed,
        out_specs=(P("gx", "gy"), P(None, None, "gx", "gy")),
        check_vma=False,
    )
```

time: 723 us -> 119 us (0.16); the launches traced: 711 us -> 119 us
  blocking collectives: 446 us -> 54.3 us
  starting transfers between devices: 171 us -> 35.8 us
  other arithmetic: 39.5 us -> 0.06 us
  waiting for transfers between devices: 23.9 us -> 7.71 us
  local copies, waits for them, and re-layouts: 22.4 us -> 6.88 us
  Pallas kernels: 0 us -> 13.2 us
  between operations: 8.86 us -> 0.78 us
    psum x4 -> x0, blocking collectives: 446 us -> none  [solve(): lax.psum((jnp.sum(residual * image), jnp.sum(image * image)), ('gx', 'gy'))]
    ppermute x52 -> x12, starting transfers between devices: 171 us -> 35.8 us  [the longest x6 26.8 us: from_low(): return lax.ppermute(values, axis, shift_pairs(axis, 1))]
    all_to_all x0 -> x2, blocking collectives: none -> 54.3 us  [total_over(): swapped = lax.all_to_all(lines, axis, 0, 0, tiled=True)]
    reduce_sum x66 -> x1, other arithmetic: 17.9 us -> 0.05 us  [total_over(): jnp.sum(swapped, axis=0, keepdims=True)]
    ppermute x52 -> x12, waiting for transfers between devices: 23.9 us -> 7.71 us  [the longest x6 4.19 us: from_low(): return lax.ppermute(values, axis, shift_pairs(axis, 1))]
    pallas_call x0 -> x6, Pallas kernels: none -> 13.2 us  [call(): pl.pallas_call(kernel, out_shape=[jax.ShapeDtypeStruct(shape, F32) for sh...]
    slice x80 -> x0, local copies, waits for them, and re-layouts: 8.03 us -> none  [the longest x26 2.45 us: padded(): lax.slice_in_dim(block, block.shape[dim] - width, None, axis=dim)]
    scatter x10 -> x0, local copies, waits for them, and re-layouts: 7.34 us -> none  [the longest x8 7.31 us: schwarz(): pack_y = jnp.zeros_like(own_part).at[:, :, :, 0].set(solved[:, :, 1:-1, 0...]
  transfers between devices with their start and end apart: 52 -> 12, of which waited for: 26 -> 6; matrix products, arithmetic and copies ran while one was open for 1% -> 1% of each run, Pallas kernels for 0% -> 0%
where the time goes in v1:
time: 119 us
  blocking collectives  54.3 us (46%)
  starting transfers between devices  35.8 us (30%)
  Pallas kernels  13.2 us (11%)
  waiting for transfers between devices  7.71 us (6%)
  local copies, waits for them, and re-layouts  6.88 us (6%)
    all_to_all x2, blocking collectives, total_over(): swapped = lax.all_to_all(lines, axis, 0, 0, tiled=True)  54.3 us
    ppermute x6, starting transfers between devices, from_low(): return lax.ppermute(values, axis, shift_pairs(axis, 1))  26.8 us
    pallas_call x6, Pallas kernels, call(): pl.pallas_call(kernel, out_shape=[jax.ShapeDtypeStruct(shape, F32) for sh...  13.2 us
    ppermute x6, starting transfers between devices, from_high(): return lax.ppermute(values, axis, shift_pairs(axis, -1))  9.01 us
    unnamed x21, local copies, waits for them, and re-layouts  6.77 us
    ppermute x6, waiting for transfers between devices, from_low(): return lax.ppermute(values, axis, shift_pairs(axis, 1))  4.19 us
    ppermute x6, waiting for transfers between devices, from_high(): return lax.ppermute(values, axis, shift_pairs(axis, -1))  3.52 us
  transfers between devices with their start and end apart: 12, of which 6 were waited for; matrix products, arithmetic and copies ran while one was open for 1% of the time, Pallas kernels for 0%

profile of v1, /device:TPU:1, one launch (start us, length us, event | category | flops | bytes accessed | tf_op | source)
XLA Modules:
  0.0 118.7 jit_solution(9348698556469123554)
XLA Ops:
  0.6 0.9 copy-done
  1.6 0.9 copy-done.1
  2.5 0.7 copy-done.2
  3.2 0.7 copy-done.4
  3.9 0.7 copy-done.5
  5.2 0.7 copy-done.8
  5.9 0.7 copy-done.9
  6.6 1.8 %prepare.1 = (f32[68,8,256]{2,1,0:T(8,128)S(1)}, f32[52,8,256]{2,1,0:T(8,128)S(1)}, f32[52,8,256]{2,1,0:T(8,128)S(1)}, f32[9,8,128]{2,1,0:T(8,128)S(1)}, f32[9,8,128]{2,1,0:T(8,128)S(1)}) custom-call(f32[16,6,2,256]{3,2,1,0:T(2,128)S(1)} %bitcast.6, f32[16,6,2,256]{3,2,1,0:T(2,128)S(1)} %bitcast.7, f32[6,2,256]{2,1,0:T(2,128)S(1)} %copy-done.4, ...), custom_call_target="tpu_custom_call" | custom-call | tf_op jit(solution)/shard_map/prepare/pallas_call | solution.py:447
  8.4 4.0 %collective-permute-start = (f32[52,8,256]{2,1,0:T(8,128)S(1)}, f32[52,8,256]{2,1,0:T(8,128)S(1)}, u32[]{:S(2)}, u32[]{:S(2)}) collective-permute-start(f32[52,8,256]{2,1,0:T(8,128)S(1)} %get-tuple-element.26), channel_id=1, source_target_pairs={{0,16},{16,32},{32,48},{48,64},{64,80},{80,96},{96,112},{112,128},... | collective-permute-start | bytes 1277960 | tf_op jit(solution)/shard_map/ppermute | solution.py:464
  12.4 1.3 %collective-permute-start.1 = (f32[52,8,256]{2,1,0:T(8,128)S(1)}, f32[52,8,256]{2,1,0:T(8,128)S(1)}, u32[]{:S(2)}, u32[]{:S(2)}) collective-permute-start(f32[52,8,256]{2,1,0:T(8,128)S(1)} %get-tuple-element.27), channel_id=1, source_target_pairs={{16,0},{32,16},{48,32},{64,48},{80,64},{96,80},{112,96},{128,112},... | collective-permute-start | bytes 1277960 | tf_op jit(solution)/shard_map/ppermute | solution.py:468
  13.7 4.8 %collective-permute-start.2 = (f32[9,8,128]{2,1,0:T(8,128)S(1)}, f32[9,8,128]{2,1,0:T(8,128)S(1)}, u32[]{:S(2)}, u32[]{:S(2)}) collective-permute-start(f32[9,8,128]{2,1,0:T(8,128)S(1)} %get-tuple-element.28), channel_id=1, source_target_pairs={{0,1},{1,2},{2,3},{3,4},{4,5},{5,6},{6,7},{7,8},{8,9},{9,10},{10,1... | collective-permute-start | bytes 110600 | tf_op jit(solution)/shard_map/ppermute | solution.py:464
  18.5 2.6 %collective-permute-start.3 = (f32[9,8,128]{2,1,0:T(8,128)S(1)}, f32[9,8,128]{2,1,0:T(8,128)S(1)}, u32[]{:S(2)}, u32[]{:S(2)}) collective-permute-start(f32[9,8,128]{2,1,0:T(8,128)S(1)} %get-tuple-element.29), channel_id=1, source_target_pairs={{1,0},{2,1},{3,2},{4,3},{5,4},{6,5},{7,6},{8,7},{9,8},{10,9},{11,1... | collective-permute-start | bytes 110600 | tf_op jit(solution)/shard_map/ppermute | solution.py:468
  21.1 3.0 %collective-permute-done.3 = f32[9,8,128]{2,1,0:T(8,128)S(1)} collective-permute-done((f32[9,8,128]{2,1,0:T(8,128)S(1)}, f32[9,8,128]{2,1,0:T(8,128)S(1)}, u32[]{:S(2)}, u32[]{:S(2)}) %collective-permute-start.3) | collective-permute-done | bytes 36896 | tf_op jit(solution)/shard_map/ppermute | solution.py:468
  24.1 1.3 %collective-permute-start.5 = (f32[9,8,128]{2,1,0:T(8,128)S(1)}, f32[9,8,128]{2,1,0:T(8,128)S(1)}, u32[]{:S(2)}, u32[]{:S(2)}) collective-permute-start(f32[9,8,128]{2,1,0:T(8,128)S(1)} %add.3.refs_4_), channel_id=1, source_target_pairs={{16,0},{32,16},{48,32},{64,48},{80,64},{96,80},{112,96},{128,112},... | collective-permute-start | bytes 110600 | tf_op jit(solution)/shard_map/ppermute | solution.py:468
  25.4 4.9 %collective-permute-start.4 = (f32[9,8,128]{2,1,0:T(8,128)S(1)}, f32[9,8,128]{2,1,0:T(8,128)S(1)}, u32[]{:S(2)}, u32[]{:S(2)}) collective-permute-start(f32[9,8,128]{2,1,0:T(8,128)S(1)} %add.3.refs_4_), channel_id=1, source_target_pairs={{0,16},{16,32},{32,48},{48,64},{64,80},{80,96},{96,112},{112,128},... | collective-permute-start | bytes 110600 | tf_op jit(solution)/shard_map/ppermute | solution.py:464
  30.3 0.8 copy.13
  31.4 3.1 %forward_first.1 = (f32[96,8,384]{2,1,0:T(8,128)S(1)}, f32[64,8,384]{2,1,0:T(8,128)S(1)}, f32[6,8,384]{2,1,0:T(8,128)S(1)}, f32[16,8,384]{2,1,0:T(8,128)S(1)}, f...) custom-call(f32[96]{0:T(128)S(1)} %reshape.21.refs_0_.coupling, ...), custom_call_target="tpu_custom_call" | custom-call | tf_op jit(solution)/shard_map/forward_first/pallas_call | solution.py:447
  34.5 1.3 %collective-permute-start.7 = (f32[17,8,128]{2,1,0:T(8,128)S(1)}, f32[17,8,128]{2,1,0:T(8,128)S(1)}, u32[]{:S(2)}, u32[]{:S(2)}) collective-permute-start(f32[17,8,128]{2,1,0:T(8,128)S(1)} %get-tuple-element.38), channel_id=1, source_target_pairs={{16,0},{32,16},{48,32},{64,48},{80,64},{96,80},{112,96},{128,112},... | collective-permute-start | bytes 208904 | tf_op jit(solution)/shard_map/ppermute | solution.py:468
  35.8 4.3 %collective-permute-start.6 = (f32[17,8,128]{2,1,0:T(8,128)S(1)}, f32[17,8,128]{2,1,0:T(8,128)S(1)}, u32[]{:S(2)}, u32[]{:S(2)}) collective-permute-start(f32[17,8,128]{2,1,0:T(8,128)S(1)} %get-tuple-element.38), channel_id=1, source_target_pairs={{0,16},{16,32},{32,48},{48,64},{64,80},{80,96},{96,112},{112,128},... | collective-permute-start | bytes 208904 | tf_op jit(solution)/shard_map/ppermute | solution.py:464
  40.1 1.8 %collective-permute-done.6.west = f32[17,8,128]{2,1,0:T(8,128)S(1)} collective-permute-done((f32[17,8,128]{2,1,0:T(8,128)S(1)}, f32[17,8,128]{2,1,0:T(8,128)S(1)}, u32[]{:S(2)}, u32[]{:S(2)}) %collective-permute-start.6) | collective-permute-done | bytes 69664 | tf_op jit(solution)/shard_map/ppermute | solution.py:464
  41.8 1.8 %forward_second.1 = (f32[8,384]{1,0:T(8,128)S(1)}, f32[8,128]{1,0:T(8,128)S(1)}) custom-call(f32[96]{0:T(128)S(1)} %reshape.21.refs_0_.coupling, f32[96,8,384]{2,1,0:T(8,128)S(1)} %get-tuple-element.30.inv, f32[64,8,384]{2,1,0:T(8,128)S(1)} %get-tuple-element.31.diag, f32[6,8,384]{2,1,0:T(8,128)S(1)} %get-tuple-element.32.vis, ...), custom_call_target="tpu_custom_call" | custom-call | tf_op jit(solution)/shard_map/forward_second/pallas_call | solution.py:447
  43.6 1.3 %collective-permute-start.9 = (f32[8,384]{1,0:T(8,128)S(1)}, f32[8,384]{1,0:T(8,128)S(1)}, u32[]{:S(2)}, u32[]{:S(2)}) collective-permute-start(f32[8,384]{1,0:T(8,128)S(1)} %get-tuple-element.39.uv), channel_id=1, source_target_pairs={{16,0},{32,16},{48,32},{64,48},{80,64},{96,80},{112,96},{128,112},... | collective-permute-start | bytes 36872 | tf_op jit(solution)/shard_map/ppermute | solution.py:468
  44.9 4.6 %collective-permute-start.8 = (f32[8,384]{1,0:T(8,128)S(1)}, f32[8,384]{1,0:T(8,128)S(1)}, u32[]{:S(2)}, u32[]{:S(2)}) collective-permute-start(f32[8,384]{1,0:T(8,128)S(1)} %get-tuple-element.39.uv), channel_id=1, source_target_pairs={{0,16},{16,32},{32,48},{48,64},{64,80},{80,96},{96,112},{112,128},... | collective-permute-start | bytes 36872 | tf_op jit(solution)/shard_map/ppermute | solution.py:464
  49.5 0.8 collective-permute-done.8.west
  50.3 2.8 %adjoint_first.1 = (f32[16,8,384]{2,1,0:T(8,128)S(1)}, f32[16,8,384]{2,1,0:T(8,128)S(1)}, f32[16,8,256]{2,1,0:T(8,128)S(1)}, f32[34,8,128]{2,1,0:T(8,128)S(1)}) custom-call(f32[96]{0:T(128)S(1)} %reshape.21.refs_0_.coupling, f32[96,8,384]{2,1,0:T(8,128)S(1)} %get-tuple-element.30.inv, f32[64,8,384]{2,1,0:T(8,128)S(1)} %get-tuple-element.31.diag, ...), custom_call_target="tpu_custom_call" | custom-call | tf_op jit(solution)/shard_map/adjoint_first/pallas_call | solution.py:447
  53.1 1.3 %collective-permute-start.11 = (f32[34,8,128]{2,1,0:T(8,128)S(1)}, f32[34,8,128]{2,1,0:T(8,128)S(1)}, u32[]{:S(2)}, u32[]{:S(2)}) collective-permute-start(f32[34,8,128]{2,1,0:T(8,128)S(1)} %get-tuple-element.42), channel_id=1, source_target_pairs={{16,0},{32,16},{48,32},{64,48},{80,64},{96,80},{112,96},{128,112},... | collective-permute-start | bytes 417800 | tf_op jit(solution)/shard_map/ppermute | solution.py:468
  54.4 4.3 %collective-permute-start.10 = (f32[34,8,128]{2,1,0:T(8,128)S(1)}, f32[34,8,128]{2,1,0:T(8,128)S(1)}, u32[]{:S(2)}, u32[]{:S(2)}) collective-permute-start(f32[34,8,128]{2,1,0:T(8,128)S(1)} %get-tuple-element.42), channel_id=1, source_target_pairs={{0,16},{16,32},{32,48},{48,64},{64,80},{80,96},{96,112},{112,128},... | collective-permute-start | bytes 417800 | tf_op jit(solution)/shard_map/ppermute | solution.py:464
  59.1 1.5 %collective-permute-done.10.west = f32[34,8,128]{2,1,0:T(8,128)S(1)} collective-permute-done((f32[34,8,128]{2,1,0:T(8,128)S(1)}, f32[34,8,128]{2,1,0:T(8,128)S(1)}, u32[]{:S(2)}, u32[]{:S(2)}) %collective-permute-start.10) | collective-permute-done | bytes 139296 | tf_op jit(solution)/shard_map/ppermute | solution.py:464
  60.6 2.9 %adjoint_second.1 = (f32[16,8,256]{2,1,0:T(8,128)S(1)}, f32[32,128]{1,0:T(8,128)S(1)}) custom-call(f32[96]{0:T(128)S(1)} %reshape.21.refs_0_.coupling, f32[96,8,384]{2,1,0:T(8,128)S(1)} %get-tuple-element.30.inv, f32[64,8,384]{2,1,0:T(8,128)S(1)} %get-tuple-element.31.diag, f32[6,8,384]{2,1,0:T(8,128)S(1)} %get-tuple-element.32.vis, ...), custom_call_target="tpu_custom_call" | custom-call | tf_op jit(solution)/shard_map/adjoint_second/pallas_call | solution.py:447
  63.5 32.1 %all_to_all.17 = f32[32,1,128]{2,1,0:T(1,128)S(1)} all-to-all(f32[32,1,128]{2,1,0:T(1,128)S(1)} %bitcast.9), channel_id=1, replica_groups=mesh['gx'=32,'gy'=16] {'gx'}, dimensions={0} | all-to-all | bytes 32768 | tf_op jit(solution)/shard_map/all_to_all | solution.py:472
  95.7 22.2 %all_to_all.18 = f32[16,1,128]{2,1,0:T(1,128)S(1)} all-to-all(f32[16,1,128]{2,1,0:T(1,128)S(1)} %broadcast_in_dim.2), channel_id=1, replica_groups=mesh['gx'=32,'gy'=16] {'gy'}, dimensions={0} | all-to-all | bytes 16384 | tf_op jit(solution)/shard_map/all_to_all | solution.py:472
  117.9 0.8 combine.1
  (25 shorter events, 1.5 us)
Async XLA Ops:
  0.6 0.9 copy-start
  1.6 0.9 copy-start.1
  2.5 0.7 copy-start.2
  3.2 0.7 copy-start.4
  3.9 0.7 copy-start.5
  4.6 0.7 copy-start.7
  5.2 0.7 copy-start.8
  5.9 0.7 copy-start.9
  8.4 22.9 %collective-permute-start = (f32[52,8,256]{2,1,0:T(8,128)S(1)}, f32[52,8,256]{2,1,0:T(8,128)S(1)}, u32[]{:S(2)}, u32[]{:S(2)}) collective-permute-start(f32[52,8,256]{2,1,0:T(8,128)S(1)} %get-tuple-element.26), channel_id=1, source_target_pairs={{0,16},{16,32},{32,48},{48,64},{64,80},{80,96},{96,112},{112,128},... | collective-permute-start | bytes 1277960 | tf_op jit(solution)/shard_map/ppermute | solution.py:464
  12.4 19.0 %collective-permute-start.1 = (f32[52,8,256]{2,1,0:T(8,128)S(1)}, f32[52,8,256]{2,1,0:T(8,128)S(1)}, u32[]{:S(2)}, u32[]{:S(2)}) collective-permute-start(f32[52,8,256]{2,1,0:T(8,128)S(1)} %get-tuple-element.27), channel_id=1, source_target_pairs={{16,0},{32,16},{48,32},{64,48},{80,64},{96,80},{112,96},{128,112},... | collective-permute-start | bytes 1277960 | tf_op jit(solution)/shard_map/ppermute | solution.py:468
  13.7 7.4 %collective-permute-start.2 = (f32[9,8,128]{2,1,0:T(8,128)S(1)}, f32[9,8,128]{2,1,0:T(8,128)S(1)}, u32[]{:S(2)}, u32[]{:S(2)}) collective-permute-start(f32[9,8,128]{2,1,0:T(8,128)S(1)} %get-tuple-element.28), channel_id=1, source_target_pairs={{0,1},{1,2},{2,3},{3,4},{4,5},{5,6},{6,7},{7,8},{8,9},{9,10},{10,1... | collective-permute-start | bytes 110600 | tf_op jit(solution)/shard_map/ppermute | solution.py:464
  18.5 5.6 %collective-permute-start.3 = (f32[9,8,128]{2,1,0:T(8,128)S(1)}, f32[9,8,128]{2,1,0:T(8,128)S(1)}, u32[]{:S(2)}, u32[]{:S(2)}) collective-permute-start(f32[9,8,128]{2,1,0:T(8,128)S(1)} %get-tuple-element.29), channel_id=1, source_target_pairs={{1,0},{2,1},{3,2},{4,3},{5,4},{6,5},{7,6},{8,7},{9,8},{10,9},{11,1... | collective-permute-start | bytes 110600 | tf_op jit(solution)/shard_map/ppermute | solution.py:468
  24.1 7.1 %collective-permute-start.5 = (f32[9,8,128]{2,1,0:T(8,128)S(1)}, f32[9,8,128]{2,1,0:T(8,128)S(1)}, u32[]{:S(2)}, u32[]{:S(2)}) collective-permute-start(f32[9,8,128]{2,1,0:T(8,128)S(1)} %add.3.refs_4_), channel_id=1, source_target_pairs={{16,0},{32,16},{48,32},{64,48},{80,64},{96,80},{112,96},{128,112},... | collective-permute-start | bytes 110600 | tf_op jit(solution)/shard_map/ppermute | solution.py:468
  25.4 5.9 %collective-permute-start.4 = (f32[9,8,128]{2,1,0:T(8,128)S(1)}, f32[9,8,128]{2,1,0:T(8,128)S(1)}, u32[]{:S(2)}, u32[]{:S(2)}) collective-permute-start(f32[9,8,128]{2,1,0:T(8,128)S(1)} %add.3.refs_4_), channel_id=1, source_target_pairs={{0,16},{16,32},{32,48},{48,64},{64,80},{80,96},{96,112},{112,128},... | collective-permute-start | bytes 110600 | tf_op jit(solution)/shard_map/ppermute | solution.py:464
  34.5 5.6 %collective-permute-start.7 = (f32[17,8,128]{2,1,0:T(8,128)S(1)}, f32[17,8,128]{2,1,0:T(8,128)S(1)}, u32[]{:S(2)}, u32[]{:S(2)}) collective-permute-start(f32[17,8,128]{2,1,0:T(8,128)S(1)} %get-tuple-element.38), channel_id=1, source_target_pairs={{16,0},{32,16},{48,32},{64,48},{80,64},{96,80},{112,96},{128,112},... | collective-permute-start | bytes 208904 | tf_op jit(solution)/shard_map/ppermute | solution.py:468
  35.8 6.1 %collective-permute-start.6 = (f32[17,8,128]{2,1,0:T(8,128)S(1)}, f32[17,8,128]{2,1,0:T(8,128)S(1)}, u32[]{:S(2)}, u32[]{:S(2)}) collective-permute-start(f32[17,8,128]{2,1,0:T(8,128)S(1)} %get-tuple-element.38), channel_id=1, source_target_pairs={{0,16},{16,32},{32,48},{48,64},{64,80},{80,96},{96,112},{112,128},... | collective-permute-start | bytes 208904 | tf_op jit(solution)/shard_map/ppermute | solution.py:464
  43.6 5.9 %collective-permute-start.9 = (f32[8,384]{1,0:T(8,128)S(1)}, f32[8,384]{1,0:T(8,128)S(1)}, u32[]{:S(2)}, u32[]{:S(2)}) collective-permute-start(f32[8,384]{1,0:T(8,128)S(1)} %get-tuple-element.39.uv), channel_id=1, source_target_pairs={{16,0},{32,16},{48,32},{64,48},{80,64},{96,80},{112,96},{128,112},... | collective-permute-start | bytes 36872 | tf_op jit(solution)/shard_map/ppermute | solution.py:468
  44.9 5.4 %collective-permute-start.8 = (f32[8,384]{1,0:T(8,128)S(1)}, f32[8,384]{1,0:T(8,128)S(1)}, u32[]{:S(2)}, u32[]{:S(2)}) collective-permute-start(f32[8,384]{1,0:T(8,128)S(1)} %get-tuple-element.39.uv), channel_id=1, source_target_pairs={{0,16},{16,32},{32,48},{48,64},{64,80},{80,96},{96,112},{112,128},... | collective-permute-start | bytes 36872 | tf_op jit(solution)/shard_map/ppermute | solution.py:464
  53.1 6.1 %collective-permute-start.11 = (f32[34,8,128]{2,1,0:T(8,128)S(1)}, f32[34,8,128]{2,1,0:T(8,128)S(1)}, u32[]{:S(2)}, u32[]{:S(2)}) collective-permute-start(f32[34,8,128]{2,1,0:T(8,128)S(1)} %get-tuple-element.42), channel_id=1, source_target_pairs={{16,0},{32,16},{48,32},{64,48},{80,64},{96,80},{112,96},{128,112},... | collective-permute-start | bytes 417800 | tf_op jit(solution)/shard_map/ppermute | solution.py:468
  54.4 6.3 %collective-permute-start.10 = (f32[34,8,128]{2,1,0:T(8,128)S(1)}, f32[34,8,128]{2,1,0:T(8,128)S(1)}, u32[]{:S(2)}, u32[]{:S(2)}) collective-permute-start(f32[34,8,128]{2,1,0:T(8,128)S(1)} %get-tuple-element.42), channel_id=1, source_target_pairs={{0,16},{16,32},{32,48},{48,64},{64,80},{80,96},{96,112},{112,128},... | collective-permute-start | bytes 417800 | tf_op jit(solution)/shard_map/ppermute | solution.py:464
  60.6 57.2 %copy-start.3 = (f32[2,2,256]{2,1,0:T(2,128)S(1)}, f32[2,2,256]{2,1,0:T(2,128)}, u32[]{:S(2)}) copy-start(f32[2,2,256]{2,1,0:T(2,128)} %vel.3) | copy-start | bytes 12292
  60.6 57.2 %copy-start.6 = (s32[2,256]{1,0:T(2,128)S(1)}, s32[2,256]{1,0:T(2,128)}, u32[]{:S(2)}) copy-start(s32[2,256]{1,0:T(2,128)} %grounded.3) | copy-start | bytes 6148

commit v2 on v0

v2 whole, which is shorter than its diff:
```python
import jax
import jax.numpy as jnp
from jax import lax
from jax.experimental import pallas as pl
from jax.experimental.pallas import tpu as pltpu
from jax.sharding import PartitionSpec as P

PRIOR_WEIGHT = 0.05
EPSILON = 1e-06
OPPOSITE = (1, 0, 3, 2, 5, 4)
F32 = jnp.float32
LAYERS = 6
ROWS = 2
COLS = 256
CHUNK = 8
SLOTS = 16
OWN = 1
COUNT_ROW, PATTERN_ROW, RHS_ROW, BETA_ROW = 0, 1, 2, 4
SPARE = 6


def iota(shape, dim):
    return lax.broadcasted_iota(jnp.int32, shape, dim)


def swap_slots(tiles):
    slot = iota((8, 128), 1) // CHUNK
    tiles = list(tiles)
    for bit in (1, 2, 4, 8):
        odd = (slot & bit) != 0
        for i in range(SLOTS):
            if i & bit:
                continue
            low, high = tiles[i], tiles[i | bit]
            tiles[i] = jnp.where(odd, pltpu.roll(high, CHUNK * bit, 1), low)
            tiles[i | bit] = jnp.where(odd, high, pltpu.roll(low, 128 - CHUNK * bit, 1))
    return tiles


def pack_kernel(
    diag_in, inv_in, visc_in, count_in, grounded_in, pattern_in, beta_in, vel_in, message,
    diag, inv, visc, count, grounded, pattern, beta, vel, folded, arrived,
):
    pairs = (
        (count_in, count), (diag_in, diag), (inv_in, inv), (visc_in, visc), (grounded_in, grounded),
        (pattern_in, pattern), (beta_in, beta), (vel_in, vel),
    )
    copies = [
        pltpu.make_async_copy(source, target, arrived.at[i])
        for i, (source, target) in enumerate(pairs)
    ]
    for copy in copies:
        copy.start()
    folded[...] = jnp.zeros(folded.shape, F32)
    for copy in copies:
        copy.wait()
    layer = iota((LAYERS, COLS), 0)
    actives = [layer < count[r : r + 1, :] for r in range(ROWS)]

    def fold(cp, carry):
        eye = jnp.where(cp % 5 == 0, 1.0, 0.0).astype(F32)
        for t, table in enumerate((inv, diag)):
            for r in range(ROWS):
                values = jnp.where(actives[r], table[cp, :, r, :], eye)
                for part in range(2):
                    folded[(t * 2 + r) * 2 + part, cp, 0:LAYERS, :] = values[
                        :, part * 128 : part * 128 + 128
                    ]
        return carry

    lax.fori_loop(0, 16, fold, 0)
    for r in range(ROWS):
        row = slice(r, r + 1)
        viscous = jnp.where(actives[r], visc[:, r, :], 0.0)
        force = -(grounded[row, :].astype(F32) * beta[row, :])
        lines = [viscous[k : k + 1] for k in range(LAYERS)]
        lines += [count[row, :].astype(F32), pattern[row, :].astype(F32)]
        lines += [force * vel[0, row, :], force * vel[1, row, :], beta[row, :]]
        for slot, line in enumerate(lines):
            for part in range(2):
                folded[r * 2 + part, slot, SPARE : SPARE + 1, :] = line[
                    :, part * 128 : part * 128 + 128
                ]

    def send(i, carry):
        tiles = swap_slots([folded[i, cp] for cp in range(16)])
        for k in range(SLOTS):
            message[(i % 2) * SLOTS + k, i // 2] = tiles[k]
        return carry

    lax.fori_loop(0, 8, send, 0)


def block_times(table, base, values, transposed):
    out = []
    for c in range(4):
        total = None
        for k in range(4):
            entry = table[base + (k * 4 + c if transposed else c * 4 + k)] * values[k]
            total = entry if total is None else total + entry
        out.append(total)
    return out


def coupled(coupling, direction, values, transposed, sums):
    for c in range(4):
        for k in range(4):
            if transposed:
                factor = coupling[OPPOSITE[direction] * 16 + k * 4 + c]
            else:
                factor = coupling[direction * 16 + c * 4 + k]
            entry = factor * values[k]
            sums[c] = entry if sums[c] is None else sums[c] + entry
    return sums


def x_plus(v):
    first = iota((8, 128), 1) < CHUNK
    inner = pltpu.roll(jnp.where(first, v[2], v[0]), 128 - CHUNK, 1)
    outer = pltpu.roll(jnp.where(first, 0.0, v[2]), 128 - CHUNK, 1)
    return jnp.stack([v[1], inner, v[3], outer])


def x_minus(v):
    last = iota((8, 128), 1) >= 128 - CHUNK
    outer = pltpu.roll(jnp.where(last, 0.0, v[1]), CHUNK, 1)
    inner = pltpu.roll(jnp.where(last, v[1], v[3]), CHUNK, 1)
    return jnp.stack([outer, v[0], inner, v[2]])


def y_plus(v, after):
    column = iota((4, 8, 128), 2) % CHUNK
    return jnp.where(
        column < CHUNK - 1, pltpu.roll(v, 127, 2), pltpu.roll(after, CHUNK - 1, 2)
    )


def y_minus(v, before):
    column = iota((4, 8, 128), 2) % CHUNK
    return jnp.where(column > 0, pltpu.roll(v, 1, 2), pltpu.roll(before, 128 - CHUNK + 1, 2))


def stencil(field, base, coupling, transposed, kappa):
    here = [field[base + c] for c in range(4)]
    sums = [None] * 4
    sums = coupled(coupling, 0, [pltpu.roll(h, 7, 1) for h in here], transposed, sums)
    sums = coupled(coupling, 1, [pltpu.roll(h, 1, 1) for h in here], transposed, sums)

    def weighted(direction, tiles):
        if kappa is None:
            return tiles
        weight = kappa(direction)
        return [weight * t for t in tiles]

    moved = weighted(0, [x_plus(h) for h in here])
    sums = coupled(coupling, 2, moved, transposed, sums)
    moved = weighted(1, [x_minus(h) for h in here])
    sums = coupled(coupling, 3, moved, transposed, sums)
    moved = weighted(2, [y_plus(here[c], field[base + 4 + c]) for c in range(4)])
    sums = coupled(coupling, 4, moved, transposed, sums)
    moved = weighted(3, [y_minus(here[c], field[base - 4 + c]) for c in range(4)])
    return coupled(coupling, 5, moved, transposed, sums)


def sweep(vectors, res, first, carried, update, image, own_only, tables, transposed):
    inv, diag, vis, kappa, coupling = tables

    def initial(i, carry):
        v, j = i // 3, i % 3
        at = (v * 5 + j + 1) * 4
        nu = vis[j]
        values = [res[i * 4 + c] for c in range(4)]
        for c, y in enumerate(block_times(inv, j * 16, values, transposed)):
            first[i * 4 + c] = y
            carried[at + c] = nu * y
        return carry

    lax.fori_loop(0, vectors * 3, initial, 0)

    def correct(i, carry):
        v, j = i // 3, i % 3
        at = (v * 5 + j + 1) * 4
        nu = vis[j]
        sums = stencil(carried, at, coupling, transposed, lambda d: kappa[j * 4 + d])
        y0 = [first[i * 4 + c] for c in range(4)]
        own = block_times(diag, j * 16, y0, transposed)
        rest = [res[i * 4 + c] - own[c] + nu * sums[c] for c in range(4)]
        for c, y in enumerate(block_times(inv, j * 16, rest, transposed)):
            update[i * 4 + c] = y0[c] + y
        return carry

    lax.fori_loop(0, vectors * 3, correct, 0)

    def carry_on(i, carry):
        v, j = i // 3, i % 3
        nu = vis[j]
        for c in range(4):
            carried[(v * 5 + j + 1) * 4 + c] = nu * update[i * 4 + c]
        return carry

    lax.fori_loop(0, vectors * 3, carry_on, 0)

    def apply(i, carry):
        v, j = (i, OWN) if own_only else (i // 3, i % 3)
        sums = stencil(carried, (v * 5 + j + 1) * 4, coupling, transposed, None)
        values = [update[(v * 3 + j) * 4 + c] for c in range(4)]
        own = block_times(diag, j * 16, values, transposed)
        nu = vis[j]
        for c in range(4):
            image[i * 4 + c] = own[c] - nu * sums[c]
        return carry

    lax.fori_loop(0, vectors if own_only else vectors * 3, apply, 0)


def dots_of(residual, image, last, pairs, at):
    lane = iota((1, 128), 1)
    total = jnp.zeros((1, 128), F32)

    def own(ref, v):
        if ref is last:
            return [ref[v * 4 + c] for c in range(4)]
        return [ref[(v * 3 + OWN) * 4 + c] for c in range(4)]

    def dot(x, i, y, j):
        part = None
        for a, b in zip(own(x, i), own(y, j)):
            part = a * b if part is None else part + a * b
        return part

    for x, y in ((image, image), (residual, image), (residual, last), (image, last), (last, last)):
        for i, j in pairs:
            part = dot(x, i, y, j)
            if i != j:
                part += part if x is y else dot(x, j, y, i)
            tile = (part[0] + part[1]) + (part[2] + part[3])
            line = jnp.sum(tile, axis=0, keepdims=True)
            total += jnp.where(lane == at, jnp.sum(line, axis=1, keepdims=True), 0.0)
            at += 1
    return total


def layer_sums(update, spread, target, vector):
    for j in range(3):
        weight = spread[j]
        active = jnp.where(weight < 0.0, 1.0, 0.0)
        for c in range(2):
            total = jnp.sum(active * update[j * 4 + c], axis=1, keepdims=True)
            target[(vector * 3 + j) * 4 + c] = weight * total
        for c in range(2, 4):
            target[(vector * 3 + j) * 4 + c] = jnp.zeros((4, 8, 128), F32)


def unpack(block, j, inv, diag, vis, small):
    sub = iota((8, 128), 0)

    def place(i, carry):
        half, r = i // 2, i % 2
        tiles = swap_slots([block[half * SLOTS + s, r] for s in range(SLOTS)])
        for cp in range(16):
            inv[j * 16 + cp, i] = jnp.where(sub < LAYERS, tiles[cp], 0.0)
        for target, base, lines in ((vis, 0, LAYERS), (small, LAYERS, 5)):
            total = jnp.zeros((8, 128), F32)
            for k in range(lines):
                total = jnp.where(sub == k, pltpu.roll(tiles[base + k], (k - SPARE) % 8, 0), total)
            target[j, i] = total
        tiles = swap_slots([block[half * SLOTS + s, 2 + r] for s in range(SLOTS)])
        for cp in range(16):
            diag[j * 16 + cp, i] = tiles[cp]
        return carry

    lax.fori_loop(0, 4, place, 0)


def solve_kernel(
    coupling, low, mine, high, message,
    inv, diag, vis, small, kappa, spread, res, res_two, first, carried, update, image, last, start, lines,
):
    gx, gy = lax.axis_index("gx"), lax.axis_index("gy")
    nx, ny = lax.axis_size("gx"), lax.axis_size("gy")
    for j, block in enumerate((low, mine, high)):
        unpack(block, j, inv, diag, vis, small)
    for v in range(2):
        for c in range(4):
            carried[v * 20 + c] = jnp.zeros((4, 8, 128), F32)
            carried[v * 20 + 16 + c] = jnp.zeros((4, 8, 128), F32)

    shape = (4, 8, 128)
    layer = iota(shape, 1)
    lane = iota(shape, 2)
    source = (iota(shape, 0) // 2) * SLOTS + lane // CHUNK
    low_row = iota(shape, 0) % 2 == 0
    for j in range(3):
        tiles = small[j]
        counts = tiles[:, COUNT_ROW : COUNT_ROW + 1, :]
        whole = jnp.maximum(counts, 1.0)
        active = jnp.where(layer.astype(F32) < counts, 1.0, 0.0)
        spread[j] = -active / (whole * whole)
        for c in range(2):
            rhs = tiles[:, RHS_ROW + c : RHS_ROW + c + 1, :]
            res[j * 4 + c] = jnp.where(layer == 0, rhs, 0.0)
        for c in range(2, 4):
            res[j * 4 + c] = jnp.zeros(shape, F32)
        column = (gy * COLS + gx * CHUNK + (j - OWN) * CHUNK) + lane % CHUNK
        within = column & (COLS - 1)
        south_on = jnp.where((within == 0) & (column > 0), 1.0, 0.0)
        north_on = jnp.where((within == COLS - 1) & (column < ny * COLS - 1), 1.0, 0.0)
        south_in = jnp.where(within == 0, 0.0, 1.0)
        north_in = jnp.where(within == COLS - 1, 0.0, 1.0)
        side_exists = (low_row & (source > 0)) | (jnp.logical_not(low_row) & (source < nx - 1))
        side = jnp.where(side_exists, 1.0, 0.0)
        shared = south_on + north_on + side
        level = (1.0 + tiles[:, PATTERN_ROW : PATTERN_ROW + 1, :]) / 5.0
        own_weight = jnp.where(shared > 0.0, level, 1.0)
        near = (1.0 - own_weight) / jnp.maximum(shared, 1.0)
        inward = own_weight + near * (south_on + north_on)
        outward = own_weight + near * side
        kappa[j * 4] = jnp.where(low_row, inward, outward)
        kappa[j * 4 + 1] = jnp.where(low_row, outward, inward)
        kappa[j * 4 + 2] = own_weight + near * (north_on + side * north_in)
        kappa[j * 4 + 3] = own_weight + near * (south_on + side * south_in)

    tables = (inv, diag, vis, kappa, coupling)
    sweep(1, res, first, carried, update, image, False, tables, False)
    layer_sums(update, spread, res_two, 0)
    for t in range(12):
        res[t] = res[t] - image[t]
    sweep(1, res, first, carried, update, last, True, tables, False)
    layer_sums(update, spread, res_two, 1)
    lines[0:1, :] = dots_of(res, image, last, ((0, 0),), 0)

    sweep(2, res_two, first, carried, update, image, False, tables, True)
    for v in range(2):
        for c in range(4):
            start[v * 4 + c] = update[(v * 3 + OWN) * 4 + c]
    for t in range(24):
        res_two[t] = res_two[t] - image[t]
    sweep(2, res_two, first, carried, update, last, True, tables, True)
    dots = lines[0:1, :] + dots_of(res_two, image, last, ((0, 0), (0, 1), (1, 1)), 5)

    before, here, after = small[0], small[1], small[2]
    around = x_plus(here) + x_minus(here) + y_plus(here, after) + y_minus(here, before)
    first[0] = 4.0 * here - around
    sub = iota((8, 128), 0)

    def send(i, carry):
        half, r = i // 2, i % 2
        tiles = [start[k, i] for k in range(8)]
        tiles += [update[(v * 3 + OWN) * 4 + c, i] for v in range(2) for c in range(4)]
        prior = pltpu.roll(first[0, i], SPARE - BETA_ROW, 0)
        tiles[0] = jnp.where(sub == SPARE, prior, tiles[0])
        tiles = swap_slots(tiles)
        for s in range(SLOTS):
            message[half * SLOTS + s, r] = jnp.where(sub == 7, dots, tiles[s])
        return carry

    lax.fori_loop(0, 4, send, 0)


def steps(image2, residual_image, residual_last, image_last, last2):
    one = (residual_image + image2) / (image2 + EPSILON)
    off = 1.0 - one
    along = off * residual_image + one * residual_last + off * off * image2 + off * one * image_last
    squared = off * off * image2 + 2.0 * off * one * image_last + one * one * last2
    two = along / (squared + EPSILON)
    return one + two * off, one * two


def gather_kernel(block, lines):
    total = None
    for k in range(block.shape[0]):
        line = block[k, 0, 7:8, :]
        total = line if total is None else total + line
    lines[...] = jnp.broadcast_to(total, lines.shape)


def final_kernel(dots, block, grounded, vel, hessian, adjoint):
    line = jnp.sum(dots[...], axis=0, keepdims=True)
    lane = iota((1, 128), 1)

    def get(k):
        return jnp.sum(jnp.where(lane == k, line, 0.0), axis=1, keepdims=True)

    a, b = steps(*[get(k) for k in range(5)])
    kinds = []
    for k in range(5):
        at = 5 + 3 * k
        kinds.append(a * a * get(at) + a * b * get(at + 1) + b * b * get(at + 2))
    p, q = steps(*kinds)
    shape = (8, 128)
    vector = iota(shape, 1) // 32
    slot = iota(shape, 1) // CHUNK
    sub = iota(shape, 0)
    weights = jnp.where(
        vector == 0, p * a, jnp.where(vector == 1, p * b, jnp.where(vector == 2, q * a, q * b))
    )
    weights = jnp.where(sub < LAYERS, weights, jnp.where((sub == SPARE) & (slot == 0), 1.0, 0.0))
    for r in range(ROWS):
        heads = []
        for part in range(2):
            out = [None] * 4
            for k in range(SLOTS):
                tile = block[part * SLOTS + k, r] * weights
                tile = tile + pltpu.roll(tile, 64, 1)
                tile = tile + pltpu.roll(tile, 32, 1)
                for c in range(4):
                    turn = (CHUNK * (k - c)) % 32
                    moved = tile if turn == 0 else pltpu.roll(tile, turn, 1)
                    out[c] = moved if out[c] is None else jnp.where(slot == k, moved, out[c])
            at = slice(part * 128, part * 128 + 128)
            for c in range(4):
                adjoint[c, :, r, at] = out[c][0:LAYERS]
            row = slice(r, r + 1)
            data = grounded[row, at].astype(F32) * (
                vel[0, row, at] * out[0][0:1] + vel[1, row, at] * out[1][0:1]
            )
            hessian[row, at] = data + PRIOR_WEIGHT * out[0][SPARE : SPARE + 1]


VMEM = pl.BlockSpec(memory_space=pltpu.VMEM)
SMEM = pl.BlockSpec(memory_space=pltpu.SMEM)
HBM = pl.BlockSpec(memory_space=pltpu.HBM)


def call(kernel, name, operands, in_specs, outs, scratch=()):
    return pl.pallas_call(
        kernel,
        out_shape=[jax.ShapeDtypeStruct(shape, F32) for shape in outs],
        in_specs=in_specs,
        out_specs=[VMEM] * len(outs),
        scratch_shapes=scratch,
        compiler_params=pltpu.CompilerParams(vmem_limit_bytes=40 * 1024 * 1024),
        name=name,
    )(*operands)


def neighbour_pairs(step):
    n_gx, n_gy = lax.axis_size("gx"), lax.axis_size("gy")
    pairs = []
    for source in range(n_gx * n_gy):
        target = source + step
        if 0 <= target < n_gx * n_gy:
            pairs.append(
                tuple((i % n_gx) * n_gy + i // n_gx for i in (source, target))
            )
    return pairs


def per_device(
    diag_block,
    block_inverse,
    viscosity,
    coupling,
    active_layers,
    grounded,
    weight_pattern,
    beta_step,
    base_vel,
):
    n_gx, n_gy = lax.axis_size("gx"), lax.axis_size("gy")
    table = (16,) + viscosity.shape
    raw = [
        diag_block.reshape(table),
        block_inverse.reshape(table),
        viscosity,
        active_layers,
        grounded,
        weight_pattern,
        beta_step,
        base_vel,
    ]
    (sent,) = call(
        pack_kernel,
        "pack_tables",
        raw,
        [HBM] * 8,
        [(n_gx, 4, 8, 128)],
        [pltpu.VMEM(x.shape, x.dtype) for x in raw]
        + [pltpu.VMEM((8, 16, 8, 128), F32), pltpu.SemaphoreType.DMA((8,))],
    )
    mine = lax.all_to_all(sent, "gx", 0, 0, tiled=True)
    low = lax.ppermute(mine, ("gx", "gy"), neighbour_pairs(1))
    high = lax.ppermute(mine, ("gx", "gy"), neighbour_pairs(-1))

    def field(count):
        return pltpu.VMEM((count, 4, 8, 128), F32)

    (back,) = call(
        solve_kernel,
        "solve_both",
        [coupling.reshape(96), low, mine, high],
        [SMEM, VMEM, VMEM, VMEM],
        [(n_gx, 2, 8, 128)],
        [
            field(48),
            field(48),
            field(3),
            field(3),
            field(12),
            field(3),
            field(12),
            field(24),
            field(24),
            field(40),
            field(24),
            field(24),
            field(8),
            field(8),
            pltpu.VMEM((8, 128), F32),
        ],
    )
    block = lax.all_to_all(back, "gx", 0, 0, tiled=True)
    (lines,) = call(gather_kernel, "sum_gx", [block], [VMEM], [(n_gy, 128)])
    lines = lax.all_to_all(lines, "gy", 0, 0, tiled=True)
    hessian_vec, adjoint = call(
        final_kernel,
        "combine",
        [lines, block, grounded, base_vel],
        [VMEM] * 4,
        [beta_step.shape, (4,) + viscosity.shape],
    )
    return hessian_vec, adjoint


def solution(mesh):
    placed = (
        P(None, None, None, "gx", "gy"),
        P(None, None, None, "gx", "gy"),
        P(None, "gx", "gy"),
        P(),
        P("gx", "gy"),
        P("gx", "gy"),
        P("gx", "gy"),
        P("gx", "gy"),
        P(None, "gx", "gy"),
    )
    return jax.shard_map(
        per_device,
        mesh=mesh,
        in_specs=placed,
        out_specs=(P("gx", "gy"), P(None, None, "gx", "gy")),
        check_vma=False,
    )
```

time: 723 us -> 110 us (0.15); the launches traced: 711 us -> 109 us
  blocking collectives: 446 us -> 61.6 us
  starting transfers between devices: 171 us -> 6.8 us
  other arithmetic: 39.5 us -> 0 us
  Pallas kernels: 0 us -> 17.3 us
  local copies, waits for them, and re-layouts: 22.4 us -> 6.19 us
  between operations: 8.86 us -> 0.7 us
    psum x4 -> x0, blocking collectives: 446 us -> none  [solve(): lax.psum((jnp.sum(residual * image), jnp.sum(image * image)), ('gx', 'gy'))]
    ppermute x52 -> x2, starting transfers between devices: 171 us -> 6.8 us  [the longest x1 4.88 us: per_device(): high = lax.ppermute(mine, ('gx', 'gy'), neighbour_pairs(-1))]
    all_to_all x0 -> x3, blocking collectives: none -> 61.6 us  [the longest x1 26.6 us: per_device(): mine = lax.all_to_all(sent, 'gx', 0, 0, tiled=True)]
    reduce_sum x66 -> x0, other arithmetic: 17.9 us -> none  [the longest x45 10.7 us: small_apply(): jnp.sum(matrix.reshape(matrix.shape + (1,) * (values.ndim - 1)) * values[...]
    pallas_call x0 -> x4, Pallas kernels: none -> 17.3 us  [call(): pl.pallas_call(kernel, out_shape=[jax.ShapeDtypeStruct(shape, F32) for sh...]
    slice x80 -> x0, local copies, waits for them, and re-layouts: 8.03 us -> none  [the longest x26 2.45 us: padded(): lax.slice_in_dim(block, block.shape[dim] - width, None, axis=dim)]
    scatter x10 -> x0, local copies, waits for them, and re-layouts: 7.34 us -> none  [the longest x8 7.31 us: schwarz(): pack_y = jnp.zeros_like(own_part).at[:, :, :, 0].set(solved[:, :, 1:-1, 0...]
    ppermute x52 -> x2, waiting for transfers between devices: 23.9 us -> 16.8 us  [the longest x1 10.9 us: per_device(): low = lax.ppermute(mine, ('gx', 'gy'), neighbour_pairs(1))]
  transfers between devices with their start and end apart: 52 -> 2, of which waited for: 26 -> 2; matrix products, arithmetic and copies ran while one was open for 1% -> 0% of each run, Pallas kernels for 0% -> 0%
where the time goes in v2:
time: 110 us; the launch traced here: 109 us
  blocking collectives  61.6 us (56%)
  Pallas kernels  17.3 us (16%)
  waiting for transfers between devices  16.8 us (15%)
  starting transfers between devices  6.8 us (6%)
  local copies, waits for them, and re-layouts  6.19 us (6%)
    all_to_all x1, blocking collectives, per_device(): mine = lax.all_to_all(sent, 'gx', 0, 0, tiled=True)  26.6 us
    all_to_all x1, blocking collectives, per_device(): lines = lax.all_to_all(lines, 'gy', 0, 0, tiled=True)  21.7 us
    pallas_call x4, Pallas kernels, call(): pl.pallas_call(kernel, out_shape=[jax.ShapeDtypeStruct(shape, F32) for sh...  17.3 us
    all_to_all x1, blocking collectives, per_device(): block = lax.all_to_all(back, 'gx', 0, 0, tiled=True)  13.4 us
    ppermute x1, waiting for transfers between devices, per_device(): low = lax.ppermute(mine, ('gx', 'gy'), neighbour_pairs(1))  10.9 us
    unnamed x21, local copies, waits for them, and re-layouts  6.08 us
    ppermute x1, waiting for transfers between devices, per_device(): high = lax.ppermute(mine, ('gx', 'gy'), neighbour_pairs(-1))  5.87 us
    ppermute x1, starting transfers between devices, per_device(): high = lax.ppermute(mine, ('gx', 'gy'), neighbour_pairs(-1))  4.88 us
  transfers between devices with their start and end apart: 2, of which 2 were waited for; matrix products, arithmetic and copies ran while one was open for 0% of the time, Pallas kernels for 0%

profile of v2, /device:TPU:1, one launch (start us, length us, event | category | flops | bytes accessed | tf_op | source)
XLA Modules:
  0.0 109.4 jit_solution(5264543364693987789)
XLA Ops:
  0.6 0.0 copy-start.5
  0.6 0.7 copy-done.5
  1.3 0.0 copy-start
  1.3 0.9 copy-done
  2.2 0.0 copy-start.1
  2.2 0.9 copy-done.1
  3.2 0.0 copy-start.2
  3.2 0.7 copy-done.2
  3.9 0.0 copy-start.4
  3.9 0.7 copy-done.4
  4.6 0.0 copy-start.6
  4.6 0.7 copy-done.6
  5.2 0.0 copy-start.7
  5.2 0.7 copy-done.7
  5.9 0.0 copy-start.8
  5.9 0.7 copy-done.8
  6.6 3.3 %pack_tables.1 = f32[32,4,8,128]{3,2,1,0:T(8,128)S(1)} custom-call(f32[16,6,2,256]{3,2,1,0:T(2,128)S(1)} %bitcast.6, f32[16,6,2,256]{3,2,1,0:T(2,128)S(1)} %bitcast.7, f32[6,2,256]{2,1,0:T(2,128)S(1)} %copy-done.4, s32[2,256]{1,0:T(2,128)S(1)} %copy-done.6, s32[2,256]{1,0:T(2,128)S(1)} %copy-done.5, s32[2,256]{1,0:T(2,128)S(1)} %copy-done.7, ...), custom_call_target="tpu_custom_call" | custom-call | tf_op jit(solution)/shard_map/pack_tables/pallas_call | solution.py:426
  10.0 0.0 copy-start.9
  10.0 26.6 %all_to_all.21.mine = f32[32,4,8,128]{3,2,1,0:T(8,128)S(1)} all-to-all(f32[32,4,8,128]{3,2,1,0:T(8,128)S(1)} %pack_tables.1), channel_id=1, replica_groups=mesh['gx'=32,'gy'=16] {'gx'}, dimensions={0} | all-to-all | bytes 1048576 | tf_op jit(solution)/shard_map/all_to_all | solution.py:481
  36.5 4.9 %collective-permute-start.1 = (f32[32,4,8,128]{3,2,1,0:T(8,128)S(1)}, f32[32,4,8,128]{3,2,1,0:T(8,128)S(1)}, u32[]{:S(2)}, u32[]{:S(2)}) collective-permute-start(f32[32,4,8,128]{3,2,1,0:T(8,128)S(1)} %all_to_all.21.mine), channel_id=1, source_target_pairs={{16,0},{32,16},{48,32},{64,48},{80,64},{96,80},{112,96},{128,112},... | collective-permute-start | bytes 1572872 | tf_op jit(solution)/shard_map/ppermute | solution.py:483
  41.4 1.9 %collective-permute-start = (f32[32,4,8,128]{3,2,1,0:T(8,128)S(1)}, f32[32,4,8,128]{3,2,1,0:T(8,128)S(1)}, u32[]{:S(2)}, u32[]{:S(2)}) collective-permute-start(f32[32,4,8,128]{3,2,1,0:T(8,128)S(1)} %all_to_all.21.mine), channel_id=1, source_target_pairs={{0,16},{16,32},{32,48},{48,64},{64,80},{80,96},{96,112},{112,128},... | collective-permute-start | bytes 1572872 | tf_op jit(solution)/shard_map/ppermute | solution.py:482
  43.4 0.0 copy-done.9
  43.4 0.1 copy.13
  43.5 0.1 reshape.15.coupling
  43.6 5.9 %collective-permute-done.1.high = f32[32,4,8,128]{3,2,1,0:T(8,128)S(1)} collective-permute-done((f32[32,4,8,128]{3,2,1,0:T(8,128)S(1)}, f32[32,4,8,128]{3,2,1,0:T(8,128)S(1)}, u32[]{:S(2)}, u32[]{:S(2)}) %collective-permute-start.1) | collective-permute-done | bytes 524320 | tf_op jit(solution)/shard_map/ppermute | solution.py:483
  49.5 10.9 %collective-permute-done.low = f32[32,4,8,128]{3,2,1,0:T(8,128)S(1)} collective-permute-done((f32[32,4,8,128]{3,2,1,0:T(8,128)S(1)}, f32[32,4,8,128]{3,2,1,0:T(8,128)S(1)}, u32[]{:S(2)}, u32[]{:S(2)}) %collective-permute-start) | collective-permute-done | bytes 524320 | tf_op jit(solution)/shard_map/ppermute | solution.py:482
  60.4 12.6 %solve_both.1 = f32[32,2,8,128]{3,2,1,0:T(8,128)S(1)} custom-call(f32[96]{0:T(128)S(1)} %reshape.15.coupling, f32[32,4,8,128]{3,2,1,0:T(8,128)S(1)} %collective-permute-done.low, f32[32,4,8,128]{3,2,1,0:T(8,128)S(1)} %all_to_all.21.mine, f32[32,4,8,128]{3,2,1,0:T(8,128)S(1)} %collective-permute-done.1.high), custom_call_target="tpu_custom_call" | custom-call | tf_op jit(solution)/shard_map/solve_both/pallas_call | solution.py:426
  73.0 13.4 %all_to_all.22.block = f32[32,2,8,128]{3,2,1,0:T(8,128)S(1)} all-to-all(f32[32,2,8,128]{3,2,1,0:T(8,128)S(1)} %solve_both.1), channel_id=1, replica_groups=mesh['gx'=32,'gy'=16] {'gx'}, dimensions={0} | all-to-all | bytes 524288 | tf_op jit(solution)/shard_map/all_to_all | solution.py:512
  86.4 0.0 copy-start.3
  86.4 21.7 %all_to_all.23 = f32[16,1,128]{2,1,0:T(1,128)S(1)} all-to-all(f32[16,1,128]{2,1,0:T(1,128)S(1)} %bitcast.9), channel_id=1, replica_groups=mesh['gx'=32,'gy'=16] {'gy'}, dimensions={0} | all-to-all | bytes 16384 | tf_op jit(solution)/shard_map/all_to_all | solution.py:514
  108.1 0.0 copy-done.3
  108.1 1.3 %combine.1 = (f32[2,256]{1,0:T(2,128)}, f32[4,6,2,256]{3,2,1,0:T(2,128)}) custom-call(f32[16,128]{1,0:T(8,128)S(1)} %bitcast.8, f32[32,2,8,128]{3,2,1,0:T(8,128)S(1)} %all_to_all.22.block, s32[2,256]{1,0:T(2,128)S(1)} %copy-done.5, f32[2,2,256]{2,1,0:T(2,128)S(1)} %copy-done.3), custom_call_target="tpu_custom_call" | custom-call | tf_op jit(solution)/shard_map/combine/pallas_call | solution.py:426
  (1 shorter events, 0.0 us)
Async XLA Ops:
  0.6 0.7 copy-start.5
  1.3 0.9 copy-start
  2.2 0.9 copy-start.1
  3.2 0.7 copy-start.2
  3.9 0.7 copy-start.4
  4.6 0.7 copy-start.6
  5.2 0.7 copy-start.7
  5.9 0.7 copy-start.8
  10.0 33.4 %copy-start.9 = (f32[6,4,4]{0,2,1:T(4,128)S(1)}, f32[6,4,4]{0,2,1:T(4,128)}, u32[]{:S(2)}) copy-start(f32[6,4,4]{0,2,1:T(4,128)} %param.12) | copy-start | bytes 1156
  36.5 12.9 %collective-permute-start.1 = (f32[32,4,8,128]{3,2,1,0:T(8,128)S(1)}, f32[32,4,8,128]{3,2,1,0:T(8,128)S(1)}, u32[]{:S(2)}, u32[]{:S(2)}) collective-permute-start(f32[32,4,8,128]{3,2,1,0:T(8,128)S(1)} %all_to_all.21.mine), channel_id=1, source_target_pairs={{16,0},{32,16},{48,32},{64,48},{80,64},{96,80},{112,96},{128,112},... | collective-permute-start | bytes 1572872 | tf_op jit(solution)/shard_map/ppermute | solution.py:483
  41.4 19.0 %collective-permute-start = (f32[32,4,8,128]{3,2,1,0:T(8,128)S(1)}, f32[32,4,8,128]{3,2,1,0:T(8,128)S(1)}, u32[]{:S(2)}, u32[]{:S(2)}) collective-permute-start(f32[32,4,8,128]{3,2,1,0:T(8,128)S(1)} %all_to_all.21.mine), channel_id=1, source_target_pairs={{0,16},{16,32},{32,48},{48,64},{64,80},{80,96},{96,112},{112,128},... | collective-permute-start | bytes 1572872 | tf_op jit(solution)/shard_map/ppermute | solution.py:482
  86.4 21.7 %copy-start.3 = (f32[2,2,256]{2,1,0:T(2,128)S(1)}, f32[2,2,256]{2,1,0:T(2,128)}, u32[]{:S(2)}) copy-start(f32[2,2,256]{2,1,0:T(2,128)} %vel.1) | copy-start | bytes 12292

commit v3 on v2

--- a/solution.py
+++ b/solution.py
@@ -14,7 +14,7 @@
 COLS = 256
 CHUNK = 8
 SLOTS = 16
-OWN = 1
+OWN, NEAR = 1, 3
 COUNT_ROW, PATTERN_ROW, RHS_ROW, BETA_ROW = 0, 1, 2, 4
 SPARE = 6
 
@@ -23,18 +23,8 @@
     return lax.broadcasted_iota(jnp.int32, shape, dim)
 
 
-def swap_slots(tiles):
-    slot = iota((8, 128), 1) // CHUNK
-    tiles = list(tiles)
-    for bit in (1, 2, 4, 8):
-        odd = (slot & bit) != 0
-        for i in range(SLOTS):
-            if i & bit:
-                continue
-            low, high = tiles[i], tiles[i | bit]
-            tiles[i] = jnp.where(odd, pltpu.roll(high, CHUNK * bit, 1), low)
-            tiles[i | bit] = jnp.where(odd, high, pltpu.roll(low, 128 - CHUNK * bit, 1))
-    return tiles
+def turned(tiles):
+    return tiles.reshape(128, 128).T.reshape(SLOTS, 8, 128)
 
 
 def pack_kernel(
@@ -82,13 +72,9 @@
                     :, part * 128 : part * 128 + 128
                 ]
 
-    def send(i, carry):
-        tiles = swap_slots([folded[i, cp] for cp in range(16)])
-        for k in range(SLOTS):
-            message[(i % 2) * SLOTS + k, i // 2] = tiles[k]
-        return carry
-
-    lax.fori_loop(0, 8, send, 0)
+    for i in range(8):
+        part = slice((i % 2) * SLOTS, (i % 2) * SLOTS + SLOTS)
+        message[part, i // 2] = turned(folded[i])
 
 
 def block_times(table, base, values, transposed):
@@ -140,7 +126,7 @@
     return jnp.where(column > 0, pltpu.roll(v, 1, 2), pltpu.roll(before, 128 - CHUNK + 1, 2))
 
 
-def stencil(field, base, coupling, transposed, kappa):
+def stencil(field, base, after, before, coupling, transposed, kappa):
     here = [field[base + c] for c in range(4)]
     sums = [None] * 4
     sums = coupled(coupling, 0, [pltpu.roll(h, 7, 1) for h in here], transposed, sums)
@@ -156,18 +142,40 @@
     sums = coupled(coupling, 2, moved, transposed, sums)
     moved = weighted(1, [x_minus(h) for h in here])
     sums = coupled(coupling, 3, moved, transposed, sums)
-    moved = weighted(2, [y_plus(here[c], field[base + 4 + c]) for c in range(4)])
+    moved = weighted(2, [y_plus(here[c], field[after + c]) for c in range(4)])
     sums = coupled(coupling, 4, moved, transposed, sums)
-    moved = weighted(3, [y_minus(here[c], field[base - 4 + c]) for c in range(4)])
+    moved = weighted(3, [y_minus(here[c], field[before + c]) for c in range(4)])
     return coupled(coupling, 5, moved, transposed, sums)
 
 
-def sweep(vectors, res, first, carried, update, image, own_only, tables, transposed):
+class Forward:
+    count, transposed, own = 3, False, 1
+
+    def block(i):
+        return i
+
+    def place(i):
+        return (i + 1) * 4, (i + 2) * 4, i * 4
+
+
+class Adjoint:
+    count, transposed, own = 4, True, 2
+
+    def block(i):
+        return (i % 2) * 2 + 1
+
+    def place(i):
+        other = (i + 1 - 2 * (i % 2)) * 4
+        return i * 4, other, other
+
+
+def sweep(kind, res, first, carried, update, image, own_only, tables):
     inv, diag, vis, kappa, coupling = tables
+    transposed = kind.transposed
 
     def initial(i, carry):
-        v, j = i // 3, i % 3
-        at = (v * 5 + j + 1) * 4
+        j = kind.block(i)
+        at = kind.place(i)[0]
         nu = vis[j]
         values = [res[i * 4 + c] for c in range(4)]
         for c, y in enumerate(block_times(inv, j * 16, values, transposed)):
@@ -175,13 +183,14 @@
             carried[at + c] = nu * y
         return carry
 
-    lax.fori_loop(0, vectors * 3, initial, 0)
+    lax.fori_loop(0, kind.count, initial, 0)
 
     def correct(i, carry):
-        v, j = i // 3, i % 3
-        at = (v * 5 + j + 1) * 4
+        j = kind.block(i)
         nu = vis[j]
-        sums = stencil(carried, at, coupling, transposed, lambda d: kappa[j * 4 + d])
+        sums = stencil(
+            carried, *kind.place(i), coupling, transposed, lambda d: kappa[j * 4 + d]
+        )
         y0 = [first[i * 4 + c] for c in range(4)]
         own = block_times(diag, j * 16, y0, transposed)
         rest = [res[i * 4 + c] - own[c] + nu * sums[c] for c in range(4)]
@@ -189,38 +198,35 @@
             update[i * 4 + c] = y0[c] + y
         return carry
 
-    lax.fori_loop(0, vectors * 3, correct, 0)
+    lax.fori_loop(0, kind.count, correct, 0)
 
     def carry_on(i, carry):
-        v, j = i // 3, i % 3
-        nu = vis[j]
+        nu = vis[kind.block(i)]
+        at = kind.place(i)[0]
         for c in range(4):
-            carried[(v * 5 + j + 1) * 4 + c] = nu * update[i * 4 + c]
-        return carry
-
-    lax.fori_loop(0, vectors * 3, carry_on, 0)
+            carried[at + c] = nu * update[i * 4 + c]
+        return carry
+
+    lax.fori_loop(0, kind.count, carry_on, 0)
 
     def apply(i, carry):
-        v, j = (i, OWN) if own_only else (i // 3, i % 3)
-        sums = stencil(carried, (v * 5 + j + 1) * 4, coupling, transposed, None)
-        values = [update[(v * 3 + j) * 4 + c] for c in range(4)]
+        if own_only:
+            i = i * 2 if kind is Adjoint else 1
+        j = kind.block(i)
+        sums = stencil(carried, *kind.place(i), coupling, transposed, None)
+        values = [update[i * 4 + c] for c in range(4)]
         own = block_times(diag, j * 16, values, transposed)
         nu = vis[j]
         for c in range(4):
             image[i * 4 + c] = own[c] - nu * sums[c]
         return carry
 
-    lax.fori_loop(0, vectors if own_only else vectors * 3, apply, 0)
-
-
-def dots_of(residual, image, last, pairs, at):
-    lane = iota((1, 128), 1)
-    total = jnp.zeros((1, 128), F32)
-
+    lax.fori_loop(0, kind.own if own_only else kind.count, apply, 0)
+
+
+def dots_of(residual, image, last, at_of, pairs):
     def own(ref, v):
-        if ref is last:
-            return [ref[v * 4 + c] for c in range(4)]
-        return [ref[(v * 3 + OWN) * 4 + c] for c in range(4)]
+        return [ref[at_of(v) + c] for c in range(4)]
 
     def dot(x, i, y, j):
         part = None
@@ -228,6 +234,7 @@
             part = a * b if part is None else part + a * b
         return part
 
+    out = []
     for x, y in ((image, image), (residual, image), (residual, last), (image, last), (last, last)):
         for i, j in pairs:
             part = dot(x, i, y, j)
@@ -235,55 +242,58 @@
                 part += part if x is y else dot(x, j, y, i)
             tile = (part[0] + part[1]) + (part[2] + part[3])
             line = jnp.sum(tile, axis=0, keepdims=True)
-            total += jnp.where(lane == at, jnp.sum(line, axis=1, keepdims=True), 0.0)
-            at += 1
-    return total
+            out.append(jnp.sum(line, axis=1, keepdims=True))
+    return out
+
+
+def merged(after, before):
+    return jnp.where(iota((4, 8, 128), 2) % CHUNK < CHUNK // 2, after, before)
 
 
 def layer_sums(update, spread, target, vector):
-    for j in range(3):
+    for i, j in enumerate((OWN, NEAR)):
         weight = spread[j]
         active = jnp.where(weight < 0.0, 1.0, 0.0)
+        at = (vector * 2 + i) * 4
         for c in range(2):
-            total = jnp.sum(active * update[j * 4 + c], axis=1, keepdims=True)
-            target[(vector * 3 + j) * 4 + c] = weight * total
+            tile = update[4 + c] if j == OWN else merged(update[8 + c], update[c])
+            target[at + c] = weight * jnp.sum(active * tile, axis=1, keepdims=True)
         for c in range(2, 4):
-            target[(vector * 3 + j) * 4 + c] = jnp.zeros((4, 8, 128), F32)
+            target[at + c] = jnp.zeros((4, 8, 128), F32)
 
 
 def unpack(block, j, inv, diag, vis, small):
     sub = iota((8, 128), 0)
 
-    def place(i, carry):
-        half, r = i // 2, i % 2
-        tiles = swap_slots([block[half * SLOTS + s, r] for s in range(SLOTS)])
-        for cp in range(16):
-            inv[j * 16 + cp, i] = jnp.where(sub < LAYERS, tiles[cp], 0.0)
-        for target, base, lines in ((vis, 0, LAYERS), (small, LAYERS, 5)):
-            total = jnp.zeros((8, 128), F32)
-            for k in range(lines):
-                total = jnp.where(sub == k, pltpu.roll(tiles[base + k], (k - SPARE) % 8, 0), total)
-            target[j, i] = total
-        tiles = swap_slots([block[half * SLOTS + s, 2 + r] for s in range(SLOTS)])
-        for cp in range(16):
-            diag[j * 16 + cp, i] = tiles[cp]
-        return carry
-
-    lax.fori_loop(0, 4, place, 0)
+    def place(half, carry):
+        part = pl.ds(half * SLOTS, SLOTS)
+        for r in range(ROWS):
+            i = half * 2 + r
+            tiles = turned(block[part, r])
+            inv[j * 16 : j * 16 + 16, i] = jnp.where(sub[None] < LAYERS, tiles, 0.0)
+            for target, base, lines in ((vis, 0, LAYERS), (small, LAYERS, 5)):
+                total = jnp.zeros((8, 128), F32)
+                for k in range(lines):
+                    moved = pltpu.roll(tiles[base + k], (k - SPARE) % 8, 0)
+                    total = jnp.where(sub == k, moved, total)
+                target[j, i] = total
+            diag[j * 16 : j * 16 + 16, i] = turned(block[part, 2 + r])
+        return carry
+
+    lax.fori_loop(0, 2, place, 0)
 
 
 def solve_kernel(
     coupling, low, mine, high, message,
-    inv, diag, vis, small, kappa, spread, res, res_two, first, carried, update, image, last, start, lines,
+    inv, diag, vis, small, kappa, spread, res, res_two, first, carried, update, image, last, start,
 ):
     gx, gy = lax.axis_index("gx"), lax.axis_index("gy")
     nx, ny = lax.axis_size("gx"), lax.axis_size("gy")
     for j, block in enumerate((low, mine, high)):
         unpack(block, j, inv, diag, vis, small)
-    for v in range(2):
-        for c in range(4):
-            carried[v * 20 + c] = jnp.zeros((4, 8, 128), F32)
-            carried[v * 20 + 16 + c] = jnp.zeros((4, 8, 128), F32)
+    for c in range(4):
+        carried[c] = jnp.zeros((4, 8, 128), F32)
+        carried[16 + c] = jnp.zeros((4, 8, 128), F32)
 
     shape = (4, 8, 128)
     layer = iota(shape, 1)
@@ -320,41 +330,53 @@
         kappa[j * 4 + 2] = own_weight + near * (north_on + side * north_in)
         kappa[j * 4 + 3] = own_weight + near * (south_on + side * south_in)
 
+    for table, size in ((inv, 16), (diag, 16), (kappa, 4), (vis, 1), (spread, 1)):
+        for k in range(size):
+            table[NEAR * size + k] = merged(table[2 * size + k], table[k])
+
     tables = (inv, diag, vis, kappa, coupling)
-    sweep(1, res, first, carried, update, image, False, tables, False)
+    sweep(Forward, res, first, carried, update, image, False, tables)
     layer_sums(update, spread, res_two, 0)
     for t in range(12):
         res[t] = res[t] - image[t]
-    sweep(1, res, first, carried, update, last, True, tables, False)
+    sweep(Forward, res, first, carried, update, last, True, tables)
     layer_sums(update, spread, res_two, 1)
-    lines[0:1, :] = dots_of(res, image, last, ((0, 0),), 0)
-
-    sweep(2, res_two, first, carried, update, image, False, tables, True)
+    dots = dots_of(res, image, last, lambda v: 4, ((0, 0),))
+
+    sweep(Adjoint, res_two, first, carried, update, image, False, tables)
     for v in range(2):
         for c in range(4):
-            start[v * 4 + c] = update[(v * 3 + OWN) * 4 + c]
-    for t in range(24):
+            start[v * 4 + c] = update[v * 8 + c]
+    for t in range(16):
         res_two[t] = res_two[t] - image[t]
-    sweep(2, res_two, first, carried, update, last, True, tables, True)
-    dots = lines[0:1, :] + dots_of(res_two, image, last, ((0, 0), (0, 1), (1, 1)), 5)
+    sweep(Adjoint, res_two, first, carried, update, last, True, tables)
+    dots += dots_of(res_two, image, last, lambda v: v * 8, ((0, 0), (0, 1), (1, 1)))
 
     before, here, after = small[0], small[1], small[2]
     around = x_plus(here) + x_minus(here) + y_plus(here, after) + y_minus(here, before)
     first[0] = 4.0 * here - around
     sub = iota((8, 128), 0)
-
-    def send(i, carry):
-        half, r = i // 2, i % 2
-        tiles = [start[k, i] for k in range(8)]
-        tiles += [update[(v * 3 + OWN) * 4 + c, i] for v in range(2) for c in range(4)]
-        prior = pltpu.roll(first[0, i], SPARE - BETA_ROW, 0)
-        tiles[0] = jnp.where(sub == SPARE, prior, tiles[0])
-        tiles = swap_slots(tiles)
-        for s in range(SLOTS):
-            message[half * SLOTS + s, r] = jnp.where(sub == 7, dots, tiles[s])
-        return carry
-
-    lax.fori_loop(0, 4, send, 0)
+    column = iota((1, 128), 1) % CHUNK
+    lines = []
+    for k in range(0, len(dots), CHUNK):
+        line = jnp.zeros((1, 128), F32)
+        for m, dot in enumerate(dots[k : k + CHUNK]):
+            line = jnp.where(column == m, dot, line)
+        lines.append(line)
+
+    def send(half, carry):
+        for r in range(ROWS):
+            i = half * 2 + r
+            tiles = [start[k, i] for k in range(8)]
+            tiles += [update[v * 8 + c, i] for v in range(2) for c in range(4)]
+            prior = pltpu.roll(first[0, i], SPARE - BETA_ROW, 0)
+            tiles[0] = jnp.where(sub == SPARE, prior, tiles[0])
+            for k, line in enumerate(lines):
+                tiles[k] = jnp.where(sub == 7, line, tiles[k])
+            message[pl.ds(half * SLOTS, SLOTS), r] = turned(jnp.stack(tiles))
+        return carry
+
+    lax.fori_loop(0, 2, send, 0)
 
 
 def steps(image2, residual_image, residual_last, image_last, last2):
@@ -369,9 +391,13 @@
 def gather_kernel(block, lines):
     total = None
     for k in range(block.shape[0]):
-        line = block[k, 0, 7:8, :]
-        total = line if total is None else total + line
-    lines[...] = jnp.broadcast_to(total, lines.shape)
+        total = block[k, 0] if total is None else total + block[k, 0]
+    lane, sub = iota((8, 128), 1), iota((8, 128), 0)
+    out = jnp.zeros((8, 128), F32)
+    for i in range(8):
+        keep = (sub == i) & (lane % CHUNK == 7)
+        out += pltpu.roll(jnp.where(keep, total, 0.0), (i - 7) % 128, 1)
+    lines[...] = jnp.broadcast_to(jnp.sum(out, axis=0, keepdims=True), lines.shape)
 
 
 def final_kernel(dots, block, grounded, vel, hessian, adjoint):
@@ -387,34 +413,23 @@
         at = 5 + 3 * k
         kinds.append(a * a * get(at) + a * b * get(at + 1) + b * b * get(at + 2))
     p, q = steps(*kinds)
-    shape = (8, 128)
-    vector = iota(shape, 1) // 32
-    slot = iota(shape, 1) // CHUNK
-    sub = iota(shape, 0)
-    weights = jnp.where(
-        vector == 0, p * a, jnp.where(vector == 1, p * b, jnp.where(vector == 2, q * a, q * b))
-    )
-    weights = jnp.where(sub < LAYERS, weights, jnp.where((sub == SPARE) & (slot == 0), 1.0, 0.0))
+    weights = (p * a, p * b, q * a, q * b)
     for r in range(ROWS):
-        heads = []
         for part in range(2):
-            out = [None] * 4
-            for k in range(SLOTS):
-                tile = block[part * SLOTS + k, r] * weights
-                tile = tile + pltpu.roll(tile, 64, 1)
-                tile = tile + pltpu.roll(tile, 32, 1)
-                for c in range(4):
-                    turn = (CHUNK * (k - c)) % 32
-                    moved = tile if turn == 0 else pltpu.roll(tile, turn, 1)
-                    out[c] = moved if out[c] is None else jnp.where(slot == k, moved, out[c])
+            tiles = turned(block[part * SLOTS : part * SLOTS + SLOTS, r])
             at = slice(part * 128, part * 128 + 128)
+            heads = []
             for c in range(4):
-                adjoint[c, :, r, at] = out[c][0:LAYERS]
+                total = weights[0] * tiles[c]
+                for v in range(1, 4):
+                    total += weights[v] * tiles[v * 4 + c]
+                adjoint[c, :, r, at] = total[0:LAYERS]
+                heads.append(total[0:1])
             row = slice(r, r + 1)
             data = grounded[row, at].astype(F32) * (
-                vel[0, row, at] * out[0][0:1] + vel[1, row, at] * out[1][0:1]
+                vel[0, row, at] * heads[0] + vel[1, row, at] * heads[1]
             )
-            hessian[row, at] = data + PRIOR_WEIGHT * out[0][SPARE : SPARE + 1]
+            hessian[row, at] = data + PRIOR_WEIGHT * tiles[0, SPARE : SPARE + 1]
 
 
 VMEM = pl.BlockSpec(memory_space=pltpu.VMEM)
@@ -429,7 +444,7 @@
         in_specs=in_specs,
         out_specs=[VMEM] * len(outs),
         scratch_shapes=scratch,
-        compiler_params=pltpu.CompilerParams(vmem_limit_bytes=40 * 1024 * 1024),
+        compiler_params=pltpu.CompilerParams(vmem_limit_bytes=(63 if name == "pack_tables" else 40) * 1024 * 1024),
         name=name,
     )(*operands)
 
@@ -492,21 +507,20 @@
         [SMEM, VMEM, VMEM, VMEM],
         [(n_gx, 2, 8, 128)],
         [
-            field(48),
-            field(48),
+            field(64),
+            field(64),
+            field(4),
             field(3),
-            field(3),
+            field(16),
+            field(4),
             field(12),
-            field(3),
-            field(12),
-            field(24),
-            field(24),
-            field(40),
-            field(24),
-            field(24),
+            field(16),
+            field(16),
+            field(20),
+            field(16),
+            field(16),
+            field(16),
             field(8),
-            field(8),
-            pltpu.VMEM((8, 128), F32),
         ],
     )
     block = lax.all_to_all(back, "gx", 0, 0, tiled=True)

time: 110 us -> 96.9 us (0.88)
  Pallas kernels: 17.3 us -> 10.2 us
  local copies, waits for them, and re-layouts: 6.19 us -> 0.23 us
    pallas_call x4, Pallas kernels: 17.3 us -> 10.2 us  [call(): pl.pallas_call(kernel, out_shape=[jax.ShapeDtypeStruct(shape, F32) for sh...]
    unnamed x21 -> x7, local copies, waits for them, and re-layouts: 6.08 us -> 0.12 us
where the time goes in v3:
time: 96.9 us; the launch traced here: 96.5 us
  blocking collectives  61.8 us (64%)
  waiting for transfers between devices  16.8 us (17%)
  Pallas kernels  10.2 us (11%)
  starting transfers between devices  6.8 us (7%)
    all_to_all x1, blocking collectives, per_device(): mine = lax.all_to_all(sent, 'gx', 0, 0, tiled=True)  26.8 us
    all_to_all x1, blocking collectives, per_device(): lines = lax.all_to_all(lines, 'gy', 0, 0, tiled=True)  21.7 us
    all_to_all x1, blocking collectives, per_device(): block = lax.all_to_all(back, 'gx', 0, 0, tiled=True)  13.4 us
    ppermute x1, waiting for transfers between devices, per_device(): low = lax.ppermute(mine, ('gx', 'gy'), neighbour_pairs(1))  10.9 us
    pallas_call x4, Pallas kernels, call(): pl.pallas_call(kernel, out_shape=[jax.ShapeDtypeStruct(shape, F32) for sh...  10.2 us
    ppermute x1, waiting for transfers between devices, per_device(): high = lax.ppermute(mine, ('gx', 'gy'), neighbour_pairs(-1))  5.87 us
    ppermute x1, starting transfers between devices, per_device(): high = lax.ppermute(mine, ('gx', 'gy'), neighbour_pairs(-1))  4.88 us
  transfers between devices with their start and end apart: 2, of which 2 were waited for; matrix products, arithmetic and copies ran while one was open for 0% of the time, Pallas kernels for 0%

profile of v3, /device:TPU:1, one launch (start us, length us, event | category | flops | bytes accessed | tf_op | source)
XLA Modules:
  0.0 96.5 jit_solution(12158539776879798066)
XLA Ops:
  0.6 2.4 %pack_tables.1 = f32[32,4,8,128]{3,2,1,0:T(8,128)} custom-call(f32[16,6,2,256]{3,2,1,0:T(2,128)} %bitcast.8, f32[16,6,2,256]{3,2,1,0:T(2,128)} %bitcast.9, f32[6,2,256]{2,1,0:T(2,128)} %visc_in.1, s32[2,256]{1,0:T(2,128)} %count_in.1, s32[2,256]{1,0:T(2,128)} %grounded.1, s32[2,256]{1,0:T(2,128)} %pattern_in.1, f32[2,256]{1,0:T(2,128)} %beta_in.1, ...), custom_call_target="tpu_custom_call" | custom-call | tf_op jit(solution)/shard_map/pack_tables/pallas_call | solution.py:441
  3.0 0.0 copy-start.2
  3.0 26.8 %all_to_all.21.mine = f32[32,4,8,128]{3,2,1,0:T(8,128)S(1)} all-to-all(f32[32,4,8,128]{3,2,1,0:T(8,128)} %pack_tables.1), channel_id=1, replica_groups=mesh['gx'=32,'gy'=16] {'gx'}, dimensions={0} | all-to-all | bytes 1048576 | tf_op jit(solution)/shard_map/all_to_all | solution.py:496
  29.8 4.9 %collective-permute-start.1 = (f32[32,4,8,128]{3,2,1,0:T(8,128)S(1)}, f32[32,4,8,128]{3,2,1,0:T(8,128)S(1)}, u32[]{:S(2)}, u32[]{:S(2)}) collective-permute-start(f32[32,4,8,128]{3,2,1,0:T(8,128)S(1)} %all_to_all.21.mine), channel_id=1, source_target_pairs={{16,0},{32,16},{48,32},{64,48},{80,64},{96,80},{112,96},{128,112},... | collective-permute-start | bytes 1572872 | tf_op jit(solution)/shard_map/ppermute | solution.py:498
  34.7 1.9 %collective-permute-start = (f32[32,4,8,128]{3,2,1,0:T(8,128)S(1)}, f32[32,4,8,128]{3,2,1,0:T(8,128)S(1)}, u32[]{:S(2)}, u32[]{:S(2)}) collective-permute-start(f32[32,4,8,128]{3,2,1,0:T(8,128)S(1)} %all_to_all.21.mine), channel_id=1, source_target_pairs={{0,16},{16,32},{32,48},{48,64},{64,80},{80,96},{96,112},{112,128},... | collective-permute-start | bytes 1572872 | tf_op jit(solution)/shard_map/ppermute | solution.py:497
  36.6 0.0 copy-done.2
  36.6 0.1 copy.13
  36.8 0.1 reshape.15.coupling
  36.9 5.9 %collective-permute-done.1.high = f32[32,4,8,128]{3,2,1,0:T(8,128)S(1)} collective-permute-done((f32[32,4,8,128]{3,2,1,0:T(8,128)S(1)}, f32[32,4,8,128]{3,2,1,0:T(8,128)S(1)}, u32[]{:S(2)}, u32[]{:S(2)}) %collective-permute-start.1) | collective-permute-done | bytes 524320 | tf_op jit(solution)/shard_map/ppermute | solution.py:498
  42.7 10.9 %collective-permute-done.low = f32[32,4,8,128]{3,2,1,0:T(8,128)S(1)} collective-permute-done((f32[32,4,8,128]{3,2,1,0:T(8,128)S(1)}, f32[32,4,8,128]{3,2,1,0:T(8,128)S(1)}, u32[]{:S(2)}, u32[]{:S(2)}) %collective-permute-start) | collective-permute-done | bytes 524320 | tf_op jit(solution)/shard_map/ppermute | solution.py:497
  53.7 6.8 %solve_both.1 = f32[32,2,8,128]{3,2,1,0:T(8,128)S(1)} custom-call(f32[96]{0:T(128)S(1)} %reshape.15.coupling, f32[32,4,8,128]{3,2,1,0:T(8,128)S(1)} %collective-permute-done.low, f32[32,4,8,128]{3,2,1,0:T(8,128)S(1)} %all_to_all.21.mine, f32[32,4,8,128]{3,2,1,0:T(8,128)S(1)} %collective-permute-done.1.high), custom_call_target="tpu_custom_call" | custom-call | tf_op jit(solution)/shard_map/solve_both/pallas_call | solution.py:441
  60.5 13.4 %all_to_all.22.block = f32[32,2,8,128]{3,2,1,0:T(8,128)S(1)} all-to-all(f32[32,2,8,128]{3,2,1,0:T(8,128)S(1)} %solve_both.1), channel_id=1, replica_groups=mesh['gx'=32,'gy'=16] {'gx'}, dimensions={0} | all-to-all | bytes 524288 | tf_op jit(solution)/shard_map/all_to_all | solution.py:526
  73.9 0.0 copy-start
  73.9 0.0 copy-start.1
  73.9 0.1 sum_gx.1
  74.0 21.7 %all_to_all.23 = f32[16,1,128]{2,1,0:T(1,128)S(1)} all-to-all(f32[16,1,128]{2,1,0:T(1,128)S(1)} %bitcast.7), channel_id=1, replica_groups=mesh['gx'=32,'gy'=16] {'gy'}, dimensions={0} | all-to-all | bytes 16384 | tf_op jit(solution)/shard_map/all_to_all | solution.py:528
  95.7 0.0 copy-done
  95.7 0.0 copy-done.1
  95.7 0.8 combine.1
Async XLA Ops:
  3.0 33.6 %copy-start.2 = (f32[6,4,4]{0,2,1:T(4,128)S(1)}, f32[6,4,4]{0,2,1:T(4,128)}, u32[]{:S(2)}) copy-start(f32[6,4,4]{0,2,1:T(4,128)} %param.12) | copy-start | bytes 1156
  29.8 12.9 %collective-permute-start.1 = (f32[32,4,8,128]{3,2,1,0:T(8,128)S(1)}, f32[32,4,8,128]{3,2,1,0:T(8,128)S(1)}, u32[]{:S(2)}, u32[]{:S(2)}) collective-permute-start(f32[32,4,8,128]{3,2,1,0:T(8,128)S(1)} %all_to_all.21.mine), channel_id=1, source_target_pairs={{16,0},{32,16},{48,32},{64,48},{80,64},{96,80},{112,96},{128,112},... | collective-permute-start | bytes 1572872 | tf_op jit(solution)/shard_map/ppermute | solution.py:498
  34.7 19.0 %collective-permute-start = (f32[32,4,8,128]{3,2,1,0:T(8,128)S(1)}, f32[32,4,8,128]{3,2,1,0:T(8,128)S(1)}, u32[]{:S(2)}, u32[]{:S(2)}) collective-permute-start(f32[32,4,8,128]{3,2,1,0:T(8,128)S(1)} %all_to_all.21.mine), channel_id=1, source_target_pairs={{0,16},{16,32},{32,48},{48,64},{64,80},{80,96},{96,112},{112,128},... | collective-permute-start | bytes 1572872 | tf_op jit(solution)/shard_map/ppermute | solution.py:497
  73.9 21.8 %copy-start = (f32[2,2,256]{2,1,0:T(2,128)S(1)}, f32[2,2,256]{2,1,0:T(2,128)}, u32[]{:S(2)}) copy-start(f32[2,2,256]{2,1,0:T(2,128)} %vel.1) | copy-start | bytes 12292
  73.9 21.8 %copy-start.1 = (s32[2,256]{1,0:T(2,128)S(1)}, s32[2,256]{1,0:T(2,128)}, u32[]{:S(2)}) copy-start(s32[2,256]{1,0:T(2,128)} %grounded.1) | copy-start | bytes 6148

commit v4 on v3

--- a/solution.py
+++ b/solution.py
@@ -21,6 +21,48 @@
 
 def iota(shape, dim):
     return lax.broadcasted_iota(jnp.int32, shape, dim)
+
+
+def chunk_order(turn, n_x, n_y):
+    order = []
+    if turn % 2 == 0:
+        for i in range(n_y):
+            for j in range(n_x):
+                x, y = (j if i % 2 == 0 else n_x - 1 - j), i
+                if turn == 2:
+                    x, y = n_x - 1 - x, n_y - 1 - y
+                order.append(y * n_x + x)
+    else:
+        for i in range(n_x):
+            for j in range(n_y):
+                x, y = i, (n_y - 1 - j if i % 2 == 0 else j)
+                if turn == 3:
+                    x, y = n_x - 1 - x, n_y - 1 - y
+                order.append(y * n_x + x)
+    return order
+
+
+GRID_X, GRID_Y = 4, 8
+ORDERS = [chunk_order(turn, GRID_X, GRID_Y) for turn in range(4)]
+
+
+def pick(turn, choices):
+    low = jnp.where(turn == 0, choices[0], choices[1])
+    return jnp.where(turn < 2, low, jnp.where(turn == 2, choices[2], choices[3]))
+
+
+def device_of(turn, chunk):
+    return pick(turn, [order[chunk] for order in ORDERS])
+
+
+def chunk_of(turn, gx):
+    x, y = gx % GRID_X, gx // GRID_X
+    back_x, back_y = GRID_X - 1 - x, GRID_Y - 1 - y
+    along_x = jnp.where(turn == 0, y, back_y)
+    step_x = jnp.where((along_x % 2 == 0) == (turn == 0), x, back_x)
+    along_y = jnp.where(turn == 1, x, back_x)
+    step_y = jnp.where((along_y % 2 == 0) == (turn == 1), back_y, y)
+    return jnp.where(turn % 2 == 0, along_x * GRID_X + step_x, along_y * GRID_Y + step_y)
 
 
 def turned(tiles):
@@ -72,9 +114,13 @@
                     :, part * 128 : part * 128 + 128
                 ]
 
-    for i in range(8):
-        part = slice((i % 2) * SLOTS, (i % 2) * SLOTS + SLOTS)
-        message[part, i // 2] = turned(folded[i])
+    turn = lax.axis_index("gy") % 4
+    for part in range(2):
+        targets = [device_of(turn, part * SLOTS + k) for k in range(SLOTS)]
+        for i in range(4):
+            tiles = turned(folded[i * 2 + part])
+            for k in range(SLOTS):
+                message[targets[k], i] = tiles[k]
 
 
 def block_times(table, base, values, transposed):
@@ -289,6 +335,7 @@
 ):
     gx, gy = lax.axis_index("gx"), lax.axis_index("gy")
     nx, ny = lax.axis_size("gx"), lax.axis_size("gy")
+    chunk = chunk_of(gy % 4, gx)
     for j, block in enumerate((low, mine, high)):
         unpack(block, j, inv, diag, vis, small)
     for c in range(4):
@@ -311,7 +358,7 @@
             res[j * 4 + c] = jnp.where(layer == 0, rhs, 0.0)
         for c in range(2, 4):
             res[j * 4 + c] = jnp.zeros(shape, F32)
-        column = (gy * COLS + gx * CHUNK + (j - OWN) * CHUNK) + lane % CHUNK
+        column = (gy * COLS + (chunk + j - OWN) * CHUNK) + lane % CHUNK
         within = column & (COLS - 1)
         south_on = jnp.where((within == 0) & (column > 0), 1.0, 0.0)
         north_on = jnp.where((within == COLS - 1) & (column < ny * COLS - 1), 1.0, 0.0)
@@ -414,9 +461,11 @@
         kinds.append(a * a * get(at) + a * b * get(at + 1) + b * b * get(at + 2))
     p, q = steps(*kinds)
     weights = (p * a, p * b, q * a, q * b)
-    for r in range(ROWS):
-        for part in range(2):
-            tiles = turned(block[part * SLOTS : part * SLOTS + SLOTS, r])
+    turn = lax.axis_index("gy") % 4
+    for part in range(2):
+        sources = [device_of(turn, part * SLOTS + k) for k in range(SLOTS)]
+        for r in range(ROWS):
+            tiles = turned(jnp.stack([block[source, r] for source in sources]))
             at = slice(part * 128, part * 128 + 128)
             heads = []
             for c in range(4):
@@ -450,15 +499,10 @@
 
 
 def neighbour_pairs(step):
-    n_gx, n_gy = lax.axis_size("gx"), lax.axis_size("gy")
-    pairs = []
-    for source in range(n_gx * n_gy):
-        target = source + step
-        if 0 <= target < n_gx * n_gy:
-            pairs.append(
-                tuple((i % n_gx) * n_gy + i // n_gx for i in (source, target))
-            )
-    return pairs
+    n_gy = lax.axis_size("gy")
+    places = [gx * n_gy + gy for gy in range(n_gy) for gx in ORDERS[gy % 4]]
+    count = len(places)
+    return [(places[i], places[i + step]) for i in range(count) if 0 <= i + step < count]
 
 
 def per_device(

time: 96.9 us -> 91.5 us (0.944)
  waiting for transfers between devices: 16.8 us -> 8.3 us
  blocking collectives: 61.8 us -> 66.5 us
  starting transfers between devices: 6.8 us -> 5.27 us
    ppermute x1, waiting for transfers between devices: 10.9 us -> 0.9 us  [per_device(): low = lax.ppermute(mine, ('gx', 'gy'), neighbour_pairs(1))]
    all_to_all x1, blocking collectives: 13.4 us -> 18.9 us  [per_device(): block = lax.all_to_all(back, 'gx', 0, 0, tiled=True)]
    ppermute x1, starting transfers between devices: 4.88 us -> 2.11 us  [per_device(): high = lax.ppermute(mine, ('gx', 'gy'), neighbour_pairs(-1))]
    ppermute x1, waiting for transfers between devices: 5.87 us -> 7.4 us  [per_device(): high = lax.ppermute(mine, ('gx', 'gy'), neighbour_pairs(-1))]
    ppermute x1, starting transfers between devices: 1.92 us -> 3.16 us  [per_device(): low = lax.ppermute(mine, ('gx', 'gy'), neighbour_pairs(1))]
where the time goes in v4:
time: 91.5 us; the launch traced here: 91.1 us
  blocking collectives  66.5 us (73%)
  Pallas kernels  10.2 us (11%)
  waiting for transfers between devices  8.3 us (9%)
  starting transfers between devices  5.27 us (6%)
    all_to_all x1, blocking collectives, per_device(): mine = lax.all_to_all(sent, 'gx', 0, 0, tiled=True)  26.8 us
    all_to_all x1, blocking collectives, per_device(): lines = lax.all_to_all(lines, 'gy', 0, 0, tiled=True)  20.8 us
    all_to_all x1, blocking collectives, per_device(): block = lax.all_to_all(back, 'gx', 0, 0, tiled=True)  18.9 us
    pallas_call x4, Pallas kernels, call(): pl.pallas_call(kernel, out_shape=[jax.ShapeDtypeStruct(shape, F32) for sh...  10.2 us
    ppermute x1, waiting for transfers between devices, per_device(): high = lax.ppermute(mine, ('gx', 'gy'), neighbour_pairs(-1))  7.4 us
    ppermute x1, starting transfers between devices, per_device(): low = lax.ppermute(mine, ('gx', 'gy'), neighbour_pairs(1))  3.16 us
    ppermute x1, starting transfers between devices, per_device(): high = lax.ppermute(mine, ('gx', 'gy'), neighbour_pairs(-1))  2.11 us
  transfers between devices with their start and end apart: 2, of which 2 were waited for; matrix products, arithmetic and copies ran while one was open for 0% of the time, Pallas kernels for 0%

profile of v4, /device:TPU:1, one launch (start us, length us, event | category | flops | bytes accessed | tf_op | source)
XLA Modules:
  0.0 91.1 jit_solution(15009207757958902569)
XLA Ops:
  0.6 2.4 %pack_tables.1 = f32[32,4,8,128]{3,2,1,0:T(8,128)} custom-call(f32[16,6,2,256]{3,2,1,0:T(2,128)} %bitcast.8, f32[16,6,2,256]{3,2,1,0:T(2,128)} %bitcast.9, f32[6,2,256]{2,1,0:T(2,128)} %visc_in.1, s32[2,256]{1,0:T(2,128)} %count_in.1, s32[2,256]{1,0:T(2,128)} %grounded.1, s32[2,256]{1,0:T(2,128)} %pattern_in.1, f32[2,256]{1,0:T(2,128)} %beta_in.1, ...), custom_call_target="tpu_custom_call" | custom-call | tf_op jit(solution)/shard_map/pack_tables/pallas_call | solution.py:490
  3.0 0.0 copy-start.2
  3.0 26.8 %all_to_all.21.mine = f32[32,4,8,128]{3,2,1,0:T(8,128)S(1)} all-to-all(f32[32,4,8,128]{3,2,1,0:T(8,128)} %pack_tables.1), channel_id=1, replica_groups=mesh['gx'=32,'gy'=16] {'gx'}, dimensions={0} | all-to-all | bytes 1048576 | tf_op jit(solution)/shard_map/all_to_all | solution.py:540
  29.8 2.1 %collective-permute-start.1 = (f32[32,4,8,128]{3,2,1,0:T(8,128)S(1)}, f32[32,4,8,128]{3,2,1,0:T(8,128)S(1)}, u32[]{:S(2)}, u32[]{:S(2)}) collective-permute-start(f32[32,4,8,128]{3,2,1,0:T(8,128)S(1)} %all_to_all.21.mine), channel_id=1, source_target_pairs={{16,0},{32,16},{48,32},{112,48},{96,112},{80,96},{64,80},{128,64},... | collective-permute-start | bytes 1572872 | tf_op jit(solution)/shard_map/ppermute | solution.py:542
  31.9 3.2 %collective-permute-start = (f32[32,4,8,128]{3,2,1,0:T(8,128)S(1)}, f32[32,4,8,128]{3,2,1,0:T(8,128)S(1)}, u32[]{:S(2)}, u32[]{:S(2)}) collective-permute-start(f32[32,4,8,128]{3,2,1,0:T(8,128)S(1)} %all_to_all.21.mine), channel_id=1, source_target_pairs={{0,16},{16,32},{32,48},{48,112},{112,96},{96,80},{80,64},{64,128},... | collective-permute-start | bytes 1572872 | tf_op jit(solution)/shard_map/ppermute | solution.py:541
  35.1 0.0 copy-done.2
  35.1 0.1 copy.13
  35.2 0.1 reshape.15.coupling
  35.3 7.4 %collective-permute-done.1.high = f32[32,4,8,128]{3,2,1,0:T(8,128)S(1)} collective-permute-done((f32[32,4,8,128]{3,2,1,0:T(8,128)S(1)}, f32[32,4,8,128]{3,2,1,0:T(8,128)S(1)}, u32[]{:S(2)}, u32[]{:S(2)}) %collective-permute-start.1) | collective-permute-done | bytes 524320 | tf_op jit(solution)/shard_map/ppermute | solution.py:542
  42.7 0.9 collective-permute-done.low
  43.6 6.8 %solve_both.1 = f32[32,2,8,128]{3,2,1,0:T(8,128)S(1)} custom-call(f32[96]{0:T(128)S(1)} %reshape.15.coupling, f32[32,4,8,128]{3,2,1,0:T(8,128)S(1)} %collective-permute-done.low, f32[32,4,8,128]{3,2,1,0:T(8,128)S(1)} %all_to_all.21.mine, f32[32,4,8,128]{3,2,1,0:T(8,128)S(1)} %collective-permute-done.1.high), custom_call_target="tpu_custom_call" | custom-call | tf_op jit(solution)/shard_map/solve_both/pallas_call | solution.py:490
  50.5 18.9 %all_to_all.22.block = f32[32,2,8,128]{3,2,1,0:T(8,128)S(1)} all-to-all(f32[32,2,8,128]{3,2,1,0:T(8,128)S(1)} %solve_both.1), channel_id=1, replica_groups=mesh['gx'=32,'gy'=16] {'gx'}, dimensions={0} | all-to-all | bytes 524288 | tf_op jit(solution)/shard_map/all_to_all | solution.py:570
  69.4 0.0 copy-start
  69.4 0.0 copy-start.1
  69.4 0.1 sum_gx.1
  69.5 20.8 %all_to_all.23 = f32[16,1,128]{2,1,0:T(1,128)S(1)} all-to-all(f32[16,1,128]{2,1,0:T(1,128)S(1)} %bitcast.7), channel_id=1, replica_groups=mesh['gx'=32,'gy'=16] {'gy'}, dimensions={0} | all-to-all | bytes 16384 | tf_op jit(solution)/shard_map/all_to_all | solution.py:572
  90.3 0.0 copy-done
  90.3 0.0 copy-done.1
  90.3 0.8 combine.1
Async XLA Ops:
  3.0 32.1 %copy-start.2 = (f32[6,4,4]{0,2,1:T(4,128)S(1)}, f32[6,4,4]{0,2,1:T(4,128)}, u32[]{:S(2)}) copy-start(f32[6,4,4]{0,2,1:T(4,128)} %param.12) | copy-start | bytes 1156
  29.8 12.9 %collective-permute-start.1 = (f32[32,4,8,128]{3,2,1,0:T(8,128)S(1)}, f32[32,4,8,128]{3,2,1,0:T(8,128)S(1)}, u32[]{:S(2)}, u32[]{:S(2)}) collective-permute-start(f32[32,4,8,128]{3,2,1,0:T(8,128)S(1)} %all_to_all.21.mine), channel_id=1, source_target_pairs={{16,0},{32,16},{48,32},{112,48},{96,112},{80,96},{64,80},{128,64},... | collective-permute-start | bytes 1572872 | tf_op jit(solution)/shard_map/ppermute | solution.py:542
  31.9 11.7 %collective-permute-start = (f32[32,4,8,128]{3,2,1,0:T(8,128)S(1)}, f32[32,4,8,128]{3,2,1,0:T(8,128)S(1)}, u32[]{:S(2)}, u32[]{:S(2)}) collective-permute-start(f32[32,4,8,128]{3,2,1,0:T(8,128)S(1)} %all_to_all.21.mine), channel_id=1, source_target_pairs={{0,16},{16,32},{32,48},{48,112},{112,96},{96,80},{80,64},{64,128},... | collective-permute-start | bytes 1572872 | tf_op jit(solution)/shard_map/ppermute | solution.py:541
  69.4 20.9 %copy-start = (f32[2,2,256]{2,1,0:T(2,128)S(1)}, f32[2,2,256]{2,1,0:T(2,128)}, u32[]{:S(2)}) copy-start(f32[2,2,256]{2,1,0:T(2,128)} %vel.1) | copy-start | bytes 12292
  69.4 20.9 %copy-start.1 = (s32[2,256]{1,0:T(2,128)S(1)}, s32[2,256]{1,0:T(2,128)}, u32[]{:S(2)}) copy-start(s32[2,256]{1,0:T(2,128)} %grounded.1) | copy-start | bytes 6148

commit v5 on v4

--- a/solution.py
+++ b/solution.py
@@ -15,35 +15,29 @@
 CHUNK = 8
 SLOTS = 16
 OWN, NEAR = 1, 3
+CHUNK_ROWS = 26
 COUNT_ROW, PATTERN_ROW, RHS_ROW, BETA_ROW = 0, 1, 2, 4
 SPARE = 6
 
 
+def table_row(table, r, entry):
+    return ((table * ROWS + r) * 16 + entry) * LAYERS
+
+
 def iota(shape, dim):
     return lax.broadcasted_iota(jnp.int32, shape, dim)
 
 
-def chunk_order(turn, n_x, n_y):
-    order = []
-    if turn % 2 == 0:
-        for i in range(n_y):
-            for j in range(n_x):
-                x, y = (j if i % 2 == 0 else n_x - 1 - j), i
-                if turn == 2:
-                    x, y = n_x - 1 - x, n_y - 1 - y
-                order.append(y * n_x + x)
-    else:
-        for i in range(n_x):
-            for j in range(n_y):
-                x, y = i, (n_y - 1 - j if i % 2 == 0 else j)
-                if turn == 3:
-                    x, y = n_x - 1 - x, n_y - 1 - y
-                order.append(y * n_x + x)
-    return order
-
-
-GRID_X, GRID_Y = 4, 8
-ORDERS = [chunk_order(turn, GRID_X, GRID_Y) for turn in range(4)]
+ORDERS = (
+    (1, 29, 25, 21, 20, 23, 22, 18, 17, 16, 19, 15, 14, 13, 12, 8)
+    + (9, 10, 11, 7, 6, 5, 4, 0, 3, 31, 28, 24, 27, 26, 30, 2),
+    (2, 3, 7, 4, 8, 11, 15, 12, 16, 20, 24, 25, 26, 22, 21, 17)
+    + (13, 9, 5, 1, 0, 28, 29, 30, 31, 27, 23, 19, 18, 14, 10, 6),
+    (6, 7, 11, 10, 9, 8, 12, 13, 14, 15, 19, 16, 17, 18, 22, 23)
+    + (20, 21, 25, 29, 1, 2, 30, 26, 27, 24, 28, 31, 3, 0, 4, 5),
+    (5, 9, 13, 17, 21, 22, 26, 25, 24, 20, 16, 12, 15, 11, 8, 4)
+    + (7, 3, 2, 6, 10, 14, 18, 19, 23, 27, 31, 30, 29, 28, 0, 1),
+)
 
 
 def pick(turn, choices):
@@ -56,13 +50,36 @@
 
 
 def chunk_of(turn, gx):
-    x, y = gx % GRID_X, gx // GRID_X
-    back_x, back_y = GRID_X - 1 - x, GRID_Y - 1 - y
-    along_x = jnp.where(turn == 0, y, back_y)
-    step_x = jnp.where((along_x % 2 == 0) == (turn == 0), x, back_x)
-    along_y = jnp.where(turn == 1, x, back_x)
-    step_y = jnp.where((along_y % 2 == 0) == (turn == 1), back_y, y)
-    return jnp.where(turn % 2 == 0, along_x * GRID_X + step_x, along_y * GRID_Y + step_y)
+    chunk = 0
+    for k in range(len(ORDERS[0])):
+        chunk = jnp.where(device_of(turn, k) == gx, k, chunk)
+    return chunk
+
+
+def swap_slots(lines):
+    slot = iota((8, 128), 1) // CHUNK
+    sub = iota((8, 128), 0)
+    tiles = []
+    for part in range(2):
+        total = jnp.zeros((8, 128), F32)
+        for k in range(8):
+            total = jnp.where(sub == k, lines[part * 8 + k], total)
+        tiles.append(total)
+    low, high = tiles
+    odd = (slot & 8) != 0
+    tiles = [
+        jnp.where(odd, pltpu.roll(high, 64, 1), low),
+        jnp.where(odd, high, pltpu.roll(low, 64, 1)),
+    ]
+    for bit in (1, 2, 4):
+        up = ((sub & bit) == 0) & ((slot & bit) != 0)
+        down = ((sub & bit) != 0) & ((slot & bit) == 0)
+        for part in range(2):
+            tile = tiles[part]
+            raised = pltpu.roll(pltpu.roll(tile, 8 - bit, 0), CHUNK * bit, 1)
+            lowered = pltpu.roll(pltpu.roll(tile, bit, 0), 128 - CHUNK * bit, 1)
+            tiles[part] = jnp.where(up, raised, jnp.where(down, lowered, tile))
+    return [tiles[t // 8][t % 8 : t % 8 + 1, :] for t in range(16)]
 
 
 def turned(tiles):
@@ -71,7 +88,7 @@
 
 def pack_kernel(
     diag_in, inv_in, visc_in, count_in, grounded_in, pattern_in, beta_in, vel_in, message,
-    diag, inv, visc, count, grounded, pattern, beta, vel, folded, arrived,
+    diag, inv, visc, count, grounded, pattern, beta, vel, folded, chunks, arrived,
 ):
     pairs = (
         (count_in, count), (diag_in, diag), (inv_in, inv), (visc_in, visc), (grounded_in, grounded),
@@ -83,24 +100,17 @@
     ]
     for copy in copies:
         copy.start()
-    folded[...] = jnp.zeros(folded.shape, F32)
     for copy in copies:
         copy.wait()
     layer = iota((LAYERS, COLS), 0)
     actives = [layer < count[r : r + 1, :] for r in range(ROWS)]
-
-    def fold(cp, carry):
-        eye = jnp.where(cp % 5 == 0, 1.0, 0.0).astype(F32)
-        for t, table in enumerate((inv, diag)):
-            for r in range(ROWS):
+    for r in range(ROWS):
+        for cp in range(16):
+            eye = 1.0 if cp % 5 == 0 else 0.0
+            for t, table in enumerate((inv, diag)):
                 values = jnp.where(actives[r], table[cp, :, r, :], eye)
-                for part in range(2):
-                    folded[(t * 2 + r) * 2 + part, cp, 0:LAYERS, :] = values[
-                        :, part * 128 : part * 128 + 128
-                    ]
-        return carry
-
-    lax.fori_loop(0, 16, fold, 0)
+                at = table_row(t, r, cp)
+                folded[at : at + LAYERS, :] = values
     for r in range(ROWS):
         row = slice(r, r + 1)
         viscous = jnp.where(actives[r], visc[:, r, :], 0.0)
@@ -108,19 +118,20 @@
         lines = [viscous[k : k + 1] for k in range(LAYERS)]
         lines += [count[row, :].astype(F32), pattern[row, :].astype(F32)]
         lines += [force * vel[0, row, :], force * vel[1, row, :], beta[row, :]]
-        for slot, line in enumerate(lines):
-            for part in range(2):
-                folded[r * 2 + part, slot, SPARE : SPARE + 1, :] = line[
-                    :, part * 128 : part * 128 + 128
-                ]
-
+        lines += [jnp.zeros((1, COLS), F32)] * (SLOTS - len(lines))
+        for part in range(2):
+            at = slice(part * 128, part * 128 + 128)
+            for k, line in enumerate(swap_slots([line[:, at] for line in lines])):
+                chunks[part * SLOTS + k, 24 + r : 25 + r, :] = line
+    for part in range(2):
+        for m in range(3):
+            tiles = folded[m * 128 : m * 128 + 128, part * 128 : part * 128 + 128].T
+            at = slice(part * SLOTS, part * SLOTS + SLOTS)
+            chunks[at, m * 8 : m * 8 + 8, :] = tiles.reshape(SLOTS, 8, 128)
     turn = lax.axis_index("gy") % 4
-    for part in range(2):
-        targets = [device_of(turn, part * SLOTS + k) for k in range(SLOTS)]
-        for i in range(4):
-            tiles = turned(folded[i * 2 + part])
-            for k in range(SLOTS):
-                message[targets[k], i] = tiles[k]
+    for device in range(2 * SLOTS):
+        chunk = pick(turn, [order.index(device) for order in ORDERS])
+        message[device * CHUNK_ROWS : (device + 1) * CHUNK_ROWS, :] = chunks[chunk, 0:CHUNK_ROWS, :]
 
 
 def block_times(table, base, values, transposed):
@@ -308,36 +319,41 @@
             target[at + c] = jnp.zeros((4, 8, 128), F32)
 
 
-def unpack(block, j, inv, diag, vis, small):
+def unpack(block, j, inv, diag, vis, small, turned_rows):
     sub = iota((8, 128), 0)
-
-    def place(half, carry):
-        part = pl.ds(half * SLOTS, SLOTS)
+    for half in range(2):
+        for m in range(3):
+            rows = [
+                block[pl.ds((half * SLOTS + s) * CHUNK_ROWS + m * 8, 8), :] for s in range(SLOTS)
+            ]
+            turned_rows[m * 128 : m * 128 + 128, :] = jnp.concatenate(rows, axis=0).T
         for r in range(ROWS):
             i = half * 2 + r
-            tiles = turned(block[part, r])
-            inv[j * 16 : j * 16 + 16, i] = jnp.where(sub[None] < LAYERS, tiles, 0.0)
-            for target, base, lines in ((vis, 0, LAYERS), (small, LAYERS, 5)):
+            for t, target in enumerate((inv, diag)):
+                for cp in range(16):
+                    at = table_row(t, r, cp)
+                    tile = turned_rows[pl.ds(at, 8), :]
+                    target[j * 16 + cp, i] = jnp.where(sub < LAYERS, tile, 0.0)
+            lines = [
+                block[pl.ds((half * SLOTS + s) * CHUNK_ROWS + 24 + r, 1), :] for s in range(SLOTS)
+            ]
+            tiles = swap_slots(lines)
+            for target, base, count in ((vis, 0, LAYERS), (small, LAYERS, 5)):
                 total = jnp.zeros((8, 128), F32)
-                for k in range(lines):
-                    moved = pltpu.roll(tiles[base + k], (k - SPARE) % 8, 0)
-                    total = jnp.where(sub == k, moved, total)
+                for k in range(count):
+                    total = jnp.where(sub == k, tiles[base + k], total)
                 target[j, i] = total
-            diag[j * 16 : j * 16 + 16, i] = turned(block[part, 2 + r])
-        return carry
-
-    lax.fori_loop(0, 2, place, 0)
 
 
 def solve_kernel(
     coupling, low, mine, high, message,
-    inv, diag, vis, small, kappa, spread, res, res_two, first, carried, update, image, last, start,
+    inv, diag, vis, small, kappa, spread, res, res_two, first, carried, update, image, last, start, turned_rows,
 ):
     gx, gy = lax.axis_index("gx"), lax.axis_index("gy")
     nx, ny = lax.axis_size("gx"), lax.axis_size("gy")
     chunk = chunk_of(gy % 4, gx)
     for j, block in enumerate((low, mine, high)):
-        unpack(block, j, inv, diag, vis, small)
+        unpack(block, j, inv, diag, vis, small, turned_rows)
     for c in range(4):
         carried[c] = jnp.zeros((4, 8, 128), F32)
         carried[16 + c] = jnp.zeros((4, 8, 128), F32)
@@ -533,13 +549,19 @@
         "pack_tables",
         raw,
         [HBM] * 8,
-        [(n_gx, 4, 8, 128)],
+        [(n_gx * CHUNK_ROWS, 128)],
         [pltpu.VMEM(x.shape, x.dtype) for x in raw]
-        + [pltpu.VMEM((8, 16, 8, 128), F32), pltpu.SemaphoreType.DMA((8,))],
+        + [
+            pltpu.VMEM((384, COLS), F32),
+            pltpu.VMEM((n_gx, 32, 128), F32),
+            pltpu.SemaphoreType.DMA((8,)),
+        ],
     )
+    sent = sent.reshape(n_gx, CHUNK_ROWS // 2, 2, 128)
     mine = lax.all_to_all(sent, "gx", 0, 0, tiled=True)
     low = lax.ppermute(mine, ("gx", "gy"), neighbour_pairs(1))
     high = lax.ppermute(mine, ("gx", "gy"), neighbour_pairs(-1))
+    blocks = [x.reshape(n_gx * CHUNK_ROWS, 128) for x in (low, mine, high)]
 
     def field(count):
         return pltpu.VMEM((count, 4, 8, 128), F32)
@@ -547,8 +569,8 @@
     (back,) = call(
         solve_kernel,
         "solve_both",
-        [coupling.reshape(96), low, mine, high],
-        [SMEM, VMEM, VMEM, VMEM],
+        [coupling.reshape(96)] + blocks,
+        [SMEM] + [VMEM] * 3,
         [(n_gx, 2, 8, 128)],
         [
             field(64),
@@ -565,6 +587,7 @@
             field(16),
             field(16),
             field(8),
+            pltpu.VMEM((392, 128), F32),
         ],
     )
     block = lax.all_to_all(back, "gx", 0, 0, tiled=True)

time: 91.5 us -> 87.3 us (0.954)
  blocking collectives: 66.5 us -> 63.4 us
  waiting for transfers between devices: 8.3 us -> 5.26 us
  starting transfers between devices: 5.27 us -> 6.48 us
    ppermute x1, waiting for transfers between devices: 7.4 us -> 3.64 us  [per_device(): high = lax.ppermute(mine, ('gx', 'gy'), neighbour_pairs(-1))]
    all_to_all x1, blocking collectives: 26.8 us -> 24.4 us  [per_device(): mine = lax.all_to_all(sent, 'gx', 0, 0, tiled=True)]
    all_to_all x1, blocking collectives: 18.9 us -> 16.6 us  [per_device(): block = lax.all_to_all(back, 'gx', 0, 0, tiled=True)]
    all_to_all x1, blocking collectives: 20.8 us -> 22.4 us  [per_device(): lines = lax.all_to_all(lines, 'gy', 0, 0, tiled=True)]
where the time goes in v5:
time: 87.3 us; the launch traced here: 87 us
  blocking collectives  63.4 us (73%)
  Pallas kernels  10.9 us (12%)
  starting transfers between devices  6.48 us (7%)
  waiting for transfers between devices  5.26 us (6%)
    all_to_all x1, blocking collectives, per_device(): mine = lax.all_to_all(sent, 'gx', 0, 0, tiled=True)  24.4 us
    all_to_all x1, blocking collectives, per_device(): lines = lax.all_to_all(lines, 'gy', 0, 0, tiled=True)  22.4 us
    all_to_all x1, blocking collectives, per_device(): block = lax.all_to_all(back, 'gx', 0, 0, tiled=True)  16.6 us
    pallas_call x4, Pallas kernels, call(): pl.pallas_call(kernel, out_shape=[jax.ShapeDtypeStruct(shape, F32) for sh...  10.9 us
    ppermute x1, starting transfers between devices, per_device(): low = lax.ppermute(mine, ('gx', 'gy'), neighbour_pairs(1))  3.67 us
    ppermute x1, waiting for transfers between devices, per_device(): high = lax.ppermute(mine, ('gx', 'gy'), neighbour_pairs(-1))  3.64 us
    ppermute x1, starting transfers between devices, per_device(): high = lax.ppermute(mine, ('gx', 'gy'), neighbour_pairs(-1))  2.81 us
  transfers between devices with their start and end apart: 2, of which 2 were waited for; matrix products, arithmetic and copies ran while one was open for 0% of the time, Pallas kernels for 0%

profile of v5, /device:TPU:1, one launch (start us, length us, event | category | flops | bytes accessed | tf_op | source)
XLA Modules:
  0.0 87.0 jit_solution(16176628591263838153)
XLA Ops:
  0.6 2.5 %pack_tables.1 = f32[832,128]{1,0:T(8,128)} custom-call(f32[16,6,2,256]{3,2,1,0:T(2,128)} %bitcast.16, f32[16,6,2,256]{3,2,1,0:T(2,128)} %bitcast.17, f32[6,2,256]{2,1,0:T(2,128)} %visc_in.1, s32[2,256]{1,0:T(2,128)} %count_in.1, s32[2,256]{1,0:T(2,128)} %grounded.1, s32[2,256]{1,0:T(2,128)} %pattern_in.1, f32[2,256]{1,0:T(2,128)} %beta_in.1, f32[2,2,256]{2,1,0:T(2,128)} %vel.1), custom_call_target="tpu_custom_call" | custom-call | tf_op jit(solution)/shard_map/pack_tables/pallas_call | solution.py:506
  3.1 0.0 copy-start.2
  3.1 24.4 %all_to_all.21 = f32[32,13,2,128]{3,2,1,0:T(2,128)S(1)} all-to-all(f32[32,13,2,128]{3,2,1,0:T(2,128)} %bitcast.15), channel_id=1, replica_groups=mesh['gx'=32,'gy'=16] {'gx'}, dimensions={0} | all-to-all | bytes 851968 | tf_op jit(solution)/shard_map/all_to_all | solution.py:561
  27.5 2.8 %collective-permute-start.1 = (f32[32,13,2,128]{3,2,1,0:T(2,128)S(1)}, f32[32,13,2,128]{3,2,1,0:T(2,128)S(1)}, u32[]{:S(2)}, u32[]{:S(2)}) collective-permute-start(f32[32,13,2,128]{3,2,1,0:T(2,128)S(1)} %all_to_all.21), channel_id=1, source_target_pairs={{464,16},{400,464},{336,400},{320,336},{368,320},{352,368},{288,35... | collective-permute-start | bytes 1277960 | tf_op jit(solution)/shard_map/ppermute | solution.py:563
  30.3 3.7 %collective-permute-start = (f32[32,13,2,128]{3,2,1,0:T(2,128)S(1)}, f32[32,13,2,128]{3,2,1,0:T(2,128)S(1)}, u32[]{:S(2)}, u32[]{:S(2)}) collective-permute-start(f32[32,13,2,128]{3,2,1,0:T(2,128)S(1)} %all_to_all.21), channel_id=1, source_target_pairs={{16,464},{464,400},{400,336},{336,320},{320,368},{368,352},{352,28... | collective-permute-start | bytes 1277960 | tf_op jit(solution)/shard_map/ppermute | solution.py:562
  34.0 0.0 copy-done.2
  34.0 0.1 copy.13
  34.1 0.1 reshape.27.coupling
  34.2 3.6 %collective-permute-done.1 = f32[32,13,2,128]{3,2,1,0:T(2,128)S(1)} collective-permute-done((f32[32,13,2,128]{3,2,1,0:T(2,128)S(1)}, f32[32,13,2,128]{3,2,1,0:T(2,128)S(1)}, u32[]{:S(2)}, u32[]{:S(2)}) %collective-permute-start.1) | collective-permute-done | bytes 426016 | tf_op jit(solution)/shard_map/ppermute | solution.py:563
  37.9 1.6 %collective-permute-done = f32[32,13,2,128]{3,2,1,0:T(2,128)S(1)} collective-permute-done((f32[32,13,2,128]{3,2,1,0:T(2,128)S(1)}, f32[32,13,2,128]{3,2,1,0:T(2,128)S(1)}, u32[]{:S(2)}, u32[]{:S(2)}) %collective-permute-start) | collective-permute-done | bytes 426016 | tf_op jit(solution)/shard_map/ppermute | solution.py:562
  39.5 7.5 %solve_both.1 = f32[32,2,8,128]{3,2,1,0:T(8,128)S(1)} custom-call(f32[96]{0:T(128)S(1)} %reshape.27.coupling, f32[832,128]{1,0:T(8,128)S(1)} %bitcast.12, f32[832,128]{1,0:T(8,128)S(1)} %bitcast.10, f32[832,128]{1,0:T(8,128)S(1)} %bitcast.11), custom_call_target="tpu_custom_call" | custom-call | tf_op jit(solution)/shard_map/solve_both/pallas_call | solution.py:506
  47.0 16.6 %all_to_all.22.block = f32[32,2,8,128]{3,2,1,0:T(8,128)S(1)} all-to-all(f32[32,2,8,128]{3,2,1,0:T(8,128)S(1)} %solve_both.1), channel_id=1, replica_groups=mesh['gx'=32,'gy'=16] {'gx'}, dimensions={0} | all-to-all | bytes 524288 | tf_op jit(solution)/shard_map/all_to_all | solution.py:593
  63.6 0.0 copy-start
  63.6 0.0 copy-start.1
  63.6 0.1 sum_gx.1
  63.7 22.4 %all_to_all.23 = f32[16,1,128]{2,1,0:T(1,128)S(1)} all-to-all(f32[16,1,128]{2,1,0:T(1,128)S(1)} %bitcast.14), channel_id=1, replica_groups=mesh['gx'=32,'gy'=16] {'gy'}, dimensions={0} | all-to-all | bytes 16384 | tf_op jit(solution)/shard_map/all_to_all | solution.py:595
  86.1 0.0 copy-done
  86.1 0.0 copy-done.1
  86.1 0.8 combine.1
Async XLA Ops:
  3.1 30.9 %copy-start.2 = (f32[6,4,4]{0,2,1:T(4,128)S(1)}, f32[6,4,4]{0,2,1:T(4,128)}, u32[]{:S(2)}) copy-start(f32[6,4,4]{0,2,1:T(4,128)} %param.12) | copy-start | bytes 1156
  27.5 10.4 %collective-permute-start.1 = (f32[32,13,2,128]{3,2,1,0:T(2,128)S(1)}, f32[32,13,2,128]{3,2,1,0:T(2,128)S(1)}, u32[]{:S(2)}, u32[]{:S(2)}) collective-permute-start(f32[32,13,2,128]{3,2,1,0:T(2,128)S(1)} %all_to_all.21), channel_id=1, source_target_pairs={{464,16},{400,464},{336,400},{320,336},{368,320},{352,368},{288,35... | collective-permute-start | bytes 1277960 | tf_op jit(solution)/shard_map/ppermute | solution.py:563
  30.3 9.2 %collective-permute-start = (f32[32,13,2,128]{3,2,1,0:T(2,128)S(1)}, f32[32,13,2,128]{3,2,1,0:T(2,128)S(1)}, u32[]{:S(2)}, u32[]{:S(2)}) collective-permute-start(f32[32,13,2,128]{3,2,1,0:T(2,128)S(1)} %all_to_all.21), channel_id=1, source_target_pairs={{16,464},{464,400},{400,336},{336,320},{320,368},{368,352},{352,28... | collective-permute-start | bytes 1277960 | tf_op jit(solution)/shard_map/ppermute | solution.py:562
  63.6 22.5 %copy-start = (f32[2,2,256]{2,1,0:T(2,128)S(1)}, f32[2,2,256]{2,1,0:T(2,128)}, u32[]{:S(2)}) copy-start(f32[2,2,256]{2,1,0:T(2,128)} %vel.1) | copy-start | bytes 12292
  63.6 22.5 %copy-start.1 = (s32[2,256]{1,0:T(2,128)S(1)}, s32[2,256]{1,0:T(2,128)}, u32[]{:S(2)}) copy-start(s32[2,256]{1,0:T(2,128)} %grounded.1) | copy-start | bytes 6148

commit v6 on v5

--- a/solution.py
+++ b/solution.py
@@ -16,6 +16,7 @@
 SLOTS = 16
 OWN, NEAR = 1, 3
 CHUNK_ROWS = 26
+LINES = 32
 COUNT_ROW, PATTERN_ROW, RHS_ROW, BETA_ROW = 0, 1, 2, 4
 SPARE = 6
 
@@ -56,39 +57,13 @@
     return chunk
 
 
-def swap_slots(lines):
-    slot = iota((8, 128), 1) // CHUNK
-    sub = iota((8, 128), 0)
-    tiles = []
-    for part in range(2):
-        total = jnp.zeros((8, 128), F32)
-        for k in range(8):
-            total = jnp.where(sub == k, lines[part * 8 + k], total)
-        tiles.append(total)
-    low, high = tiles
-    odd = (slot & 8) != 0
-    tiles = [
-        jnp.where(odd, pltpu.roll(high, 64, 1), low),
-        jnp.where(odd, high, pltpu.roll(low, 64, 1)),
-    ]
-    for bit in (1, 2, 4):
-        up = ((sub & bit) == 0) & ((slot & bit) != 0)
-        down = ((sub & bit) != 0) & ((slot & bit) == 0)
-        for part in range(2):
-            tile = tiles[part]
-            raised = pltpu.roll(pltpu.roll(tile, 8 - bit, 0), CHUNK * bit, 1)
-            lowered = pltpu.roll(pltpu.roll(tile, bit, 0), 128 - CHUNK * bit, 1)
-            tiles[part] = jnp.where(up, raised, jnp.where(down, lowered, tile))
-    return [tiles[t // 8][t % 8 : t % 8 + 1, :] for t in range(16)]
-
-
 def turned(tiles):
     return tiles.reshape(128, 128).T.reshape(SLOTS, 8, 128)
 
 
 def pack_kernel(
     diag_in, inv_in, visc_in, count_in, grounded_in, pattern_in, beta_in, vel_in, message,
-    diag, inv, visc, count, grounded, pattern, beta, vel, folded, chunks, arrived,
+    diag, inv, visc, count, grounded, pattern, beta, vel, folded, others, chunks, arrived,
 ):
     pairs = (
         (count_in, count), (diag_in, diag), (inv_in, inv), (visc_in, visc), (grounded_in, grounded),
@@ -111,18 +86,20 @@
                 values = jnp.where(actives[r], table[cp, :, r, :], eye)
                 at = table_row(t, r, cp)
                 folded[at : at + LAYERS, :] = values
+    others[...] = jnp.zeros(others.shape, F32)
     for r in range(ROWS):
         row = slice(r, r + 1)
-        viscous = jnp.where(actives[r], visc[:, r, :], 0.0)
         force = -(grounded[row, :].astype(F32) * beta[row, :])
-        lines = [viscous[k : k + 1] for k in range(LAYERS)]
-        lines += [count[row, :].astype(F32), pattern[row, :].astype(F32)]
+        others[r * 16 : r * 16 + LAYERS, :] = jnp.where(actives[r], visc[:, r, :], 0.0)
+        lines = [count[row, :].astype(F32), pattern[row, :].astype(F32)]
         lines += [force * vel[0, row, :], force * vel[1, row, :], beta[row, :]]
-        lines += [jnp.zeros((1, COLS), F32)] * (SLOTS - len(lines))
-        for part in range(2):
-            at = slice(part * 128, part * 128 + 128)
-            for k, line in enumerate(swap_slots([line[:, at] for line in lines])):
-                chunks[part * SLOTS + k, 24 + r : 25 + r, :] = line
+        for k, line in enumerate(lines):
+            others[r * 16 + 8 + k : r * 16 + 9 + k, :] = line
+    for part in range(2):
+        at = slice(part * 128, part * 128 + 128)
+        moved = [pltpu.roll(others[:, at], 6 - 2 * m, 1) for m in range(3)] + [others[:, at]]
+        tiles = jnp.concatenate(moved, axis=0).T
+        chunks[part * SLOTS : part * SLOTS + SLOTS, 18:26, :] = tiles.reshape(SLOTS, 8, 128)
     for part in range(2):
         for m in range(3):
             tiles = folded[m * 128 : m * 128 + 128, part * 128 : part * 128 + 128].T
@@ -226,7 +203,12 @@
         return i * 4, other, other
 
 
-def sweep(kind, res, first, carried, update, image, own_only, tables):
+def run_all(count, step):
+    for i in range(count):
+        step(i, 0)
+
+
+def sweep(kind, res, first, carried, carried_on, update, image, own_only, tables):
     inv, diag, vis, kappa, coupling = tables
     transposed = kind.transposed
 
@@ -240,7 +222,7 @@
             carried[at + c] = nu * y
         return carry
 
-    lax.fori_loop(0, kind.count, initial, 0)
+    run_all(kind.count, initial)
 
     def correct(i, carry):
         j = kind.block(i)
@@ -251,26 +233,20 @@
         y0 = [first[i * 4 + c] for c in range(4)]
         own = block_times(diag, j * 16, y0, transposed)
         rest = [res[i * 4 + c] - own[c] + nu * sums[c] for c in range(4)]
+        at = kind.place(i)[0]
         for c, y in enumerate(block_times(inv, j * 16, rest, transposed)):
-            update[i * 4 + c] = y0[c] + y
+            z = y0[c] + y
+            update[i * 4 + c] = z
+            carried_on[at + c] = nu * z
         return carry
 
-    lax.fori_loop(0, kind.count, correct, 0)
-
-    def carry_on(i, carry):
-        nu = vis[kind.block(i)]
-        at = kind.place(i)[0]
-        for c in range(4):
-            carried[at + c] = nu * update[i * 4 + c]
-        return carry
-
-    lax.fori_loop(0, kind.count, carry_on, 0)
+    run_all(kind.count, correct)
 
     def apply(i, carry):
         if own_only:
             i = i * 2 if kind is Adjoint else 1
         j = kind.block(i)
-        sums = stencil(carried, *kind.place(i), coupling, transposed, None)
+        sums = stencil(carried_on, *kind.place(i), coupling, transposed, None)
         values = [update[i * 4 + c] for c in range(4)]
         own = block_times(diag, j * 16, values, transposed)
         nu = vis[j]
@@ -278,7 +254,7 @@
             image[i * 4 + c] = own[c] - nu * sums[c]
         return carry
 
-    lax.fori_loop(0, kind.own if own_only else kind.count, apply, 0)
+    run_all(kind.own if own_only else kind.count, apply)
 
 
 def dots_of(residual, image, last, at_of, pairs):
@@ -321,33 +297,33 @@
 
 def unpack(block, j, inv, diag, vis, small, turned_rows):
     sub = iota((8, 128), 0)
+    pair = iota((LINES, 128), 1) % CHUNK // 2
     for half in range(2):
+
+        def rows_at(row):
+            at = [(half * SLOTS + s) * CHUNK_ROWS + row for s in range(SLOTS)]
+            return jnp.concatenate([block[pl.ds(k, 8), :] for k in at], axis=0).T
+
         for m in range(3):
-            rows = [
-                block[pl.ds((half * SLOTS + s) * CHUNK_ROWS + m * 8, 8), :] for s in range(SLOTS)
-            ]
-            turned_rows[m * 128 : m * 128 + 128, :] = jnp.concatenate(rows, axis=0).T
+            turned_rows[m * 128 : m * 128 + 128, :] = rows_at(m * 8)
         for r in range(ROWS):
-            i = half * 2 + r
             for t, target in enumerate((inv, diag)):
                 for cp in range(16):
-                    at = table_row(t, r, cp)
-                    tile = turned_rows[pl.ds(at, 8), :]
-                    target[j * 16 + cp, i] = jnp.where(sub < LAYERS, tile, 0.0)
-            lines = [
-                block[pl.ds((half * SLOTS + s) * CHUNK_ROWS + 24 + r, 1), :] for s in range(SLOTS)
-            ]
-            tiles = swap_slots(lines)
-            for target, base, count in ((vis, 0, LAYERS), (small, LAYERS, 5)):
-                total = jnp.zeros((8, 128), F32)
-                for k in range(count):
-                    total = jnp.where(sub == k, tiles[base + k], total)
-                target[j, i] = total
+                    tile = turned_rows[pl.ds(table_row(t, r, cp), 8), :]
+                    target[j * 16 + cp, half * 2 + r] = jnp.where(sub < LAYERS, tile, 0.0)
+        others = rows_at(18)
+        lines = others[3 * LINES :]
+        for m in range(3):
+            moved = pltpu.roll(others[m * LINES : (m + 1) * LINES], (2 * m - 6) % 128, 1)
+            lines = jnp.where(pair == m, moved, lines)
+        for r in range(ROWS):
+            vis[j, half * 2 + r] = lines[r * 16 : r * 16 + 8]
+            small[j, half * 2 + r] = lines[r * 16 + 8 : r * 16 + 16]
 
 
 def solve_kernel(
     coupling, low, mine, high, message,
-    inv, diag, vis, small, kappa, spread, res, res_two, first, carried, update, image, last, start, turned_rows,
+    inv, diag, vis, small, kappa, spread, res, res_two, first, carried, carried_on, update, image, last, start, turned_rows,
 ):
     gx, gy = lax.axis_index("gx"), lax.axis_index("gy")
     nx, ny = lax.axis_size("gx"), lax.axis_size("gy")
@@ -355,8 +331,9 @@
     for j, block in enumerate((low, mine, high)):
         unpack(block, j, inv, diag, vis, small, turned_rows)
     for c in range(4):
-        carried[c] = jnp.zeros((4, 8, 128), F32)
-        carried[16 + c] = jnp.zeros((4, 8, 128), F32)
+        for field in (carried, carried_on):
+            field[c] = jnp.zeros((4, 8, 128), F32)
+            field[16 + c] = jnp.zeros((4, 8, 128), F32)
 
     shape = (4, 8, 128)
     layer = iota(shape, 1)
@@ -398,21 +375,21 @@
             table[NEAR * size + k] = merged(table[2 * size + k], table[k])
 
     tables = (inv, diag, vis, kappa, coupling)
-    sweep(Forward, res, first, carried, update, image, False, tables)
+    sweep(Forward, res, first, carried, carried_on, update, image, False, tables)
     layer_sums(update, spread, res_two, 0)
     for t in range(12):
         res[t] = res[t] - image[t]
-    sweep(Forward, res, first, carried, update, last, True, tables)
+    sweep(Forward, res, first, carried, carried_on, update, last, True, tables)
     layer_sums(update, spread, res_two, 1)
     dots = dots_of(res, image, last, lambda v: 4, ((0, 0),))
 
-    sweep(Adjoint, res_two, first, carried, update, image, False, tables)
+    sweep(Adjoint, res_two, first, carried, carried_on, update, image, False, tables)
     for v in range(2):
         for c in range(4):
             start[v * 4 + c] = update[v * 8 + c]
     for t in range(16):
         res_two[t] = res_two[t] - image[t]
-    sweep(Adjoint, res_two, first, carried, update, last, True, tables)
+    sweep(Adjoint, res_two, first, carried, carried_on, update, last, True, tables)
     dots += dots_of(res_two, image, last, lambda v: v * 8, ((0, 0), (0, 1), (1, 1)))
 
     before, here, after = small[0], small[1], small[2]
@@ -553,6 +530,7 @@
         [pltpu.VMEM(x.shape, x.dtype) for x in raw]
         + [
             pltpu.VMEM((384, COLS), F32),
+            pltpu.VMEM((LINES, COLS), F32),
             pltpu.VMEM((n_gx, 32, 128), F32),
             pltpu.SemaphoreType.DMA((8,)),
         ],
@@ -582,6 +560,7 @@
             field(12),
             field(16),
             field(16),
+            field(20),
             field(20),
             field(16),
             field(16),

time: 87.3 us -> 85.5 us (0.979)
  Pallas kernels: 10.9 us -> 9.07 us
    pallas_call x4, Pallas kernels: 10.9 us -> 9.07 us  [call(): pl.pallas_call(kernel, out_shape=[jax.ShapeDtypeStruct(shape, F32) for sh...]
where the time goes in v6:
time: 85.5 us; the launch traced here: 85.1 us
  blocking collectives  63.4 us (74%)
  Pallas kernels  9.07 us (11%)
  starting transfers between devices  6.48 us (8%)
  waiting for transfers between devices  5.25 us (6%)
    all_to_all x1, blocking collectives, per_device(): mine = lax.all_to_all(sent, 'gx', 0, 0, tiled=True)  24.4 us
    all_to_all x1, blocking collectives, per_device(): lines = lax.all_to_all(lines, 'gy', 0, 0, tiled=True)  22.4 us
    all_to_all x1, blocking collectives, per_device(): block = lax.all_to_all(back, 'gx', 0, 0, tiled=True)  16.6 us
    pallas_call x4, Pallas kernels, call(): pl.pallas_call(kernel, out_shape=[jax.ShapeDtypeStruct(shape, F32) for sh...  9.07 us
    ppermute x1, starting transfers between devices, per_device(): low = lax.ppermute(mine, ('gx', 'gy'), neighbour_pairs(1))  3.68 us
    ppermute x1, waiting for transfers between devices, per_device(): high = lax.ppermute(mine, ('gx', 'gy'), neighbour_pairs(-1))  3.64 us
    ppermute x1, starting transfers between devices, per_device(): high = lax.ppermute(mine, ('gx', 'gy'), neighbour_pairs(-1))  2.8 us
  transfers between devices with their start and end apart: 2, of which 2 were waited for; matrix products, arithmetic and copies ran while one was open for 0% of the time, Pallas kernels for 0%

profile of v6, /device:TPU:1, one launch (start us, length us, event | category | flops | bytes accessed | tf_op | source)
XLA Modules:
  0.0 85.1 jit_solution(4602834132404182026)
XLA Ops:
  0.6 2.3 %pack_tables.1 = f32[832,128]{1,0:T(8,128)} custom-call(f32[16,6,2,256]{3,2,1,0:T(2,128)} %bitcast.16, f32[16,6,2,256]{3,2,1,0:T(2,128)} %bitcast.17, f32[6,2,256]{2,1,0:T(2,128)} %visc_in.1, s32[2,256]{1,0:T(2,128)} %count_in.1, s32[2,256]{1,0:T(2,128)} %grounded.1, s32[2,256]{1,0:T(2,128)} %pattern_in.1, f32[2,256]{1,0:T(2,128)} %beta_in.1, f32[2,2,256]{2,1,0:T(2,128)} %vel.1), custom_call_target="tpu_custom_call" | custom-call | tf_op jit(solution)/shard_map/pack_tables/pallas_call | solution.py:483
  2.9 0.0 copy-start.2
  2.9 24.4 %all_to_all.21 = f32[32,13,2,128]{3,2,1,0:T(2,128)S(1)} all-to-all(f32[32,13,2,128]{3,2,1,0:T(2,128)} %bitcast.15), channel_id=1, replica_groups=mesh['gx'=32,'gy'=16] {'gx'}, dimensions={0} | all-to-all | bytes 851968 | tf_op jit(solution)/shard_map/all_to_all | solution.py:539
  27.3 2.8 %collective-permute-start.1 = (f32[32,13,2,128]{3,2,1,0:T(2,128)S(1)}, f32[32,13,2,128]{3,2,1,0:T(2,128)S(1)}, u32[]{:S(2)}, u32[]{:S(2)}) collective-permute-start(f32[32,13,2,128]{3,2,1,0:T(2,128)S(1)} %all_to_all.21), channel_id=1, source_target_pairs={{464,16},{400,464},{336,400},{320,336},{368,320},{352,368},{288,35... | collective-permute-start | bytes 1277960 | tf_op jit(solution)/shard_map/ppermute | solution.py:541
  30.1 3.7 %collective-permute-start = (f32[32,13,2,128]{3,2,1,0:T(2,128)S(1)}, f32[32,13,2,128]{3,2,1,0:T(2,128)S(1)}, u32[]{:S(2)}, u32[]{:S(2)}) collective-permute-start(f32[32,13,2,128]{3,2,1,0:T(2,128)S(1)} %all_to_all.21), channel_id=1, source_target_pairs={{16,464},{464,400},{400,336},{336,320},{320,368},{368,352},{352,28... | collective-permute-start | bytes 1277960 | tf_op jit(solution)/shard_map/ppermute | solution.py:540
  33.8 0.0 copy-done.2
  33.8 0.1 copy.13
  34.0 0.1 reshape.27.coupling
  34.1 3.6 %collective-permute-done.1 = f32[32,13,2,128]{3,2,1,0:T(2,128)S(1)} collective-permute-done((f32[32,13,2,128]{3,2,1,0:T(2,128)S(1)}, f32[32,13,2,128]{3,2,1,0:T(2,128)S(1)}, u32[]{:S(2)}, u32[]{:S(2)}) %collective-permute-start.1) | collective-permute-done | bytes 426016 | tf_op jit(solution)/shard_map/ppermute | solution.py:541
  37.7 1.6 %collective-permute-done = f32[32,13,2,128]{3,2,1,0:T(2,128)S(1)} collective-permute-done((f32[32,13,2,128]{3,2,1,0:T(2,128)S(1)}, f32[32,13,2,128]{3,2,1,0:T(2,128)S(1)}, u32[]{:S(2)}, u32[]{:S(2)}) %collective-permute-start) | collective-permute-done | bytes 426016 | tf_op jit(solution)/shard_map/ppermute | solution.py:540
  39.3 5.8 %solve_both.1 = f32[32,2,8,128]{3,2,1,0:T(8,128)S(1)} custom-call(f32[96]{0:T(128)S(1)} %reshape.27.coupling, f32[832,128]{1,0:T(8,128)S(1)} %bitcast.12, f32[832,128]{1,0:T(8,128)S(1)} %bitcast.10, f32[832,128]{1,0:T(8,128)S(1)} %bitcast.11), custom_call_target="tpu_custom_call" | custom-call | tf_op jit(solution)/shard_map/solve_both/pallas_call | solution.py:483
  45.2 16.6 %all_to_all.22.block = f32[32,2,8,128]{3,2,1,0:T(8,128)S(1)} all-to-all(f32[32,2,8,128]{3,2,1,0:T(8,128)S(1)} %solve_both.1), channel_id=1, replica_groups=mesh['gx'=32,'gy'=16] {'gx'}, dimensions={0} | all-to-all | bytes 524288 | tf_op jit(solution)/shard_map/all_to_all | solution.py:572
  61.8 0.0 copy-start
  61.8 0.0 copy-start.1
  61.8 0.1 sum_gx.1
  61.9 22.4 %all_to_all.23 = f32[16,1,128]{2,1,0:T(1,128)S(1)} all-to-all(f32[16,1,128]{2,1,0:T(1,128)S(1)} %bitcast.14), channel_id=1, replica_groups=mesh['gx'=32,'gy'=16] {'gy'}, dimensions={0} | all-to-all | bytes 16384 | tf_op jit(solution)/shard_map/all_to_all | solution.py:574
  84.3 0.0 copy-done
  84.3 0.0 copy-done.1
  84.3 0.8 combine.1
Async XLA Ops:
  2.9 30.9 %copy-start.2 = (f32[6,4,4]{0,2,1:T(4,128)S(1)}, f32[6,4,4]{0,2,1:T(4,128)}, u32[]{:S(2)}) copy-start(f32[6,4,4]{0,2,1:T(4,128)} %param.12) | copy-start | bytes 1156
  27.3 10.4 %collective-permute-start.1 = (f32[32,13,2,128]{3,2,1,0:T(2,128)S(1)}, f32[32,13,2,128]{3,2,1,0:T(2,128)S(1)}, u32[]{:S(2)}, u32[]{:S(2)}) collective-permute-start(f32[32,13,2,128]{3,2,1,0:T(2,128)S(1)} %all_to_all.21), channel_id=1, source_target_pairs={{464,16},{400,464},{336,400},{320,336},{368,320},{352,368},{288,35... | collective-permute-start | bytes 1277960 | tf_op jit(solution)/shard_map/ppermute | solution.py:541
  30.1 9.2 %collective-permute-start = (f32[32,13,2,128]{3,2,1,0:T(2,128)S(1)}, f32[32,13,2,128]{3,2,1,0:T(2,128)S(1)}, u32[]{:S(2)}, u32[]{:S(2)}) collective-permute-start(f32[32,13,2,128]{3,2,1,0:T(2,128)S(1)} %all_to_all.21), channel_id=1, source_target_pairs={{16,464},{464,400},{400,336},{336,320},{320,368},{368,352},{352,28... | collective-permute-start | bytes 1277960 | tf_op jit(solution)/shard_map/ppermute | solution.py:540
  61.8 22.5 %copy-start = (f32[2,2,256]{2,1,0:T(2,128)S(1)}, f32[2,2,256]{2,1,0:T(2,128)}, u32[]{:S(2)}) copy-start(f32[2,2,256]{2,1,0:T(2,128)} %vel.1) | copy-start | bytes 12292
  61.8 22.5 %copy-start.1 = (s32[2,256]{1,0:T(2,128)S(1)}, s32[2,256]{1,0:T(2,128)}, u32[]{:S(2)}) copy-start(s32[2,256]{1,0:T(2,128)} %grounded.1) | copy-start | bytes 6148

commit v7 on v6

--- a/solution.py
+++ b/solution.py
@@ -16,13 +16,16 @@
 SLOTS = 16
 OWN, NEAR = 1, 3
 CHUNK_ROWS = 26
+RUNS = (((0, 6, 7), (7, 7, 25)), ((0, 2, 4), (3, 7, 16)), ((0, 3, 0), (4, 7, 21)))
+OTHER_ROWS = 14
+TO_BEFORE, TO_AFTER = (0, 18), (8, 26)
 LINES = 32
 COUNT_ROW, PATTERN_ROW, RHS_ROW, BETA_ROW = 0, 1, 2, 4
 SPARE = 6
 
 
-def table_row(table, r, entry):
-    return ((table * ROWS + r) * 16 + entry) * LAYERS
+def table_line(table, r, entry):
+    return ((table * ROWS + r) * 16 + entry) * 2
 
 
 def iota(shape, dim):
@@ -84,8 +87,9 @@
             eye = 1.0 if cp % 5 == 0 else 0.0
             for t, table in enumerate((inv, diag)):
                 values = jnp.where(actives[r], table[cp, :, r, :], eye)
-                at = table_row(t, r, cp)
-                folded[at : at + LAYERS, :] = values
+                for m in range(3):
+                    at = m * 128 + table_line(t, r, cp)
+                    folded[at : at + 2, :] = values[2 * m : 2 * m + 2]
     others[...] = jnp.zeros(others.shape, F32)
     for r in range(ROWS):
         row = slice(r, r + 1)
@@ -99,12 +103,17 @@
         at = slice(part * 128, part * 128 + 128)
         moved = [pltpu.roll(others[:, at], 6 - 2 * m, 1) for m in range(3)] + [others[:, at]]
         tiles = jnp.concatenate(moved, axis=0).T
-        chunks[part * SLOTS : part * SLOTS + SLOTS, 18:26, :] = tiles.reshape(SLOTS, 8, 128)
+        targets = slice(part * SLOTS, part * SLOTS + SLOTS)
+        rows = slice(OTHER_ROWS, OTHER_ROWS + 2)
+        chunks[targets, rows, :] = tiles.reshape(SLOTS, 8, 128)[:, 6:8]
     for part in range(2):
         for m in range(3):
             tiles = folded[m * 128 : m * 128 + 128, part * 128 : part * 128 + 128].T
-            at = slice(part * SLOTS, part * SLOTS + SLOTS)
-            chunks[at, m * 8 : m * 8 + 8, :] = tiles.reshape(SLOTS, 8, 128)
+            tiles = tiles.reshape(SLOTS, 8, 128)
+            targets = slice(part * SLOTS, part * SLOTS + SLOTS)
+            for first, last, row in RUNS[m]:
+                rows = slice(row, row + last - first + 1)
+                chunks[targets, rows, :] = tiles[:, first : last + 1]
     turn = lax.axis_index("gy") % 4
     for device in range(2 * SLOTS):
         chunk = pick(turn, [order.index(device) for order in ORDERS])
@@ -295,23 +304,44 @@
             target[at + c] = jnp.zeros((4, 8, 128), F32)
 
 
-def unpack(block, j, inv, diag, vis, small, turned_rows):
+def unpack(block, part, j, inv, diag, vis, small, turned_rows):
     sub = iota((8, 128), 0)
     pair = iota((LINES, 128), 1) % CHUNK // 2
+    size = part[1] - part[0]
+    last_start = 2 * SLOTS * size - 8
+
+    def eight(start):
+        if start < 0:
+            return pltpu.roll(block[pl.ds(0, 8), :], -start, 0)
+        if start > last_start:
+            return pltpu.roll(block[pl.ds(last_start, 8), :], 8 + last_start - start, 0)
+        return block[pl.ds(start, 8), :]
+
     for half in range(2):
-
-        def rows_at(row):
-            at = [(half * SLOTS + s) * CHUNK_ROWS + row for s in range(SLOTS)]
-            return jnp.concatenate([block[pl.ds(k, 8), :] for k in at], axis=0).T
-
+        bases = [(half * SLOTS + s) * size - part[0] for s in range(SLOTS)]
         for m in range(3):
-            turned_rows[m * 128 : m * 128 + 128, :] = rows_at(m * 8)
+            tiles = [jnp.zeros((8, 128), F32)] * SLOTS
+            for first, last, row in RUNS[m]:
+                from_row, to_row = max(row, part[0]), min(row + last - first, part[1] - 1)
+                if from_row > to_row:
+                    continue
+                keep = (sub >= from_row - row + first) & (sub <= to_row - row + first)
+                tiles = [
+                    jnp.where(keep, eight(base + row - first), tile)
+                    for base, tile in zip(bases, tiles)
+                ]
+            turned_rows[m * 128 : m * 128 + 128, :] = jnp.concatenate(tiles, axis=0).T
         for r in range(ROWS):
             for t, target in enumerate((inv, diag)):
                 for cp in range(16):
-                    tile = turned_rows[pl.ds(table_row(t, r, cp), 8), :]
-                    target[j * 16 + cp, half * 2 + r] = jnp.where(sub < LAYERS, tile, 0.0)
-        others = rows_at(18)
+                    line = table_line(t, r, cp)
+                    tile = jnp.zeros((8, 128), F32)
+                    for m in range(3):
+                        layers = turned_rows[pl.ds(m * 128 + line - 2 * m, 8), :]
+                        tile = jnp.where(sub // 2 == m, layers, tile)
+                    target[j * 16 + cp, half * 2 + r] = tile
+        tiles = [eight(base + OTHER_ROWS - 6) for base in bases]
+        others = jnp.concatenate(tiles, axis=0).T
         lines = others[3 * LINES :]
         for m in range(3):
             moved = pltpu.roll(others[m * LINES : (m + 1) * LINES], (2 * m - 6) % 128, 1)
@@ -328,8 +358,9 @@
     gx, gy = lax.axis_index("gx"), lax.axis_index("gy")
     nx, ny = lax.axis_size("gx"), lax.axis_size("gy")
     chunk = chunk_of(gy % 4, gx)
-    for j, block in enumerate((low, mine, high)):
-        unpack(block, j, inv, diag, vis, small, turned_rows)
+    parts = ((low, TO_AFTER), (mine, (0, CHUNK_ROWS)), (high, TO_BEFORE))
+    for j, (block, part) in enumerate(parts):
+        unpack(block, part, j, inv, diag, vis, small, turned_rows)
     for c in range(4):
         for field in (carried, carried_on):
             field[c] = jnp.zeros((4, 8, 128), F32)
@@ -537,9 +568,11 @@
     )
     sent = sent.reshape(n_gx, CHUNK_ROWS // 2, 2, 128)
     mine = lax.all_to_all(sent, "gx", 0, 0, tiled=True)
-    low = lax.ppermute(mine, ("gx", "gy"), neighbour_pairs(1))
-    high = lax.ppermute(mine, ("gx", "gy"), neighbour_pairs(-1))
-    blocks = [x.reshape(n_gx * CHUNK_ROWS, 128) for x in (low, mine, high)]
+    to_after = mine[:, TO_AFTER[0] // 2 : TO_AFTER[1] // 2]
+    to_before = mine[:, TO_BEFORE[0] // 2 : TO_BEFORE[1] // 2]
+    low = lax.ppermute(to_after, ("gx", "gy"), neighbour_pairs(1))
+    high = lax.ppermute(to_before, ("gx", "gy"), neighbour_pairs(-1))
+    blocks = [x.reshape(-1, 128) for x in (low, mine, high)]
 
     def field(count):
         return pltpu.VMEM((count, 4, 8, 128), F32)

time: 85.5 us -> 84.4 us (0.987)
  starting transfers between devices: 6.48 us -> 5.28 us
    all_to_all x1, blocking collectives: 22.4 us -> 20.9 us  [per_device(): lines = lax.all_to_all(lines, 'gy', 0, 0, tiled=True)]
    all_to_all x1, blocking collectives: 16.6 us -> 18.1 us  [per_device(): block = lax.all_to_all(back, 'gx', 0, 0, tiled=True)]
    ppermute x2, starting transfers between devices: 6.48 us -> 5.28 us  [the longest x1 3.36 us: per_device(): high = lax.ppermute(to_before, ('gx', 'gy'), neighbour_pairs(-1))]
where the time goes in v7:
time: 84.4 us; the launch traced here: 84 us
  blocking collectives  63.4 us (75%)
  Pallas kernels  9.28 us (11%)
  starting transfers between devices  5.28 us (6%)
  waiting for transfers between devices  5.08 us (6%)
    all_to_all x1, blocking collectives, per_device(): mine = lax.all_to_all(sent, 'gx', 0, 0, tiled=True)  24.4 us
    all_to_all x1, blocking collectives, per_device(): lines = lax.all_to_all(lines, 'gy', 0, 0, tiled=True)  20.9 us
    all_to_all x1, blocking collectives, per_device(): block = lax.all_to_all(back, 'gx', 0, 0, tiled=True)  18.1 us
    pallas_call x4, Pallas kernels, call(): pl.pallas_call(kernel, out_shape=[jax.ShapeDtypeStruct(shape, F32) for sh...  9.28 us
    ppermute x1, starting transfers between devices, per_device(): high = lax.ppermute(to_before, ('gx', 'gy'), neighbour_pairs(-1))  3.36 us
    ppermute x1, waiting for transfers between devices, per_device(): high = lax.ppermute(to_before, ('gx', 'gy'), neighbour_pairs(-1))  3.14 us
    ppermute x1, waiting for transfers between devices, per_device(): low = lax.ppermute(to_after, ('gx', 'gy'), neighbour_pairs(1))  1.94 us
    ppermute x1, starting transfers between devices, per_device(): low = lax.ppermute(to_after, ('gx', 'gy'), neighbour_pairs(1))  1.92 us
  transfers between devices with their start and end apart: 2, of which 2 were waited for; matrix products, arithmetic and copies ran while one was open for 0% of the time, Pallas kernels for 0%

profile of v7, /device:TPU:1, one launch (start us, length us, event | category | flops | bytes accessed | tf_op | source)
XLA Modules:
  0.0 84.0 jit_solution(12233201480505656164)
XLA Ops:
  0.6 2.4 %pack_tables.1 = f32[832,128]{1,0:T(8,128)} custom-call(f32[16,6,2,256]{3,2,1,0:T(2,128)} %bitcast.16, f32[16,6,2,256]{3,2,1,0:T(2,128)} %bitcast.17, f32[6,2,256]{2,1,0:T(2,128)} %visc_in.1, s32[2,256]{1,0:T(2,128)} %count_in.1, s32[2,256]{1,0:T(2,128)} %grounded.1, s32[2,256]{1,0:T(2,128)} %pattern_in.1, f32[2,256]{1,0:T(2,128)} %beta_in.1, f32[2,2,256]{2,1,0:T(2,128)} %vel.1), custom_call_target="tpu_custom_call" | custom-call | tf_op jit(solution)/shard_map/pack_tables/pallas_call | solution.py:514
  3.0 24.4 %all_to_all.21 = f32[32,13,2,128]{3,2,1,0:T(2,128)S(1)} all-to-all(f32[32,13,2,128]{3,2,1,0:T(2,128)} %bitcast.15), channel_id=1, replica_groups=mesh['gx'=32,'gy'=16] {'gx'}, dimensions={0} | all-to-all | bytes 851968 | tf_op jit(solution)/shard_map/all_to_all | solution.py:570
  27.4 0.0 copy-start.2
  27.4 0.1 fusion
  27.5 1.9 %collective-permute-start = (f32[32,9,2,128]{3,2,1,0:T(2,128)S(1)}, f32[32,9,2,128]{3,2,1,0:T(2,128)S(1)}, u32[]{:S(2)}, u32[]{:S(2)}) collective-permute-start(f32[32,9,2,128]{3,2,1,0:T(2,128)S(1)} %get-tuple-element.3), channel_id=1, source_target_pairs={{16,464},{464,400},{400,336},{336,320},{320,368},{368,352},{352,28... | collective-permute-start | bytes 884744 | tf_op jit(solution)/shard_map/ppermute | solution.py:573
  29.4 3.4 %collective-permute-start.1 = (f32[32,9,2,128]{3,2,1,0:T(2,128)S(1)}, f32[32,9,2,128]{3,2,1,0:T(2,128)S(1)}, u32[]{:S(2)}, u32[]{:S(2)}) collective-permute-start(f32[32,9,2,128]{3,2,1,0:T(2,128)S(1)} %get-tuple-element.2), channel_id=1, source_target_pairs={{464,16},{400,464},{336,400},{320,336},{368,320},{352,368},{288,35... | collective-permute-start | bytes 884744 | tf_op jit(solution)/shard_map/ppermute | solution.py:574
  32.8 0.0 copy-done.2
  32.8 0.1 copy.13
  32.9 0.1 reshape.27.coupling
  33.0 1.9 %collective-permute-done = f32[32,9,2,128]{3,2,1,0:T(2,128)S(1)} collective-permute-done((f32[32,9,2,128]{3,2,1,0:T(2,128)S(1)}, f32[32,9,2,128]{3,2,1,0:T(2,128)S(1)}, u32[]{:S(2)}, u32[]{:S(2)}) %collective-permute-start) | collective-permute-done | bytes 294944 | tf_op jit(solution)/shard_map/ppermute | solution.py:573
  35.0 3.1 %collective-permute-done.1 = f32[32,9,2,128]{3,2,1,0:T(2,128)S(1)} collective-permute-done((f32[32,9,2,128]{3,2,1,0:T(2,128)S(1)}, f32[32,9,2,128]{3,2,1,0:T(2,128)S(1)}, u32[]{:S(2)}, u32[]{:S(2)}) %collective-permute-start.1) | collective-permute-done | bytes 294944 | tf_op jit(solution)/shard_map/ppermute | solution.py:574
  38.1 6.0 %solve_both.1 = f32[32,2,8,128]{3,2,1,0:T(8,128)S(1)} custom-call(f32[96]{0:T(128)S(1)} %reshape.27.coupling, f32[576,128]{1,0:T(8,128)S(1)} %bitcast.11, f32[832,128]{1,0:T(8,128)S(1)} %bitcast.10, f32[576,128]{1,0:T(8,128)S(1)} %bitcast.12), custom_call_target="tpu_custom_call" | custom-call | tf_op jit(solution)/shard_map/solve_both/pallas_call | solution.py:514
  44.1 18.1 %all_to_all.22.block = f32[32,2,8,128]{3,2,1,0:T(8,128)S(1)} all-to-all(f32[32,2,8,128]{3,2,1,0:T(8,128)S(1)} %solve_both.1), channel_id=1, replica_groups=mesh['gx'=32,'gy'=16] {'gx'}, dimensions={0} | all-to-all | bytes 524288 | tf_op jit(solution)/shard_map/all_to_all | solution.py:605
  62.2 0.0 copy-start
  62.2 0.0 copy-start.1
  62.2 0.1 sum_gx.1
  62.3 20.9 %all_to_all.23 = f32[16,1,128]{2,1,0:T(1,128)S(1)} all-to-all(f32[16,1,128]{2,1,0:T(1,128)S(1)} %bitcast.14), channel_id=1, replica_groups=mesh['gx'=32,'gy'=16] {'gy'}, dimensions={0} | all-to-all | bytes 16384 | tf_op jit(solution)/shard_map/all_to_all | solution.py:607
  83.2 0.0 copy-done
  83.2 0.0 copy-done.1
  83.2 0.8 combine.1
Async XLA Ops:
  27.4 5.4 %copy-start.2 = (f32[6,4,4]{0,2,1:T(4,128)S(1)}, f32[6,4,4]{0,2,1:T(4,128)}, u32[]{:S(2)}) copy-start(f32[6,4,4]{0,2,1:T(4,128)} %param.12) | copy-start | bytes 1156
  27.5 7.5 %collective-permute-start = (f32[32,9,2,128]{3,2,1,0:T(2,128)S(1)}, f32[32,9,2,128]{3,2,1,0:T(2,128)S(1)}, u32[]{:S(2)}, u32[]{:S(2)}) collective-permute-start(f32[32,9,2,128]{3,2,1,0:T(2,128)S(1)} %get-tuple-element.3), channel_id=1, source_target_pairs={{16,464},{464,400},{400,336},{336,320},{320,368},{368,352},{352,28... | collective-permute-start | bytes 884744 | tf_op jit(solution)/shard_map/ppermute | solution.py:573
  29.4 8.7 %collective-permute-start.1 = (f32[32,9,2,128]{3,2,1,0:T(2,128)S(1)}, f32[32,9,2,128]{3,2,1,0:T(2,128)S(1)}, u32[]{:S(2)}, u32[]{:S(2)}) collective-permute-start(f32[32,9,2,128]{3,2,1,0:T(2,128)S(1)} %get-tuple-element.2), channel_id=1, source_target_pairs={{464,16},{400,464},{336,400},{320,336},{368,320},{352,368},{288,35... | collective-permute-start | bytes 884744 | tf_op jit(solution)/shard_map/ppermute | solution.py:574
  62.2 21.0 %copy-start = (f32[2,2,256]{2,1,0:T(2,128)S(1)}, f32[2,2,256]{2,1,0:T(2,128)}, u32[]{:S(2)}) copy-start(f32[2,2,256]{2,1,0:T(2,128)} %vel.1) | copy-start | bytes 12292
  62.2 21.0 %copy-start.1 = (s32[2,256]{1,0:T(2,128)S(1)}, s32[2,256]{1,0:T(2,128)}, u32[]{:S(2)}) copy-start(s32[2,256]{1,0:T(2,128)} %grounded.1) | copy-start | bytes 6148

commit v8 on v7

--- a/solution.py
+++ b/solution.py
@@ -131,16 +131,48 @@
     return out
 
 
-def coupled(coupling, direction, values, transposed, sums):
+def split(values):
+    parts = []
+    for _ in range(3):
+        parts.append(values.astype(jnp.bfloat16))
+        values = values - parts[-1].astype(F32)
+    return parts
+
+
+PASSES = ((0, 0), (0, 1), (1, 0), (0, 2), (1, 1), (2, 0))
+GROUPS = 5
+
+
+def coupling_matrix(coupling, transposed):
+    shape = (8, 32)
+    source, layer = iota(shape, 1) // 8, iota(shape, 1) % 8 - iota(shape, 0)
+
+    def line(direction, c):
+        if transposed:
+            entries = [coupling[OPPOSITE[direction] * 16 + k * 4 + c] for k in range(4)]
+        else:
+            entries = [coupling[direction * 16 + c * 4 + k] for k in range(4)]
+        low = jnp.where(source == 0, entries[0], entries[1])
+        high = jnp.where(source == 2, entries[2], entries[3])
+        return jnp.where(source < 2, low, high)
+
+    lines = []
     for c in range(4):
-        for k in range(4):
-            if transposed:
-                factor = coupling[OPPOSITE[direction] * 16 + k * 4 + c]
-            else:
-                factor = coupling[direction * 16 + c * 4 + k]
-            entry = factor * values[k]
-            sums[c] = entry if sums[c] is None else sums[c] + entry
-    return sums
+        below = jnp.where(layer == -1, line(1, c), 0.0)
+        lines.append(jnp.where(layer == 1, line(0, c), below))
+    for direction in range(2, 6):
+        lines += [jnp.where(layer == 0, line(direction, c), 0.0) for c in range(4)]
+    parts = split(jnp.concatenate(lines, axis=0))
+    return jnp.concatenate([parts[a] for a, _ in PASSES], axis=1)
+
+
+def products(matrix, tiles, start=0):
+    field = jnp.concatenate(
+        [jnp.concatenate([tiles[c][i] for c in range(4)], axis=0) for i in range(4)], axis=1
+    )
+    parts = split(field)
+    rows = jnp.concatenate([parts[b] for _, b in PASSES], axis=0)
+    return jnp.dot(matrix[start:], rows, preferred_element_type=F32)
 
 
 def x_plus(v):
@@ -169,26 +201,30 @@
     return jnp.where(column > 0, pltpu.roll(v, 1, 2), pltpu.roll(before, 128 - CHUNK + 1, 2))
 
 
-def stencil(field, base, after, before, coupling, transposed, kappa):
-    here = [field[base + c] for c in range(4)]
-    sums = [None] * 4
-    sums = coupled(coupling, 0, [pltpu.roll(h, 7, 1) for h in here], transposed, sums)
-    sums = coupled(coupling, 1, [pltpu.roll(h, 1, 1) for h in here], transposed, sums)
-
-    def weighted(direction, tiles):
-        if kappa is None:
-            return tiles
-        weight = kappa(direction)
-        return [weight * t for t in tiles]
-
-    moved = weighted(0, [x_plus(h) for h in here])
-    sums = coupled(coupling, 2, moved, transposed, sums)
-    moved = weighted(1, [x_minus(h) for h in here])
-    sums = coupled(coupling, 3, moved, transposed, sums)
-    moved = weighted(2, [y_plus(here[c], field[after + c]) for c in range(4)])
-    sums = coupled(coupling, 4, moved, transposed, sums)
-    moved = weighted(3, [y_minus(here[c], field[before + c]) for c in range(4)])
-    return coupled(coupling, 5, moved, transposed, sums)
+def stencil(field, place, kappa):
+    at, after, before = place
+
+    def group(block, g):
+        return [
+            jnp.stack(
+                [field[block, (g * 4 + c) * 8 : (g * 4 + c) * 8 + 8, pl.ds(i * 128, 128)] for i in range(4)]
+            )
+            for c in range(4)
+        ]
+
+    moved = [
+        [x_plus(t) for t in group(at, 1)],
+        [x_minus(t) for t in group(at, 2)],
+        [y_plus(t, n) for t, n in zip(group(at, 3), group(after, 3))],
+        [y_minus(t, n) for t, n in zip(group(at, 4), group(before, 4))],
+    ]
+    sums = group(at, 0)
+    for direction, tiles in enumerate(moved):
+        if kappa is not None:
+            weight = kappa(direction)
+            tiles = [weight * t for t in tiles]
+        sums = [a + b for a, b in zip(sums, tiles)]
+    return sums
 
 
 class Forward:
@@ -198,7 +234,7 @@
         return i
 
     def place(i):
-        return (i + 1) * 4, (i + 2) * 4, i * 4
+        return i + 1, i + 2, i
 
 
 class Adjoint:
@@ -208,8 +244,8 @@
         return (i % 2) * 2 + 1
 
     def place(i):
-        other = (i + 1 - 2 * (i % 2)) * 4
-        return i * 4, other, other
+        other = i + 1 - 2 * (i % 2)
+        return i, other, other
 
 
 def run_all(count, step):
@@ -218,17 +254,19 @@
 
 
 def sweep(kind, res, first, carried, carried_on, update, image, own_only, tables):
-    inv, diag, vis, kappa, coupling = tables
+    inv, diag, vis, kappa, matrices = tables
     transposed = kind.transposed
+    matrix = matrices[int(transposed)]
 
     def initial(i, carry):
         j = kind.block(i)
         at = kind.place(i)[0]
         nu = vis[j]
         values = [res[i * 4 + c] for c in range(4)]
-        for c, y in enumerate(block_times(inv, j * 16, values, transposed)):
-            first[i * 4 + c] = y
-            carried[at + c] = nu * y
+        y0 = block_times(inv, j * 16, values, transposed)
+        for c in range(4):
+            first[i * 4 + c] = y0[c]
+        carried[at] = products(matrix, [nu * y for y in y0])
         return carry
 
     run_all(kind.count, initial)
@@ -236,17 +274,17 @@
     def correct(i, carry):
         j = kind.block(i)
         nu = vis[j]
-        sums = stencil(
-            carried, *kind.place(i), coupling, transposed, lambda d: kappa[j * 4 + d]
-        )
+        sums = stencil(carried, kind.place(i), lambda d: kappa[j * 4 + d])
         y0 = [first[i * 4 + c] for c in range(4)]
         own = block_times(diag, j * 16, y0, transposed)
         rest = [res[i * 4 + c] - own[c] + nu * sums[c] for c in range(4)]
         at = kind.place(i)[0]
-        for c, y in enumerate(block_times(inv, j * 16, rest, transposed)):
-            z = y0[c] + y
-            update[i * 4 + c] = z
-            carried_on[at + c] = nu * z
+        y = block_times(inv, j * 16, rest, transposed)
+        z = [a + b for a, b in zip(y0, y)]
+        for c in range(4):
+            update[i * 4 + c] = z[c]
+        start = 3 * 32 if own_only and j != OWN else 0
+        carried_on[at, start:] = products(matrix, [nu * t for t in z], start)
         return carry
 
     run_all(kind.count, correct)
@@ -255,7 +293,7 @@
         if own_only:
             i = i * 2 if kind is Adjoint else 1
         j = kind.block(i)
-        sums = stencil(carried_on, *kind.place(i), coupling, transposed, None)
+        sums = stencil(carried_on, kind.place(i), None)
         values = [update[i * 4 + c] for c in range(4)]
         own = block_times(diag, j * 16, values, transposed)
         nu = vis[j]
@@ -354,6 +392,7 @@
 def solve_kernel(
     coupling, low, mine, high, message,
     inv, diag, vis, small, kappa, spread, res, res_two, first, carried, carried_on, update, image, last, start, turned_rows,
+    matrix_forward, matrix_adjoint,
 ):
     gx, gy = lax.axis_index("gx"), lax.axis_index("gy")
     nx, ny = lax.axis_size("gx"), lax.axis_size("gy")
@@ -361,10 +400,11 @@
     parts = ((low, TO_AFTER), (mine, (0, CHUNK_ROWS)), (high, TO_BEFORE))
     for j, (block, part) in enumerate(parts):
         unpack(block, part, j, inv, diag, vis, small, turned_rows)
-    for c in range(4):
-        for field in (carried, carried_on):
-            field[c] = jnp.zeros((4, 8, 128), F32)
-            field[16 + c] = jnp.zeros((4, 8, 128), F32)
+    for field in (carried, carried_on):
+        for empty in (0, 4):
+            field[empty] = jnp.zeros(field.shape[1:], F32)
+    for transposed, matrix in enumerate((matrix_forward, matrix_adjoint)):
+        matrix[...] = coupling_matrix(coupling, transposed)
 
     shape = (4, 8, 128)
     layer = iota(shape, 1)
@@ -405,7 +445,7 @@
         for k in range(size):
             table[NEAR * size + k] = merged(table[2 * size + k], table[k])
 
-    tables = (inv, diag, vis, kappa, coupling)
+    tables = (inv, diag, vis, kappa, (matrix_forward, matrix_adjoint))
     sweep(Forward, res, first, carried, carried_on, update, image, False, tables)
     layer_sums(update, spread, res_two, 0)
     for t in range(12):
@@ -593,14 +633,15 @@
             field(12),
             field(16),
             field(16),
-            field(20),
-            field(20),
+            pltpu.VMEM((5, GROUPS * 32, 512), F32),
+            pltpu.VMEM((5, GROUPS * 32, 512), F32),
             field(16),
             field(16),
             field(16),
             field(8),
             pltpu.VMEM((392, 128), F32),
-        ],
+        ]
+        + [pltpu.VMEM((GROUPS * 32, len(PASSES) * 32), jnp.bfloat16)] * 2,
     )
     block = lax.all_to_all(back, "gx", 0, 0, tiled=True)
     (lines,) = call(gather_kernel, "sum_gx", [block], [VMEM], [(n_gy, 128)])

time: 84.4 us -> 83.8 us (level)
  no operation moved by 1% of the time
where the time goes in v8:
time: 83.8 us; the launch traced here: 83.4 us
  blocking collectives  63.4 us (76%)
  Pallas kernels  8.62 us (10%)
  starting transfers between devices  5.28 us (6%)
  waiting for transfers between devices  5.08 us (6%)
    all_to_all x1, blocking collectives, per_device(): mine = lax.all_to_all(sent, 'gx', 0, 0, tiled=True)  24.4 us
    all_to_all x1, blocking collectives, per_device(): lines = lax.all_to_all(lines, 'gy', 0, 0, tiled=True)  20.9 us
    all_to_all x1, blocking collectives, per_device(): block = lax.all_to_all(back, 'gx', 0, 0, tiled=True)  18.1 us
    pallas_call x4, Pallas kernels, call(): pl.pallas_call(kernel, out_shape=[jax.ShapeDtypeStruct(shape, F32) for sh...  8.62 us
    ppermute x1, starting transfers between devices, per_device(): high = lax.ppermute(to_before, ('gx', 'gy'), neighbour_pairs(-1))  3.36 us
    ppermute x1, waiting for transfers between devices, per_device(): high = lax.ppermute(to_before, ('gx', 'gy'), neighbour_pairs(-1))  3.14 us
    ppermute x1, waiting for transfers between devices, per_device(): low = lax.ppermute(to_after, ('gx', 'gy'), neighbour_pairs(1))  1.94 us
    ppermute x1, starting transfers between devices, per_device(): low = lax.ppermute(to_after, ('gx', 'gy'), neighbour_pairs(1))  1.92 us
  transfers between devices with their start and end apart: 2, of which 2 were waited for; matrix products, arithmetic and copies ran while one was open for 0% of the time, Pallas kernels for 0%

profile of v8, /device:TPU:1, one launch (start us, length us, event | category | flops | bytes accessed | tf_op | source)
XLA Modules:
  0.0 83.4 jit_solution(12509639900949246333)
XLA Ops:
  0.6 2.4 %pack_tables.1 = f32[832,128]{1,0:T(8,128)} custom-call(f32[16,6,2,256]{3,2,1,0:T(2,128)} %bitcast.16, f32[16,6,2,256]{3,2,1,0:T(2,128)} %bitcast.17, f32[6,2,256]{2,1,0:T(2,128)} %visc_in.1, s32[2,256]{1,0:T(2,128)} %count_in.1, s32[2,256]{1,0:T(2,128)} %grounded.1, s32[2,256]{1,0:T(2,128)} %pattern_in.1, f32[2,256]{1,0:T(2,128)} %beta_in.1, f32[2,2,256]{2,1,0:T(2,128)} %vel.1), custom_call_target="tpu_custom_call" | custom-call | tf_op jit(solution)/shard_map/pack_tables/pallas_call | solution.py:554
  3.0 24.4 %all_to_all.21 = f32[32,13,2,128]{3,2,1,0:T(2,128)S(1)} all-to-all(f32[32,13,2,128]{3,2,1,0:T(2,128)} %bitcast.15), channel_id=1, replica_groups=mesh['gx'=32,'gy'=16] {'gx'}, dimensions={0} | all-to-all | bytes 851968 | tf_op jit(solution)/shard_map/all_to_all | solution.py:610
  27.4 0.0 copy-start.2
  27.4 0.1 fusion
  27.5 1.9 %collective-permute-start = (f32[32,9,2,128]{3,2,1,0:T(2,128)S(1)}, f32[32,9,2,128]{3,2,1,0:T(2,128)S(1)}, u32[]{:S(2)}, u32[]{:S(2)}) collective-permute-start(f32[32,9,2,128]{3,2,1,0:T(2,128)S(1)} %get-tuple-element.3), channel_id=1, source_target_pairs={{16,464},{464,400},{400,336},{336,320},{320,368},{368,352},{352,28... | collective-permute-start | bytes 884744 | tf_op jit(solution)/shard_map/ppermute | solution.py:613
  29.4 3.4 %collective-permute-start.1 = (f32[32,9,2,128]{3,2,1,0:T(2,128)S(1)}, f32[32,9,2,128]{3,2,1,0:T(2,128)S(1)}, u32[]{:S(2)}, u32[]{:S(2)}) collective-permute-start(f32[32,9,2,128]{3,2,1,0:T(2,128)S(1)} %get-tuple-element.2), channel_id=1, source_target_pairs={{464,16},{400,464},{336,400},{320,336},{368,320},{352,368},{288,35... | collective-permute-start | bytes 884744 | tf_op jit(solution)/shard_map/ppermute | solution.py:614
  32.8 0.0 copy-done.2
  32.8 0.1 copy.13
  32.9 0.1 reshape.27.coupling
  33.0 1.9 %collective-permute-done = f32[32,9,2,128]{3,2,1,0:T(2,128)S(1)} collective-permute-done((f32[32,9,2,128]{3,2,1,0:T(2,128)S(1)}, f32[32,9,2,128]{3,2,1,0:T(2,128)S(1)}, u32[]{:S(2)}, u32[]{:S(2)}) %collective-permute-start) | collective-permute-done | bytes 294944 | tf_op jit(solution)/shard_map/ppermute | solution.py:613
  35.0 3.1 %collective-permute-done.1 = f32[32,9,2,128]{3,2,1,0:T(2,128)S(1)} collective-permute-done((f32[32,9,2,128]{3,2,1,0:T(2,128)S(1)}, f32[32,9,2,128]{3,2,1,0:T(2,128)S(1)}, u32[]{:S(2)}, u32[]{:S(2)}) %collective-permute-start.1) | collective-permute-done | bytes 294944 | tf_op jit(solution)/shard_map/ppermute | solution.py:614
  38.1 5.3 %solve_both.1 = f32[32,2,8,128]{3,2,1,0:T(8,128)S(1)} custom-call(f32[96]{0:T(128)S(1)} %reshape.27.coupling, f32[576,128]{1,0:T(8,128)S(1)} %bitcast.11, f32[832,128]{1,0:T(8,128)S(1)} %bitcast.10, f32[576,128]{1,0:T(8,128)S(1)} %bitcast.12), custom_call_target="tpu_custom_call" | custom-call | tf_op jit(solution)/shard_map/solve_both/pallas_call | solution.py:554
  43.4 18.1 %all_to_all.22.block = f32[32,2,8,128]{3,2,1,0:T(8,128)S(1)} all-to-all(f32[32,2,8,128]{3,2,1,0:T(8,128)S(1)} %solve_both.1), channel_id=1, replica_groups=mesh['gx'=32,'gy'=16] {'gx'}, dimensions={0} | all-to-all | bytes 524288 | tf_op jit(solution)/shard_map/all_to_all | solution.py:646
  61.6 0.0 copy-start
  61.6 0.0 copy-start.1
  61.6 0.1 sum_gx.1
  61.7 20.9 %all_to_all.23 = f32[16,1,128]{2,1,0:T(1,128)S(1)} all-to-all(f32[16,1,128]{2,1,0:T(1,128)S(1)} %bitcast.14), channel_id=1, replica_groups=mesh['gx'=32,'gy'=16] {'gy'}, dimensions={0} | all-to-all | bytes 16384 | tf_op jit(solution)/shard_map/all_to_all | solution.py:648
  82.6 0.0 copy-done
  82.6 0.0 copy-done.1
  82.6 0.8 combine.1
Async XLA Ops:
  27.4 5.4 %copy-start.2 = (f32[6,4,4]{0,2,1:T(4,128)S(1)}, f32[6,4,4]{0,2,1:T(4,128)}, u32[]{:S(2)}) copy-start(f32[6,4,4]{0,2,1:T(4,128)} %param.12) | copy-start | bytes 1156
  27.5 7.5 %collective-permute-start = (f32[32,9,2,128]{3,2,1,0:T(2,128)S(1)}, f32[32,9,2,128]{3,2,1,0:T(2,128)S(1)}, u32[]{:S(2)}, u32[]{:S(2)}) collective-permute-start(f32[32,9,2,128]{3,2,1,0:T(2,128)S(1)} %get-tuple-element.3), channel_id=1, source_target_pairs={{16,464},{464,400},{400,336},{336,320},{320,368},{368,352},{352,28... | collective-permute-start | bytes 884744 | tf_op jit(solution)/shard_map/ppermute | solution.py:613
  29.4 8.7 %collective-permute-start.1 = (f32[32,9,2,128]{3,2,1,0:T(2,128)S(1)}, f32[32,9,2,128]{3,2,1,0:T(2,128)S(1)}, u32[]{:S(2)}, u32[]{:S(2)}) collective-permute-start(f32[32,9,2,128]{3,2,1,0:T(2,128)S(1)} %get-tuple-element.2), channel_id=1, source_target_pairs={{464,16},{400,464},{336,400},{320,336},{368,320},{352,368},{288,35... | collective-permute-start | bytes 884744 | tf_op jit(solution)/shard_map/ppermute | solution.py:614
  61.6 21.0 %copy-start = (f32[2,2,256]{2,1,0:T(2,128)S(1)}, f32[2,2,256]{2,1,0:T(2,128)}, u32[]{:S(2)}) copy-start(f32[2,2,256]{2,1,0:T(2,128)} %vel.1) | copy-start | bytes 12292
  61.6 21.0 %copy-start.1 = (s32[2,256]{1,0:T(2,128)S(1)}, s32[2,256]{1,0:T(2,128)}, u32[]{:S(2)}) copy-start(s32[2,256]{1,0:T(2,128)} %grounded.1) | copy-start | bytes 6148

commit v9 on v8

--- a/solution.py
+++ b/solution.py
@@ -120,11 +120,11 @@
         message[device * CHUNK_ROWS : (device + 1) * CHUNK_ROWS, :] = chunks[chunk, 0:CHUNK_ROWS, :]
 
 
-def block_times(table, base, values, transposed):
+def block_times(table, base, values, transposed, used=4):
     out = []
     for c in range(4):
         total = None
-        for k in range(4):
+        for k in range(used):
             entry = table[base + (k * 4 + c if transposed else c * 4 + k)] * values[k]
             total = entry if total is None else total + entry
         out.append(total)
@@ -257,13 +257,14 @@
     inv, diag, vis, kappa, matrices = tables
     transposed = kind.transposed
     matrix = matrices[int(transposed)]
+    from_top = not own_only
 
     def initial(i, carry):
         j = kind.block(i)
         at = kind.place(i)[0]
         nu = vis[j]
         values = [res[i * 4 + c] for c in range(4)]
-        y0 = block_times(inv, j * 16, values, transposed)
+        y0 = block_times(inv, j * 16, values, transposed, 2 if from_top else 4)
         for c in range(4):
             first[i * 4 + c] = y0[c]
         carried[at] = products(matrix, [nu * y for y in y0])
@@ -304,26 +305,21 @@
     run_all(kind.own if own_only else kind.count, apply)
 
 
-def dots_of(residual, image, last, at_of, pairs):
-    def own(ref, v):
-        return [ref[at_of(v) + c] for c in range(4)]
-
-    def dot(x, i, y, j):
-        part = None
-        for a, b in zip(own(x, i), own(y, j)):
-            part = a * b if part is None else part + a * b
-        return part
-
-    out = []
-    for x, y in ((image, image), (residual, image), (residual, last), (image, last), (last, last)):
-        for i, j in pairs:
-            part = dot(x, i, y, j)
-            if i != j:
-                part += part if x is y else dot(x, j, y, i)
-            tile = (part[0] + part[1]) + (part[2] + part[3])
-            line = jnp.sum(tile, axis=0, keepdims=True)
-            out.append(jnp.sum(line, axis=1, keepdims=True))
-    return out
+def dots_of(residual, image, last, at_of, vectors):
+    sums = None
+    for c in range(4):
+        e, q, p = [[ref[at_of(v) + c] for v in range(vectors)] for ref in (residual, image, last)]
+        parts = []
+        for x, y in ((q, q), (e, q), (e, p), (q, p), (p, p)):
+            parts.append(x[0] * y[0])
+            if vectors == 2:
+                mixed = x[0] * y[1]
+                parts.append(mixed + mixed if x is y else mixed + x[1] * y[0])
+                parts.append(x[1] * y[1])
+        parts = [(a[0] + a[1]) + (a[2] + a[3]) for a in parts]
+        sums = parts if sums is None else [a + b for a, b in zip(sums, parts)]
+    lines = [jnp.sum(tile, axis=0, keepdims=True) for tile in sums]
+    return [jnp.sum(line, axis=1, keepdims=True) for line in lines]
 
 
 def merged(after, before):
@@ -452,7 +448,7 @@
         res[t] = res[t] - image[t]
     sweep(Forward, res, first, carried, carried_on, update, last, True, tables)
     layer_sums(update, spread, res_two, 1)
-    dots = dots_of(res, image, last, lambda v: 4, ((0, 0),))
+    dots = dots_of(res, image, last, lambda v: 4, 1)
 
     sweep(Adjoint, res_two, first, carried, carried_on, update, image, False, tables)
     for v in range(2):
@@ -461,7 +457,7 @@
     for t in range(16):
         res_two[t] = res_two[t] - image[t]
     sweep(Adjoint, res_two, first, carried, carried_on, update, last, True, tables)
-    dots += dots_of(res_two, image, last, lambda v: v * 8, ((0, 0), (0, 1), (1, 1)))
+    dots += dots_of(res_two, image, last, lambda v: v * 8, 2)
 
     before, here, after = small[0], small[1], small[2]
     around = x_plus(here) + x_minus(here) + y_plus(here, after) + y_minus(here, before)

time: 83.8 us -> 83.7 us (level)
  no operation moved by 1% of the time
where the time goes in v9:
time: 83.7 us; the launch traced here: 83.4 us
  blocking collectives  63.4 us (76%)
  Pallas kernels  8.62 us (10%)
  starting transfers between devices  5.28 us (6%)
  waiting for transfers between devices  5.08 us (6%)
    all_to_all x1, blocking collectives, per_device(): mine = lax.all_to_all(sent, 'gx', 0, 0, tiled=True)  24.4 us
    all_to_all x1, blocking collectives, per_device(): lines = lax.all_to_all(lines, 'gy', 0, 0, tiled=True)  20.9 us
    all_to_all x1, blocking collectives, per_device(): block = lax.all_to_all(back, 'gx', 0, 0, tiled=True)  18.1 us
    pallas_call x4, Pallas kernels, call(): pl.pallas_call(kernel, out_shape=[jax.ShapeDtypeStruct(shape, F32) for sh...  8.62 us
    ppermute x1, starting transfers between devices, per_device(): high = lax.ppermute(to_before, ('gx', 'gy'), neighbour_pairs(-1))  3.36 us
    ppermute x1, waiting for transfers between devices, per_device(): high = lax.ppermute(to_before, ('gx', 'gy'), neighbour_pairs(-1))  3.14 us
    ppermute x1, waiting for transfers between devices, per_device(): low = lax.ppermute(to_after, ('gx', 'gy'), neighbour_pairs(1))  1.94 us
    ppermute x1, starting transfers between devices, per_device(): low = lax.ppermute(to_after, ('gx', 'gy'), neighbour_pairs(1))  1.92 us
  transfers between devices with their start and end apart: 2, of which 2 were waited for; matrix products, arithmetic and copies ran while one was open for 0% of the time, Pallas kernels for 0%

profile of v9, /device:TPU:1, one launch (start us, length us, event | category | flops | bytes accessed | tf_op | source)
XLA Modules:
  0.0 83.4 jit_solution(5107629109412050928)
XLA Ops:
  0.6 2.4 %pack_tables.1 = f32[832,128]{1,0:T(8,128)} custom-call(f32[16,6,2,256]{3,2,1,0:T(2,128)} %bitcast.16, f32[16,6,2,256]{3,2,1,0:T(2,128)} %bitcast.17, f32[6,2,256]{2,1,0:T(2,128)} %visc_in.1, s32[2,256]{1,0:T(2,128)} %count_in.1, s32[2,256]{1,0:T(2,128)} %grounded.1, s32[2,256]{1,0:T(2,128)} %pattern_in.1, f32[2,256]{1,0:T(2,128)} %beta_in.1, f32[2,2,256]{2,1,0:T(2,128)} %vel.1), custom_call_target="tpu_custom_call" | custom-call | tf_op jit(solution)/shard_map/pack_tables/pallas_call | solution.py:550
  3.0 24.4 %all_to_all.21 = f32[32,13,2,128]{3,2,1,0:T(2,128)S(1)} all-to-all(f32[32,13,2,128]{3,2,1,0:T(2,128)} %bitcast.15), channel_id=1, replica_groups=mesh['gx'=32,'gy'=16] {'gx'}, dimensions={0} | all-to-all | bytes 851968 | tf_op jit(solution)/shard_map/all_to_all | solution.py:606
  27.4 0.0 copy-start.2
  27.4 0.1 fusion
  27.5 1.9 %collective-permute-start = (f32[32,9,2,128]{3,2,1,0:T(2,128)S(1)}, f32[32,9,2,128]{3,2,1,0:T(2,128)S(1)}, u32[]{:S(2)}, u32[]{:S(2)}) collective-permute-start(f32[32,9,2,128]{3,2,1,0:T(2,128)S(1)} %get-tuple-element.3), channel_id=1, source_target_pairs={{16,464},{464,400},{400,336},{336,320},{320,368},{368,352},{352,28... | collective-permute-start | bytes 884744 | tf_op jit(solution)/shard_map/ppermute | solution.py:609
  29.4 3.4 %collective-permute-start.1 = (f32[32,9,2,128]{3,2,1,0:T(2,128)S(1)}, f32[32,9,2,128]{3,2,1,0:T(2,128)S(1)}, u32[]{:S(2)}, u32[]{:S(2)}) collective-permute-start(f32[32,9,2,128]{3,2,1,0:T(2,128)S(1)} %get-tuple-element.2), channel_id=1, source_target_pairs={{464,16},{400,464},{336,400},{320,336},{368,320},{352,368},{288,35... | collective-permute-start | bytes 884744 | tf_op jit(solution)/shard_map/ppermute | solution.py:610
  32.8 0.0 copy-done.2
  32.8 0.1 copy.13
  32.9 0.1 reshape.27.coupling
  33.0 1.9 %collective-permute-done = f32[32,9,2,128]{3,2,1,0:T(2,128)S(1)} collective-permute-done((f32[32,9,2,128]{3,2,1,0:T(2,128)S(1)}, f32[32,9,2,128]{3,2,1,0:T(2,128)S(1)}, u32[]{:S(2)}, u32[]{:S(2)}) %collective-permute-start) | collective-permute-done | bytes 294944 | tf_op jit(solution)/shard_map/ppermute | solution.py:609
  35.0 3.1 %collective-permute-done.1 = f32[32,9,2,128]{3,2,1,0:T(2,128)S(1)} collective-permute-done((f32[32,9,2,128]{3,2,1,0:T(2,128)S(1)}, f32[32,9,2,128]{3,2,1,0:T(2,128)S(1)}, u32[]{:S(2)}, u32[]{:S(2)}) %collective-permute-start.1) | collective-permute-done | bytes 294944 | tf_op jit(solution)/shard_map/ppermute | solution.py:610
  38.1 5.3 %solve_both.1 = f32[32,2,8,128]{3,2,1,0:T(8,128)S(1)} custom-call(f32[96]{0:T(128)S(1)} %reshape.27.coupling, f32[576,128]{1,0:T(8,128)S(1)} %bitcast.11, f32[832,128]{1,0:T(8,128)S(1)} %bitcast.10, f32[576,128]{1,0:T(8,128)S(1)} %bitcast.12), custom_call_target="tpu_custom_call" | custom-call | tf_op jit(solution)/shard_map/solve_both/pallas_call | solution.py:550
  43.4 18.1 %all_to_all.22.block = f32[32,2,8,128]{3,2,1,0:T(8,128)S(1)} all-to-all(f32[32,2,8,128]{3,2,1,0:T(8,128)S(1)} %solve_both.1), channel_id=1, replica_groups=mesh['gx'=32,'gy'=16] {'gx'}, dimensions={0} | all-to-all | bytes 524288 | tf_op jit(solution)/shard_map/all_to_all | solution.py:642
  61.6 0.0 copy-start
  61.6 0.0 copy-start.1
  61.6 0.1 sum_gx.1
  61.7 20.9 %all_to_all.23 = f32[16,1,128]{2,1,0:T(1,128)S(1)} all-to-all(f32[16,1,128]{2,1,0:T(1,128)S(1)} %bitcast.14), channel_id=1, replica_groups=mesh['gx'=32,'gy'=16] {'gy'}, dimensions={0} | all-to-all | bytes 16384 | tf_op jit(solution)/shard_map/all_to_all | solution.py:644
  82.5 0.0 copy-done
  82.5 0.0 copy-done.1
  82.5 0.8 combine.1
Async XLA Ops:
  27.4 5.4 %copy-start.2 = (f32[6,4,4]{0,2,1:T(4,128)S(1)}, f32[6,4,4]{0,2,1:T(4,128)}, u32[]{:S(2)}) copy-start(f32[6,4,4]{0,2,1:T(4,128)} %param.12) | copy-start | bytes 1156
  27.5 7.5 %collective-permute-start = (f32[32,9,2,128]{3,2,1,0:T(2,128)S(1)}, f32[32,9,2,128]{3,2,1,0:T(2,128)S(1)}, u32[]{:S(2)}, u32[]{:S(2)}) collective-permute-start(f32[32,9,2,128]{3,2,1,0:T(2,128)S(1)} %get-tuple-element.3), channel_id=1, source_target_pairs={{16,464},{464,400},{400,336},{336,320},{320,368},{368,352},{352,28... | collective-permute-start | bytes 884744 | tf_op jit(solution)/shard_map/ppermute | solution.py:609
  29.4 8.7 %collective-permute-start.1 = (f32[32,9,2,128]{3,2,1,0:T(2,128)S(1)}, f32[32,9,2,128]{3,2,1,0:T(2,128)S(1)}, u32[]{:S(2)}, u32[]{:S(2)}) collective-permute-start(f32[32,9,2,128]{3,2,1,0:T(2,128)S(1)} %get-tuple-element.2), channel_id=1, source_target_pairs={{464,16},{400,464},{336,400},{320,336},{368,320},{352,368},{288,35... | collective-permute-start | bytes 884744 | tf_op jit(solution)/shard_map/ppermute | solution.py:610
  61.6 21.0 %copy-start = (f32[2,2,256]{2,1,0:T(2,128)S(1)}, f32[2,2,256]{2,1,0:T(2,128)}, u32[]{:S(2)}) copy-start(f32[2,2,256]{2,1,0:T(2,128)} %vel.1) | copy-start | bytes 12292
  61.6 21.0 %copy-start.1 = (s32[2,256]{1,0:T(2,128)S(1)}, s32[2,256]{1,0:T(2,128)}, u32[]{:S(2)}) copy-start(s32[2,256]{1,0:T(2,128)} %grounded.1) | copy-start | bytes 6148
